TPU v7x, 32 devices: a whole 2x2x4 slice. The times are simulated.
32 devices in a mesh: groups: 2 (over x), cache: 16 (over z, y, core).
Axes of the slice: x: 2, y: 2, z: 4, core: 2. Of those that a mesh axis runs over, the one named last changes fastest.
Arguments:
- prefix_len: int32 [32], P('groups'), parts along dimension 0, may hold values from 128 to 1024, as said below
- hits: int32 [32, 1], P('groups'), parts along dimension 0, may hold values from 0 to 15, as said below
- span_block: int32 [32, 16], P('groups'), parts along dimension 0, may hold values from 0 to 15, each once within a row
- queries: bfloat16 [2048, 2048], P(('groups', 'cache')), parts along dimension 0, may hold values from -100 to 100
- fresh_keys: bfloat16 [2048, 128], P(('groups', 'cache')), parts along dimension 0, may hold values from -4 to 4
- fresh_values: bfloat16 [2048, 128], P(('groups', 'cache')), parts along dimension 0, may hold values from -4 to 4
- cache_keys: bfloat16 [65536, 128], P(('groups', 'cache')), parts along dimension 0, may hold values from -4 to 4
- cache_values: bfloat16 [65536, 128], P(('groups', 'cache')), parts along dimension 0, may hold values from -4 to 4
Outputs:
- attended: bfloat16 [2048, 2048], P(('groups', 'cache')), parts along dimension 0
There are 2 independent parts, one for each index of `groups`. A program takes and returns all parts, laid end to end along the dimension named above; each array names one. Nothing has to cross between parts.
Inputs may be any that keep to these rules, and one draw needn't show every extreme that they name: `prefix_len`: every request's prefix holds at least 128 tokens, and one request in every draw holds exactly 1024. `hits`: each row names 1 different devices. Each device is named by at most 2 requests; 4 devices are named by exactly 2, half of them by one, a quarter by none. `span_block`: each row is a permutation.
All inputs are finite; a program needn't handle non-finite values.
Results may differ from a plain program's by a relative error of at most 0.0065.
Values may be sent and summed in bfloat16 or wider, within the bound.
No kernel may reach another device: no remote copies, remote signals or barrier semaphores. Data moves between devices by JAX's collectives and lax.ppermute only.
A program may use at most 64 MiB of HBM per device.

v0:
```python
import math

import jax
import jax.numpy as jnp
from jax import lax
from jax.sharding import PartitionSpec as P

HEADS = 16
HD = 128
PAGE = 128
CAP = 2
REQUESTS = 16
TOK_REQ = 4
PAGES_DEV = 16


floor_score = -1e30


def owner_block(query_block, page_keys, page_values, visible):
    scale = HD ** (-0.5)
    scores = (
        jnp.einsum("thd,kd->thk", query_block, page_keys, preferred_element_type=jnp.float32)
        * scale
    )
    scores = jnp.where(visible, scores, floor_score)
    maxima = jnp.max(scores, axis=2)
    weights = jnp.exp(scores - maxima[:, :, None]) * visible
    totals = jnp.maximum(jnp.sum(weights, axis=2), 1.0)
    summed = jnp.einsum(
        "thk,kd->thd", weights.astype(jnp.bfloat16), page_values, preferred_element_type=jnp.float32
    )
    partial_out = (summed / totals[:, :, None]).astype(jnp.bfloat16)
    return (partial_out, maxima + jnp.log(totals))


def serve_slots(slot_queries, slot_keys, slot_values, slot_visible, devices):
    per_group = math.gcd(devices, 16)

    def one_slot(packed):
        queries_in, page_keys, page_values, visible = packed
        grouped = queries_in.reshape(devices // per_group, per_group * TOK_REQ, HEADS, HD)

        def one_group(query_block):
            return owner_block(query_block, page_keys, page_values, visible)

        outputs, lse_rows = lax.map(one_group, grouped)
        return (
            outputs.reshape(devices, TOK_REQ, HEADS * HD),
            lse_rows.reshape(devices, TOK_REQ, HEADS),
        )

    return lax.map(one_slot, (slot_queries, slot_keys, slot_values, slot_visible))


def body(prefix_len, hits, span_block, queries, fresh_keys, fresh_values, cache_keys, cache_values):
    devices = lax.axis_size("cache")
    myself = lax.axis_index("cache")
    hit_count = hits.shape[1]
    region = PAGES_DEV // CAP * PAGE
    per_device = REQUESTS * TOK_REQ
    scale = HD ** (-0.5)
    offsets = jnp.arange(TOK_REQ, dtype=jnp.int32)
    request_ids = jnp.arange(REQUESTS, dtype=jnp.int32)
    owner_ids = jnp.arange(devices, dtype=jnp.int32)
    slot_ids = jnp.arange(CAP, dtype=jnp.int32)
    is_named = jnp.any(hits[:, :, None] == owner_ids[None, None, :], axis=1).astype(jnp.int32)
    earlier = (request_ids[None, :] < request_ids[:, None]).astype(jnp.int32)
    slot_rank = jnp.sum(earlier[:, :, None] * is_named[None, :, :], axis=1)
    holding = (is_named[None] == 1) & (slot_rank[None] == slot_ids[:, None, None])
    occupied = jnp.any(holding, axis=1)
    send_request = jnp.sum(holding * request_ids[None, :, None], axis=1)
    local_request = jnp.take(send_request, myself, axis=1)
    local_occupied = jnp.take(occupied, myself, axis=1)
    local_hits = jnp.take(hits, local_request, axis=0)
    hit_place = jnp.sum(
        jnp.where(local_hits == myself, jnp.arange(hit_count, dtype=jnp.int32)[None, :], 0), axis=1
    )
    page_limit = jnp.take(prefix_len, local_request)
    prefix_spot = hit_place[:, None] * region + jnp.arange(region, dtype=jnp.int32)[None, :]
    slot_visible = local_occupied[:, None] & (prefix_spot < page_limit[:, None])
    region_keys = cache_keys.reshape(CAP, region, HD)
    region_values = cache_values.reshape(CAP, region, HD)
    query_heads = queries.reshape(REQUESTS, TOK_REQ, HEADS, HD)
    my_blocks = jnp.take(span_block, myself, axis=1)
    query_spot = my_blocks[:, None] * TOK_REQ + offsets[None, :]
    running = jnp.full((REQUESTS, TOK_REQ, HEADS), floor_score, jnp.float32)
    key_piece = lax.all_gather(fresh_keys, "cache", axis=0, tiled=True)
    value_piece = lax.all_gather(fresh_values, "cache", axis=0, tiled=True)
    count = key_piece.shape[0] // per_device
    key_rows = jnp.transpose(key_piece.reshape(count, REQUESTS, TOK_REQ, HD), (1, 0, 2, 3)).reshape(
        REQUESTS, count * TOK_REQ, HD
    )
    value_rows = jnp.transpose(
        value_piece.reshape(count, REQUESTS, TOK_REQ, HD), (1, 0, 2, 3)
    ).reshape(REQUESTS, count * TOK_REQ, HD)
    key_spot = (span_block[:, :, None] * TOK_REQ + offsets[None, None, :]).reshape(
        REQUESTS, count * TOK_REQ
    )
    visible = (key_spot[:, None, :] <= query_spot[:, :, None])[:, :, None, :]
    scores = (
        jnp.einsum("rthd,rkd->rthk", query_heads, key_rows, preferred_element_type=jnp.float32)
        * scale
    )
    scores = jnp.where(visible, scores, floor_score)
    highest = jnp.maximum(running, jnp.max(scores, axis=3))
    weights = jnp.exp(scores - highest[..., None]) * visible
    totals = jnp.sum(weights, axis=3)
    value_wide = value_rows.astype(jnp.float32)
    summed = jnp.einsum("rthk,rkd->rthd", weights, value_wide, precision=lax.Precision.HIGHEST)
    running, totals, summed = (highest, totals, summed)
    prompt_out = summed / totals[..., None]
    prompt_lse = running + jnp.log(totals)
    units = queries.reshape(REQUESTS, TOK_REQ, HEADS * HD)
    outgoing = jnp.take(units, send_request, axis=0)
    arrived_queries = lax.all_to_all(outgoing, "cache", split_axis=1, concat_axis=1, tiled=True)
    partial_out, partial_lse = serve_slots(
        arrived_queries, region_keys, region_values, slot_visible, devices
    )
    returned_out, returned_lse = (
        lax.all_to_all(
            partial_out.astype(jnp.float32), "cache", split_axis=1, concat_axis=1, tiled=True
        ).astype(partial_out.dtype),
        lax.all_to_all(partial_lse, "cache", split_axis=1, concat_axis=1, tiled=True),
    )
    flat_out = returned_out.reshape(CAP * devices, TOK_REQ, HEADS, HD)
    flat_lse = returned_lse.reshape(CAP * devices, TOK_REQ, HEADS)
    hit_rank = jnp.take_along_axis(slot_rank, hits, axis=1)
    source = hit_rank * devices + hits
    owner_out = jnp.take(flat_out, source, axis=0)
    owner_lse = jnp.take(flat_lse, source, axis=0)
    every_lse = jnp.concatenate([prompt_lse[:, None], owner_lse], axis=1)
    highest = jnp.max(every_lse, axis=1)
    shares = jnp.exp(every_lse - highest[:, None])
    combined = shares[:, 0, :, :, None] * prompt_out + jnp.einsum(
        "rith,rithd->rthd", shares[:, 1:], owner_out, preferred_element_type=jnp.float32
    )
    result = combined / jnp.sum(shares, axis=1)[..., None]
    return result.astype(jnp.bfloat16).reshape(per_device, HEADS * HD)


def solution(mesh):
    in_specs = (
        P("groups"),
        P("groups", None),
        P("groups", None),
        P(("groups", "cache"), None),
        P(("groups", "cache"), None),
        P(("groups", "cache"), None),
        P(("groups", "cache"), None),
        P(("groups", "cache"), None),
    )
    out_specs = P(("groups", "cache"), None)
    return jax.shard_map(body, mesh=mesh, in_specs=in_specs, out_specs=out_specs, check_vma=False)
```

profile of v0, /device:TPU:0, one launch (start us, length us, event | category | flops | bytes accessed | tf_op | source)
XLA Modules:
  0.0 96.3 jit_solution(12392458391359597815)
XLA Ops:
  0.0 0.8 broadcast_compare_fusion.1
  0.8 0.1 multiply_reduce_fusion
  1.0 0.1 reshape.447
  1.1 1.1 %reshape.331 = bf16[16,4,2048]{2,1,0:T(4,128)(2,1)S(1)} reshape(bf16[64,2048]{1,0:T(8,128)(2,1)} %param.13) | data formatting | bytes 524288 | tf_op jit(solution)/shard_map/reshape | solution.py:114
  2.1 1.0 %gather_fusion.1 = bf16[32,4,2048]{2,1,0:T(4,128)(2,1)S(1)} fusion(bf16[16,4,2048]{2,1,0:T(4,128)(2,1)S(1)} %reshape.331, s32[1024]{0:T(1024)S(1)} %pad_clamp_fusion.1), kind=kCustom, calls=%fused_computation.1 | custom fusion | bytes 1048704 | tf_op jit(solution)/shard_map/jit(_take)/gather | solution.py:115
  3.1 0.0 copy-start.1
  3.1 0.0 copy-start.7
  3.2 0.3 copy.71
  3.5 0.1 broadcast_select_fusion
  3.6 1.2 %copy.72 = bf16[2,16,4,2048]{3,2,0,1:T(4,128)(2,1)} copy(bf16[2,16,4,2048]{3,1,0,2:T(8,128)(2,1)S(1)} %broadcast_select_fusion) | data formatting | bytes 1048576 | tf_op jit(solution)/shard_map/jit(_take)/select_n | solution.py:115
  4.8 7.4 %all-to-all-start = ((bf16[2,16,4,2048]{3,2,0,1:T(4,128)(2,1)}), bf16[2,16,4,2048]{3,2,0,1:T(4,128)(2,1)S(1)}, u32[]{:S(2)}, u32[]{:S(2)}) async-start(bf16[2,16,4,2048]{3,2,0,1:T(4,128)(2,1)} %copy.72), calls=%async_computation | async-start | bytes 1048576 | tf_op jit(solution)/shard_map/all_to_all | solution.py:116
  12.2 0.1 constant_dynamic-slice_fusion
  12.3 0.2 fusion.39
  12.5 0.2 select_reduce_fusion.1
  12.7 0.7 gather_fusion.4
  13.4 0.1 copy.90
  13.5 0.1 iota_add_fusion
  13.6 0.1 copy.67
  13.6 0.1 add.155
  13.8 0.1 broadcast_add_fusion
  13.8 0.1 copy.68
  13.9 24.2 %all_gather.6 = bf16[1024,128]{1,0:T(8,128)(2,1)S(1)} all-gather(bf16[64,128]{1,0:T(8,128)(2,1)S(1)} %copy-done.4), channel_id=1, replica_groups=mesh['groups'=2,'cache'=16] {'cache'}, dimensions={0}, use_global_device_ids=true | all-gather | bytes 278528 | tf_op jit(solution)/shard_map/all_gather | solution.py:88
  38.1 0.1 copy.70
  38.3 0.6 gather_fusion
  38.9 0.1 fusion.42
  39.0 0.4 fusion.43
  39.4 0.4 fusion.26
  39.8 0.1 compare_and_fusion
  39.9 0.0 all-to-all-done
  40.0 0.0 copy-start.5
  40.0 7.6 %while.20 = (s32[]{:T(128)}, bf16[2,16,4,2048]{3,1,2,0:T(8,128)(2,1)S(1)}, f32[2,16,4,16]{3,2,0,1:T(4,128)S(1)}, pred[2,1024]{1,0:T(4,128)(4,1)S(1)}, bf16[2,16,...) while((s32[]{:T(128)}, ...), condition=%wide.region_8.9_spmd, body=%wide.region_5.0_spmd.sunk | while | flops 550765568 | bytes 15906925 | solution.py:53
  40.0 0.1 dynamic-slice_bitcast_fusion.2
  40.1 0.2 squeeze.19
  40.3 0.8 fusion.57
  41.1 1.2 %fusion.58 = f32[64,16]{1,0:T(8,128)S(1)} fusion(f32[64,16,1024]{2,1,0:T(8,128)S(1)} %get-tuple-element.216, f32[1024]{0:T(1024)S(1)} %convert_element_type.76, f32[64,16]{1,0:T(8,128)S(1)} %get-tuple-element.217, pred[1024]{0:T(1024)(128)(4,1)S(1)} %dynamic-slice_reduce_fusion.2), kind=kLoop, calls=%fused_computation.8.clone.1 | loop fusion | flops 5241856 | bytes 4207616 | tf_op jit(solution)/shard_map/while/body/eval_jaxpr/while/body/eval_jaxpr/reduce_sum | solution.py:29
  42.3 1.1 %fusion.59 = bf16[64,16,128]{2,1,0:T(8,128)(2,1)S(1)} fusion(f32[64,16,1024]{2,1,0:T(8,128)S(1)} %get-tuple-element.216, f32[1024]{0:T(1024)S(1)} %convert_element_type.76, f32[64,16]{1,0:T(8,128)S(1)} %get-tuple-element.217, pred[1024]{0:T(1024)(128)(4,1)S(1)} %dynamic-slice_reduce_fusion.2, f32[64,16]{1,0:T(8,128)S(1)} %get-tuple-element.218, ...), kind=kOutput, calls=%fused_computation.13.clone.1 | convolution fusion | flops 273940480 | bytes 4789252 | tf_op jit(solution)/shard_map/while/body/eval_jaxpr/while/body/eval_jaxpr/thk,kd->thd/dot_general | solution.py:30
  43.5 0.1 broadcast_in_dim.205
  43.6 0.2 copy_dynamic-update-slice_fusion.2
  43.8 0.1 dynamic-slice_bitcast_fusion.2
  43.9 0.2 squeeze.19
  44.1 0.8 fusion.57
  44.9 1.2 %fusion.58 = f32[64,16]{1,0:T(8,128)S(1)} fusion(f32[64,16,1024]{2,1,0:T(8,128)S(1)} %get-tuple-element.216, f32[1024]{0:T(1024)S(1)} %convert_element_type.76, f32[64,16]{1,0:T(8,128)S(1)} %get-tuple-element.217, pred[1024]{0:T(1024)(128)(4,1)S(1)} %dynamic-slice_reduce_fusion.2), kind=kLoop, calls=%fused_computation.8.clone.1 | loop fusion | flops 5241856 | bytes 4207616 | tf_op jit(solution)/shard_map/while/body/eval_jaxpr/while/body/eval_jaxpr/reduce_sum | solution.py:29
  46.1 1.1 %fusion.59 = bf16[64,16,128]{2,1,0:T(8,128)(2,1)S(1)} fusion(f32[64,16,1024]{2,1,0:T(8,128)S(1)} %get-tuple-element.216, f32[1024]{0:T(1024)S(1)} %convert_element_type.76, f32[64,16]{1,0:T(8,128)S(1)} %get-tuple-element.217, pred[1024]{0:T(1024)(128)(4,1)S(1)} %dynamic-slice_reduce_fusion.2, f32[64,16]{1,0:T(8,128)S(1)} %get-tuple-element.218, ...), kind=kOutput, calls=%fused_computation.13.clone.1 | convolution fusion | flops 273940480 | bytes 4789252 | tf_op jit(solution)/shard_map/while/body/eval_jaxpr/while/body/eval_jaxpr/thk,kd->thd/dot_general | solution.py:30
  47.3 0.1 broadcast_in_dim.205
  47.4 0.2 copy_dynamic-update-slice_fusion.2
  47.5 0.7 reshape.490
  48.3 3.5 %all-to-all-start.1 = ((f32[16,1,128]{2,1,0:T(1,128)}), f32[16,1,128]{2,1,0:T(1,128)S(1)}, u32[]{:S(2)}, u32[]{:S(2)}) async-start(f32[16,1,128]{2,1,0:T(1,128)} %reshape.490), calls=%async_computation.1 | async-start | bytes 16384 | tf_op jit(solution)/shard_map/all_to_all | solution.py:124
  51.7 22.4 %all_gather.7 = bf16[1024,128]{1,0:T(8,128)(2,1)S(1)} all-gather(bf16[64,128]{1,0:T(8,128)(2,1)S(1)} %copy-done.5), channel_id=1, replica_groups=mesh['groups'=2,'cache'=16] {'cache'}, dimensions={0}, use_global_device_ids=true | all-gather | bytes 278528 | tf_op jit(solution)/shard_map/all_gather | solution.py:89
  74.1 0.1 copy.77
  74.3 1.2 %copy.79 = bf16[2,16,4,2048]{3,2,0,1:T(4,128)(2,1)} copy(bf16[2,16,4,2048]{3,1,2,0:T(8,128)(2,1)S(1)} %get-tuple-element.65) | data formatting | bytes 1048576 | tf_op jit(solution)/shard_map/convert_element_type | solution.py:122
  75.5 3.6 %all-to-all-start.2 = ((bf16[2,16,4,2048]{3,2,0,1:T(4,128)(2,1)}), bf16[2,16,4,2048]{3,2,0,1:T(4,128)(2,1)S(1)}, u32[]{:S(2)}, u32[]{:S(2)}) async-start(bf16[2,16,4,2048]{3,2,0,1:T(4,128)(2,1)} %copy.79), calls=%async_computation.2 | async-start | bytes 1048576 | tf_op jit(solution)/shard_map/all_to_all | solution.py:121
  79.1 0.5 broadcast.506
  79.6 0.7 reduce.10
  80.2 0.1 reshape.491
  80.4 0.6 gather_fusion.2
  81.0 0.1 bitcast_select_fusion
  81.0 0.1 fusion.32
  81.1 0.1 fusion.40
  81.2 12.3 %all-to-all-done.2 = bf16[2,16,4,2048]{3,2,0,1:T(4,128)(2,1)S(1)} async-done(((bf16[2,16,4,2048]{3,2,0,1:T(4,128)(2,1)}), bf16[2,16,4,2048]{3,2,0,1:T(4,128)(2,1)S(1)}, u32[]{:S(2)}, u32[]{:S(2)}) %all-to-all-start.2) | async-done | bytes 524320 | tf_op jit(solution)/shard_map/all_to_all | solution.py:121
  93.5 0.3 copy.80
  93.8 0.1 copy.94
  93.9 0.6 gather_fusion.3
  94.5 1.0 %fusion.25 = bf16[16,4,16,128]{3,2,1,0:T(8,128)(2,1)S(1)} fusion(bf16[16,64,128,1]{2,1,3,0:T(8,128)(2,1)S(1)} %bitcast.106, f32[16,4,16,64]{3,2,1,0:T(8,128)S(1)} %get-tuple-element.167, f32[16,4,16]{2,1,0:T(4,128)S(1)} %get-tuple-element.150, bf16[16,4,16,128]{3,2,1,0:T(8,128)(2,1)S(1)} %gather_fusion.3, f32[16,4,16]{2,1,0:T(4,128)S(1)} %get-tuple-element.161, ...), kind=kOutput, calls=%fused_computation.35 | convolution fusion | flops 101842944 | bytes 1085456 | tf_op jit(solution)/shard_map/rthk,rkd->rthd/dot_general | solution.py:110
  95.5 0.8 copy.98
  (45 shorter events, 0.4 us)
Async XLA Ops:
  0.0 38.2 %copy-start = (s32[16]{0:T(128)S(1)}, s32[16]{0:T(128)}, u32[]{:S(2)}) copy-start(s32[16]{0:T(128)} %param.10) | copy-start | bytes 196
  0.0 12.2 %copy-start.6 = (s32[16,1]{0,1:T(1,128)S(1)}, s32[16,1]{0,1:T(1,128)}, u32[]{:S(2)}) copy-start(s32[16,1]{0,1:T(1,128)} %param.11) | copy-start | bytes 196
  0.0 38.2 %copy-start.2 = (bf16[64,2048]{1,0:T(8,128)(2,1)S(1)}, bf16[64,2048]{1,0:T(8,128)(2,1)}, u32[]{:S(2)}) copy-start(bf16[64,2048]{1,0:T(8,128)(2,1)} %param.13) | copy-start | bytes 786436
  0.0 12.2 %copy-start.3 = (s32[16,16]{1,0:T(8,128)S(1)}, s32[16,16]{1,0:T(8,128)}, u32[]{:S(2)}) copy-start(s32[16,16]{1,0:T(8,128)} %param.12) | copy-start | bytes 3076
  0.0 13.9 %copy-start.4 = (bf16[64,128]{1,0:T(8,128)(2,1)S(1)}, bf16[64,128]{1,0:T(8,128)(2,1)}, u32[]{:S(2)}) copy-start(bf16[64,128]{1,0:T(8,128)(2,1)} %param.14) | copy-start | bytes 49156
  3.1 36.8 %copy-start.1 = (bf16[2048,128]{1,0:T(8,128)(2,1)S(1)}, bf16[2048,128]{1,0:T(8,128)(2,1)}, u32[]{:S(2)}) copy-start(bf16[2048,128]{1,0:T(8,128)(2,1)} %param.16) | copy-start | bytes 1572868
  3.1 36.8 %copy-start.7 = (bf16[2048,128]{1,0:T(8,128)(2,1)S(1)}, bf16[2048,128]{1,0:T(8,128)(2,1)}, u32[]{:S(2)}) copy-start(bf16[2048,128]{1,0:T(8,128)(2,1)} %param.17) | copy-start | bytes 1572868
  4.8 35.2 %all-to-all-start = ((bf16[2,16,4,2048]{3,2,0,1:T(4,128)(2,1)}), bf16[2,16,4,2048]{3,2,0,1:T(4,128)(2,1)S(1)}, u32[]{:S(2)}, u32[]{:S(2)}) async-start(bf16[2,16,4,2048]{3,2,0,1:T(4,128)(2,1)} %copy.72), calls=%async_computation | async-start | bytes 1048576 | tf_op jit(solution)/shard_map/all_to_all | solution.py:116
  40.0 11.8 %copy-start.5 = (bf16[64,128]{1,0:T(8,128)(2,1)S(1)}, bf16[64,128]{1,0:T(8,128)(2,1)}, u32[]{:S(2)}) copy-start(bf16[64,128]{1,0:T(8,128)(2,1)} %param.15) | copy-start | bytes 49156
  48.3 27.2 %all-to-all-start.1 = ((f32[16,1,128]{2,1,0:T(1,128)}), f32[16,1,128]{2,1,0:T(1,128)S(1)}, u32[]{:S(2)}, u32[]{:S(2)}) async-start(f32[16,1,128]{2,1,0:T(1,128)} %reshape.490), calls=%async_computation.1 | async-start | bytes 16384 | tf_op jit(solution)/shard_map/all_to_all | solution.py:124
  75.5 18.0 %all-to-all-start.2 = ((bf16[2,16,4,2048]{3,2,0,1:T(4,128)(2,1)}), bf16[2,16,4,2048]{3,2,0,1:T(4,128)(2,1)S(1)}, u32[]{:S(2)}, u32[]{:S(2)}) async-start(bf16[2,16,4,2048]{3,2,0,1:T(4,128)(2,1)} %copy.79), calls=%async_computation.2 | async-start | bytes 1048576 | tf_op jit(solution)/shard_map/all_to_all | solution.py:121
where the time goes:
time: 96.7 us; the launch traced here: 96.3 us
  blocking collectives  46.6 us (48%)
  starting transfers between devices  14.4 us (15%)
  waiting for transfers between devices  12.3 us (13%)
  local copies, waits for them, and re-layouts  11.6 us (12%)
  other arithmetic  5.59 us (6%)
  matrix products  5.26 us (5%)
    all_gather x1, blocking collectives, body(): key_piece = lax.all_gather(fresh_keys, 'cache', axis=0, tiled=True)  24.2 us
    all_gather x1, blocking collectives, body(): value_piece = lax.all_gather(fresh_values, 'cache', axis=0, tiled=True)  22.4 us
    all_to_all x1, waiting for transfers between devices, body(): lax.all_to_all(partial_out.astype(jnp.float32), 'cache', split_axis=1, co...  12.3 us
    all_to_all x1, starting transfers between devices, body(): lax.all_to_all(outgoing, 'cache', split_axis=1, concat_axis=1, tiled=True)  7.38 us
    all_to_all x1, starting transfers between devices, body(): lax.all_to_all(partial_out.astype(jnp.float32), 'cache', split_axis=1, co...  3.57 us
    all_to_all x1, starting transfers between devices, body(): lax.all_to_all(partial_lse, 'cache', split_axis=1, concat_axis=1, tiled=T...  3.47 us
    reduce_sum x2, other arithmetic, owner_block(): totals = jnp.maximum(jnp.sum(weights, axis=2), 1.0)  2.34 us
    dot_general x2, matrix products, owner_block(): jnp.einsum('thk,kd->thd', weights.astype(jnp.bfloat16), page_values, pref...  2.27 us
  transfers between devices with their start and end apart: 3, of which 1 were waited for; matrix products, arithmetic and copies ran while one was open for 7% of the time, Pallas kernels for 0%

commit v1 on v0

v1 whole, which is shorter than its diff:
```python
import functools
import math

import jax
import jax.numpy as jnp
from jax import lax
from jax.experimental import pallas as pl
from jax.experimental.pallas import tpu as pltpu
from jax.sharding import PartitionSpec as P

HEADS = 16
HD = 128
PAGE = 128
CAP = 2
REQUESTS = 16
TOK_REQ = 4
PAGES_DEV = 16

REGION = PAGES_DEV // CAP * PAGE
HALF = HEADS // 2
MSG = 2 * TOK_REQ
WIDE = HALF * HD
ROWS = REQUESTS * TOK_REQ
SCALE = HD**-0.5
FLOOR = -1e30
NT = (((1,), (1,)), ((), ()))
NN = (((1,), (0,)), ((), ()))
TN = (((0,), (0,)), ((), ()))


def iota(shape, axis):
    return lax.broadcasted_iota(jnp.int32, shape, axis)


def dot(a, b, dims, **kw):
    return lax.dot_general(a, b, dims, preferred_element_type=jnp.float32, **kw)


def pack_kernel(devices, hit_count, hits, q, k, v, *refs):
    sends, places, held, count = refs[:CAP], refs[CAP], refs[CAP + 1], refs[CAP + 2]
    held[:ROWS, :WIDE] = q[:, :WIDE]
    held[ROWS:, :WIDE] = q[:, WIDE:]
    held[:ROWS, WIDE:] = k[...]
    held[ROWS:, WIDE:] = v[...]
    lane = iota((1, 2 * ROWS), 1)
    lane_request = (lane % ROWS) // TOK_REQ
    for r in range(REQUESTS):
        for i in range(hit_count):
            count[hits[r, i]] = 0
    rows = [[jnp.full((1, 2 * ROWS), -4 * MSG, jnp.int32)] * hit_count for _ in range(CAP)]
    for r in range(REQUESTS):
        for i in range(hit_count):
            owner = hits[r, i]
            rank = count[owner]
            count[owner] = rank + 1
            for s in range(CAP):
                place = jnp.where(rank == s, owner * MSG, -4 * MSG)
                rows[s][i] = jnp.where(lane_request == r, place, rows[s][i])
    inner = lane // ROWS * TOK_REQ + lane % TOK_REQ
    target = iota((devices * MSG, 2 * ROWS), 0)
    for s in range(CAP):
        chosen = None
        for i in range(hit_count):
            row = rows[s][i] + inner
            places[s * hit_count + i : s * hit_count + i + 1, :] = row
            hit = target == row
            chosen = hit if chosen is None else chosen | hit
        chosen = jnp.where(chosen, 1.0, 0.0).astype(jnp.bfloat16)
        sends[s][...] = dot(chosen, held[...], NN).astype(jnp.bfloat16)


def attend_kernel(
    slot, devices, hit_count, hits, prefix_len, span, got, keys, values, *refs
):
    if hit_count > 1:
        out, lse = refs[:2]
        refs = refs[2:]
    else:
        out, lse = refs[0], None
        refs = refs[1:]
    key_rows, value_rows, sems = refs
    copies = [
        pltpu.make_async_copy(keys.at[pl.ds(slot * REGION, REGION)], key_rows, sems.at[0]),
        pltpu.make_async_copy(
            values.at[pl.ds(slot * REGION, REGION)], value_rows.at[:, pl.ds(0, HD)], sems.at[1]
        ),
    ]
    for copy in copies:
        copy.start()
    value_rows[:, HD:] = jnp.ones((REGION, HD), jnp.bfloat16)
    me = lax.axis_index("cache")
    seen = jnp.int32(0)
    request = jnp.int32(0)
    which = jnp.int32(0)
    for r in range(REQUESTS):
        for i in range(hit_count):
            mine = hits[r, i] == me
            here = mine & (seen == slot)
            request = jnp.where(here, r, request)
            which = jnp.where(here, i, which)
            seen = seen + mine.astype(jnp.int32)
    occupied = seen > slot
    limit = prefix_len[request] - which * REGION
    for copy in copies:
        copy.wait()

    @pl.when(jnp.logical_not(occupied))
    def _():
        out[...] = jnp.zeros(out.shape, out.dtype)
        if lse is not None:
            lse[...] = jnp.zeros(lse.shape, lse.dtype)

    @pl.when(occupied)
    def _():
        total_rows = devices * MSG
        span_row = span[pl.ds(request, 1), :].astype(jnp.float32)
        source = iota((devices, total_rows), 0)
        spread = (iota((devices, total_rows), 1) // MSG == source).astype(jnp.float32)
        spans = jnp.broadcast_to(span_row, (16, devices)).astype(jnp.bfloat16)
        key_span = dot(spans, spread.astype(jnp.bfloat16), NN)[:1]
        lane = iota((1, total_rows), 1)
        key_spot = key_span.astype(jnp.int32) * TOK_REQ + lane % TOK_REQ
        is_key = lane % MSG < TOK_REQ
        if hit_count > 1:
            is_key = is_key & (which == 0)
        key_spot = jnp.where(is_key, key_spot, devices * TOK_REQ)
        prompt_keys = got[:, WIDE:]
        moved = pltpu.roll(prompt_keys.astype(jnp.float32), total_rows - TOK_REQ, 0)
        prompt_values = jnp.concatenate(
            [moved.astype(jnp.bfloat16), jnp.ones((total_rows, HD), jnp.bfloat16)], axis=1
        )
        cached_bias = jnp.where(iota((1, REGION), 1) < limit, 0.0, FLOOR)
        block = 16 * MSG

        def one_block(at):
            row = iota((block, devices), 0)
            row_source = at * 16 + row // MSG
            mine = iota((block, devices), 1) == row_source
            row_span = jnp.sum(jnp.where(mine, span_row, 0.0), axis=1, keepdims=True)
            row_spot = row_span.astype(jnp.int32) * TOK_REQ + iota((block, 1), 0) % TOK_REQ
            prompt_bias = jnp.where(key_spot <= row_spot, 0.0, FLOOR)
            prompt_bias = jnp.concatenate([prompt_bias, prompt_bias], axis=0)
            here = pl.ds(pl.multiple_of(at * block, block), block)
            lane_id = iota((block, HD), 1)
            logs = jnp.zeros((block, HD), jnp.float32)
            for c in range(0, HALF, 2):
                pair = jnp.concatenate(
                    [got[here, c * HD : (c + 1) * HD], got[here, (c + 1) * HD : (c + 2) * HD]],
                    axis=0,
                )
                cached = dot(pair, key_rows[...], NT) + cached_bias
                prompt = dot(pair, prompt_keys, NT) + prompt_bias
                top = jnp.maximum(
                    jnp.max(cached, axis=1, keepdims=True), jnp.max(prompt, axis=1, keepdims=True)
                )
                if hit_count > 1:
                    top = jnp.maximum(top, 0.1 * FLOOR)
                factor = SCALE * math.log2(math.e)
                cached = jnp.exp2((cached - top) * factor).astype(jnp.bfloat16)
                prompt = jnp.exp2((prompt - top) * factor).astype(jnp.bfloat16)
                summed = dot(cached, value_rows[...], NN) + dot(prompt, prompt_values, NN)
                totals = summed[:, HD:]
                if hit_count > 1:
                    totals = jnp.maximum(totals, 1.0)
                    level = top * SCALE + jnp.log(totals)
                    logs = jnp.where(lane_id == c, level[:block], logs)
                    logs = jnp.where(lane_id == c + 1, level[block:], logs)
                result = (summed[:, :HD] / totals).astype(jnp.bfloat16)
                out[here, c * HD : (c + 1) * HD] = result[:block]
                out[here, (c + 1) * HD : (c + 2) * HD] = result[block:]
            if lse is not None:
                lse[here, :] = logs

        blocks = devices // 16
        if blocks == 1:
            one_block(0)
        else:

            @pl.loop(0, blocks)
            def _(at):
                one_block(at)


def unpack_kernel(devices, hit_count, places, *refs):
    outs, logs, result = refs[:CAP], refs[CAP:-1], refs[-1]
    target = iota((devices * MSG, 2 * ROWS), 0)

    def chosen(s, i, dtype):
        place = s * hit_count + i
        return jnp.where(target == places[place : place + 1, :], 1.0, 0.0).astype(dtype)

    def rows_of(i):
        parts = [dot(chosen(s, i, jnp.bfloat16), outs[s][...], TN) for s in range(CAP)]
        return sum(parts[1:], parts[0])

    def logs_of(i):
        parts = [
            dot(chosen(s, i, jnp.float32), logs[s][...], TN, precision=lax.Precision.HIGHEST)
            for s in range(CAP)
        ]
        return sum(parts[1:], parts[0])

    if hit_count == 1:
        joined = rows_of(0)
    else:
        levels = [logs_of(i) for i in range(hit_count)]
        top = functools.reduce(jnp.maximum, levels)
        shares = [jnp.exp(level - top) for level in levels]
        total = sum(shares[1:], shares[0])
        pieces = [rows_of(i) for i in range(hit_count)]
        columns = []
        for c in range(HALF):
            part = sum(
                shares[i][:, c : c + 1] * pieces[i][:, c * HD : (c + 1) * HD]
                for i in range(hit_count)
            )
            columns.append(part / total[:, c : c + 1])
        joined = jnp.concatenate(columns, axis=1)
    joined = joined.astype(jnp.bfloat16)
    result[:, :WIDE] = joined[:ROWS]
    result[:, WIDE:] = joined[ROWS:]


def vmem(count):
    return [pl.BlockSpec(memory_space=pltpu.VMEM)] * count


def smem(count):
    return [pl.BlockSpec(memory_space=pltpu.SMEM)] * count


def body(prefix_len, hits, span_block, queries, fresh_keys, fresh_values, cache_keys, cache_values):
    devices = lax.axis_size("cache")
    hit_count = hits.shape[1]
    rows = devices * MSG
    params = pltpu.CompilerParams(vmem_limit_bytes=40 * 2**20)
    message = jax.ShapeDtypeStruct((rows, WIDE + HD), jnp.bfloat16)
    answer = jax.ShapeDtypeStruct((rows, WIDE), jnp.bfloat16)
    level = jax.ShapeDtypeStruct((rows, HD), jnp.float32)

    def exchange(x):
        return lax.all_to_all(x, "cache", split_axis=0, concat_axis=0, tiled=True)

    *sends, places = pl.pallas_call(
        functools.partial(pack_kernel, devices, hit_count),
        out_shape=[message] * CAP
        + [jax.ShapeDtypeStruct((CAP * hit_count, 2 * ROWS), jnp.int32)],
        in_specs=smem(1) + vmem(3),
        out_specs=vmem(CAP + 1),
        scratch_shapes=[
            pltpu.VMEM((2 * ROWS, WIDE + HD), jnp.bfloat16),
            pltpu.SMEM((devices,), jnp.int32),
        ],
        compiler_params=params,
        name="pack",
    )(hits, queries, fresh_keys, fresh_values)
    got = [exchange(x) for x in sends]
    pairs = rows * HALF * (REGION + rows)
    answers = []
    for slot in range(CAP):
        answers.append(
            pl.pallas_call(
                functools.partial(attend_kernel, slot, devices, hit_count),
                out_shape=[answer] + [level] * (hit_count > 1),
                in_specs=smem(2) + vmem(2) + [pl.BlockSpec(memory_space=pl.ANY)] * 2,
                out_specs=vmem(1 + (hit_count > 1)),
                scratch_shapes=[
                    pltpu.VMEM((REGION, HD), jnp.bfloat16),
                    pltpu.VMEM((REGION, 2 * HD), jnp.bfloat16),
                    pltpu.SemaphoreType.DMA((2,)),
                ],
                compiler_params=params,
                cost_estimate=pl.CostEstimate(
                    flops=4 * pairs * HD, bytes_accessed=4 * rows * WIDE, transcendentals=pairs
                ),
                name="attend",
            )(hits, prefix_len, span_block, got[slot], cache_keys, cache_values)
        )
    returned = [exchange(a[0]) for a in answers] + [exchange(a[1]) for a in answers if len(a) > 1]
    return pl.pallas_call(
        functools.partial(unpack_kernel, devices, hit_count),
        out_shape=jax.ShapeDtypeStruct((ROWS, HEADS * HD), jnp.bfloat16),
        in_specs=vmem(1 + len(returned)),
        out_specs=vmem(1)[0],
        compiler_params=params,
        name="unpack",
    )(places, *returned)


def solution(mesh):
    in_specs = (
        P("groups"),
        P("groups", None),
        P("groups", None),
        P(("groups", "cache"), None),
        P(("groups", "cache"), None),
        P(("groups", "cache"), None),
        P(("groups", "cache"), None),
        P(("groups", "cache"), None),
    )
    out_specs = P(("groups", "cache"), None)
    return jax.shard_map(body, mesh=mesh, in_specs=in_specs, out_specs=out_specs, check_vma=False)
```

time: 96.7 us -> 65 us (0.67)
  blocking collectives: 46.6 us -> 30.7 us
  local copies, waits for them, and re-layouts: 11.6 us -> 3.75 us
  starting transfers between devices: 14.4 us -> 7.2 us
  other arithmetic: 5.59 us -> 0 us
  matrix products: 5.26 us -> 0 us
  waiting for transfers between devices: 12.3 us -> 17.5 us
  Pallas kernels: 0 us -> 5.11 us
    all_gather x2 -> x0, blocking collectives: 46.6 us -> none  [the longest x1 24.2 us: body(): key_piece = lax.all_gather(fresh_keys, 'cache', axis=0, tiled=True)]
    all_to_all x0 -> x2, blocking collectives: none -> 30.7 us  [exchange(): return lax.all_to_all(x, 'cache', split_axis=0, concat_axis=0, tiled=True)]
    all_to_all x3 -> x2, starting transfers between devices: 14.4 us -> 7.2 us  [exchange(): return lax.all_to_all(x, 'cache', split_axis=0, concat_axis=0, tiled=True)]
    all_to_all x3 -> x2, waiting for transfers between devices: 12.3 us -> 17.5 us  [exchange(): return lax.all_to_all(x, 'cache', split_axis=0, concat_axis=0, tiled=True)]
    dot_general x6 -> x0, matrix products: 5.26 us -> none  [the longest x2 2.27 us: owner_block(): jnp.einsum('thk,kd->thd', weights.astype(jnp.bfloat16), page_values, pref...]
    pallas_call x0 -> x4, Pallas kernels: none -> 5.11 us  [the longest x2 2.34 us: body(): pl.pallas_call(functools.partial(attend_kernel, slot, devices, hit_count)...]
    gather x6 -> x0, local copies, waits for them, and re-layouts: 3.8 us -> none  [the longest x2 1.29 us: body(): outgoing = jnp.take(units, send_request, axis=0)]
    reduce_sum x6 -> x0, other arithmetic: 2.96 us -> none  [the longest x2 2.34 us: owner_block(): totals = jnp.maximum(jnp.sum(weights, axis=2), 1.0)]
  transfers between devices with their start and end apart: 3 -> 2, of which waited for: 1 -> 2; matrix products, arithmetic and copies ran while one was open for 7% -> 0% of each run, Pallas kernels for 0% -> 4%
where the time goes in v1:
time: 65 us; the launch traced here: 64.4 us
  blocking collectives  30.7 us (47%)
  waiting for transfers between devices  17.5 us (27%)
  starting transfers between devices  7.2 us (11%)
  Pallas kernels  5.11 us (8%)
  local copies, waits for them, and re-layouts  3.75 us (6%)
    all_to_all x2, blocking collectives, exchange(): return lax.all_to_all(x, 'cache', split_axis=0, concat_axis=0, tiled=True)  30.7 us
    all_to_all x2, waiting for transfers between devices, exchange(): return lax.all_to_all(x, 'cache', split_axis=0, concat_axis=0, tiled=True)  17.5 us
    all_to_all x2, starting transfers between devices, exchange(): return lax.all_to_all(x, 'cache', split_axis=0, concat_axis=0, tiled=True)  7.2 us
    unnamed x15, local copies, waits for them, and re-layouts  3.75 us
    pallas_call x2, Pallas kernels, body(): pl.pallas_call(functools.partial(attend_kernel, slot, devices, hit_count)...  2.34 us
    pallas_call x1, Pallas kernels, body(): pl.pallas_call(functools.partial(pack_kernel, devices, hit_count), out_sh...  1.75 us
  transfers between devices with their start and end apart: 2, of which 2 were waited for; matrix products, arithmetic and copies ran while one was open for 0% of the time, Pallas kernels for 4%

profile of v1, /device:TPU:0, one launch (start us, length us, event | category | flops | bytes accessed | tf_op | source)
XLA Modules:
  0.0 64.4 jit_solution(16523898843197811760)
XLA Ops:
  0.0 0.7 %copy.9.hits = s32[16,1]{1,0:T(8,128)S(1)} copy(s32[16,1]{0,1:T(1,128)} %param.9) | data formatting | bytes 128 | tf_op args[1]
  0.7 0.0 copy-start
  0.7 0.9 %copy-done = bf16[64,2048]{1,0:T(8,128)(2,1)S(1)} copy-done((bf16[64,2048]{1,0:T(8,128)(2,1)S(1)}, bf16[64,2048]{1,0:T(8,128)(2,1)}, u32[]{:S(2)}) %copy-start) | copy-done | bytes 262168
  1.7 0.0 copy-start.1
  1.7 0.7 %copy-done.1 = bf16[64,128]{1,0:T(8,128)(2,1)S(1)} copy-done((bf16[64,128]{1,0:T(8,128)(2,1)S(1)}, bf16[64,128]{1,0:T(8,128)(2,1)}, u32[]{:S(2)}) %copy-start.1) | copy-done | bytes 16408
  2.4 0.0 copy-start.2
  2.4 0.7 %copy-done.2 = bf16[64,128]{1,0:T(8,128)(2,1)S(1)} copy-done((bf16[64,128]{1,0:T(8,128)(2,1)S(1)}, bf16[64,128]{1,0:T(8,128)(2,1)}, u32[]{:S(2)}) %copy-start.2) | copy-done | bytes 16408
  3.1 1.7 %pack.1 = (bf16[128,1152]{1,0:T(8,128)(2,1)S(1)}, bf16[128,1152]{1,0:T(8,128)(2,1)}, s32[2,128]{1,0:T(2,128)S(1)}) custom-call(s32[16,1]{1,0:T(8,128)S(1)} %copy.9.hits, bf16[64,2048]{1,0:T(8,128)(2,1)S(1)} %copy-done, bf16[64,128]{1,0:T(8,128)(2,1)S(1)} %copy-done.1, bf16[64,128]{1,0:T(8,128)(2,1)S(1)} %copy-done.2), custom_call_target="tpu_custom_call" | custom-call | tf_op jit(solution)/shard_map/pack/pallas_call | solution.py:244
  4.9 0.0 copy-start.3
  4.9 0.0 copy-start.4
  4.9 17.9 %all_to_all.44 = bf16[16,8,1152]{2,1,0:T(8,128)(2,1)S(1)} all-to-all(bf16[16,8,1152]{2,1,0:T(8,128)(2,1)S(1)} %bitcast.12), channel_id=1, replica_groups=mesh['groups'=2,'cache'=16] {'cache'}, dimensions={0} | all-to-all | bytes 589824 | tf_op jit(solution)/shard_map/all_to_all | solution.py:242
  22.8 0.0 copy-start.5
  22.8 3.7 %all-to-all-start.2 = ((bf16[16,8,1152]{2,1,0:T(8,128)(2,1)}), bf16[16,8,1152]{2,1,0:T(8,128)(2,1)S(1)}, u32[]{:S(2)}, u32[]{:S(2)}) async-start(bf16[16,8,1152]{2,1,0:T(8,128)(2,1)} %bitcast.4), calls=%async_computation.2 | async-start | bytes 589824 | tf_op jit(solution)/shard_map/all_to_all | solution.py:242
  26.4 0.0 copy-start.6
  26.4 0.0 copy-done.3
  26.5 0.0 copy-done.4
  26.5 0.0 copy-done.5
  26.5 0.6 copy-done.6
  27.1 1.5 %attend.2 = bf16[128,1024]{1,0:T(8,128)(2,1)} custom-call(s32[16,1]{1,0:T(8,128)S(1)} %copy.9.hits, s32[16]{0:T(128)S(1)} %copy-done.6, s32[16,16]{1,0:T(8,128)S(1)} %copy-done.5, bf16[128,1152]{1,0:T(8,128)(2,1)S(1)} %bitcast.11, bf16[2048,128]{1,0:T(8,128)(2,1)S(1)} %copy-done.3, bf16[2048,128]{1,0:T(8,128)(2,1)S(1)} %copy-done.4), custom_call_target="tpu_custom_call" | custom-call | flops 603979776 | bytes 524288 | tf_op jit(solution)/shard_map/attend/pallas_call | solution.py:262
  28.6 8.3 %all-to-all-done.2 = bf16[16,8,1152]{2,1,0:T(8,128)(2,1)S(1)} async-done(((bf16[16,8,1152]{2,1,0:T(8,128)(2,1)}), bf16[16,8,1152]{2,1,0:T(8,128)(2,1)S(1)}, u32[]{:S(2)}, u32[]{:S(2)}) %all-to-all-start.2) | async-done | bytes 294944 | tf_op jit(solution)/shard_map/all_to_all | solution.py:242
  37.0 3.5 %all-to-all-start.1 = ((bf16[16,8,1024]{2,1,0:T(8,128)(2,1)}), bf16[16,8,1024]{2,1,0:T(8,128)(2,1)S(1)}, u32[]{:S(2)}, u32[]{:S(2)}) async-start(bf16[16,8,1024]{2,1,0:T(8,128)(2,1)} %bitcast.2), calls=%async_computation.1 | async-start | bytes 524288 | tf_op jit(solution)/shard_map/all_to_all | solution.py:242
  40.5 0.8 %attend.3 = bf16[128,1024]{1,0:T(8,128)(2,1)S(1)} custom-call(s32[16,1]{1,0:T(8,128)S(1)} %copy.9.hits, s32[16]{0:T(128)S(1)} %copy-done.6, s32[16,16]{1,0:T(8,128)S(1)} %copy-done.5, bf16[128,1152]{1,0:T(8,128)(2,1)S(1)} %bitcast.10, bf16[2048,128]{1,0:T(8,128)(2,1)S(1)} %copy-done.3, bf16[2048,128]{1,0:T(8,128)(2,1)S(1)} %copy-done.4), custom_call_target="tpu_custom_call" | custom-call | flops 603979776 | bytes 524288 | tf_op jit(solution)/shard_map/attend/pallas_call | solution.py:262
  41.3 9.2 %all-to-all-done.1 = bf16[16,8,1024]{2,1,0:T(8,128)(2,1)S(1)} async-done(((bf16[16,8,1024]{2,1,0:T(8,128)(2,1)}), bf16[16,8,1024]{2,1,0:T(8,128)(2,1)S(1)}, u32[]{:S(2)}, u32[]{:S(2)}) %all-to-all-start.1) | async-done | bytes 262176 | tf_op jit(solution)/shard_map/all_to_all | solution.py:242
  50.5 12.8 %all_to_all.45 = bf16[16,8,1024]{2,1,0:T(8,128)(2,1)S(1)} all-to-all(bf16[16,8,1024]{2,1,0:T(8,128)(2,1)S(1)} %bitcast.13), channel_id=1, replica_groups=mesh['groups'=2,'cache'=16] {'cache'}, dimensions={0} | all-to-all | bytes 524288 | tf_op jit(solution)/shard_map/all_to_all | solution.py:242
  63.3 1.0 %unpack.1 = bf16[64,2048]{1,0:T(8,128)(2,1)} custom-call(s32[2,128]{1,0:T(2,128)S(1)} %get-tuple-element.8.places, bf16[128,1024]{1,0:T(8,128)(2,1)S(1)} %bitcast.8, bf16[128,1024]{1,0:T(8,128)(2,1)S(1)} %bitcast.9), custom_call_target="tpu_custom_call" | custom-call | tf_op jit(solution)/shard_map/unpack/pallas_call | solution.py:280
Async XLA Ops:
  0.7 0.9 %copy-start = (bf16[64,2048]{1,0:T(8,128)(2,1)S(1)}, bf16[64,2048]{1,0:T(8,128)(2,1)}, u32[]{:S(2)}) copy-start(bf16[64,2048]{1,0:T(8,128)(2,1)} %q.1) | copy-start | bytes 786436
  1.7 0.7 %copy-start.1 = (bf16[64,128]{1,0:T(8,128)(2,1)S(1)}, bf16[64,128]{1,0:T(8,128)(2,1)}, u32[]{:S(2)}) copy-start(bf16[64,128]{1,0:T(8,128)(2,1)} %k.1) | copy-start | bytes 49156
  2.4 0.7 %copy-start.2 = (bf16[64,128]{1,0:T(8,128)(2,1)S(1)}, bf16[64,128]{1,0:T(8,128)(2,1)}, u32[]{:S(2)}) copy-start(bf16[64,128]{1,0:T(8,128)(2,1)} %v.1) | copy-start | bytes 49156
  4.9 21.6 %copy-start.3 = (bf16[2048,128]{1,0:T(8,128)(2,1)S(1)}, bf16[2048,128]{1,0:T(8,128)(2,1)}, u32[]{:S(2)}) copy-start(bf16[2048,128]{1,0:T(8,128)(2,1)} %keys.3) | copy-start | bytes 1572868
  4.9 21.6 %copy-start.4 = (bf16[2048,128]{1,0:T(8,128)(2,1)S(1)}, bf16[2048,128]{1,0:T(8,128)(2,1)}, u32[]{:S(2)}) copy-start(bf16[2048,128]{1,0:T(8,128)(2,1)} %values.3) | copy-start | bytes 1572868
  22.8 3.7 %copy-start.5 = (s32[16,16]{1,0:T(8,128)S(1)}, s32[16,16]{1,0:T(8,128)}, u32[]{:S(2)}) copy-start(s32[16,16]{1,0:T(8,128)} %span.3) | copy-start | bytes 3076
  22.8 14.2 %all-to-all-start.2 = ((bf16[16,8,1152]{2,1,0:T(8,128)(2,1)}), bf16[16,8,1152]{2,1,0:T(8,128)(2,1)S(1)}, u32[]{:S(2)}, u32[]{:S(2)}) async-start(bf16[16,8,1152]{2,1,0:T(8,128)(2,1)} %bitcast.4), calls=%async_computation.2 | async-start | bytes 589824 | tf_op jit(solution)/shard_map/all_to_all | solution.py:242
  26.4 0.7 %copy-start.6 = (s32[16]{0:T(128)S(1)}, s32[16]{0:T(128)}, u32[]{:S(2)}) copy-start(s32[16]{0:T(128)} %prefix_len.3) | copy-start | bytes 196
  37.0 13.5 %all-to-all-start.1 = ((bf16[16,8,1024]{2,1,0:T(8,128)(2,1)}), bf16[16,8,1024]{2,1,0:T(8,128)(2,1)S(1)}, u32[]{:S(2)}, u32[]{:S(2)}) async-start(bf16[16,8,1024]{2,1,0:T(8,128)(2,1)} %bitcast.2), calls=%async_computation.1 | async-start | bytes 524288 | tf_op jit(solution)/shard_map/all_to_all | solution.py:242

commit v2 on v1

v2 whole, which is shorter than its diff:
```python
import functools
import math

import jax
import jax.numpy as jnp
from jax import lax
from jax.experimental import pallas as pl
from jax.experimental.pallas import tpu as pltpu
from jax.sharding import PartitionSpec as P

HEADS = 16
HD = 128
PAGE = 128
CAP = 2
REQUESTS = 16
TOK_REQ = 4
PAGES_DEV = 16

REGION = PAGES_DEV // CAP * PAGE
HALF = HEADS // 2
MSG = 2 * TOK_REQ
WIDE = HALF * HD
ROWS = REQUESTS * TOK_REQ
SCALE = HD**-0.5
FLOOR = -1e30
NT = (((1,), (1,)), ((), ()))
NN = (((1,), (0,)), ((), ()))
TN = (((0,), (0,)), ((), ()))


def iota(shape, axis):
    return lax.broadcasted_iota(jnp.int32, shape, axis)


def dot(a, b, dims, **kw):
    return lax.dot_general(a, b, dims, preferred_element_type=jnp.float32, **kw)


def pack_kernel(devices, hit_count, hits, q, k, v, send, places, held, count, sems):
    copies = [
        pltpu.make_async_copy(source, held.at[pl.ds(row, ROWS), pl.ds(column, width)], sems.at[n])
        for n, (source, row, column, width) in enumerate(
            [
                (q.at[:, pl.ds(0, WIDE)], 0, 0, WIDE),
                (q.at[:, pl.ds(WIDE, WIDE)], ROWS, 0, WIDE),
                (k, 0, WIDE, HD),
                (v, ROWS, WIDE, HD),
            ]
        )
    ]
    for copy in copies:
        copy.start()
    lane = iota((1, 2 * ROWS), 1)
    lane_request = (lane % ROWS) // TOK_REQ
    for r in range(REQUESTS):
        for i in range(hit_count):
            count[hits[r * hit_count + i]] = 0
    rows = [[jnp.full((1, 2 * ROWS), -4 * MSG, jnp.int32)] * hit_count for _ in range(CAP)]
    for r in range(REQUESTS):
        for i in range(hit_count):
            owner = hits[r * hit_count + i]
            rank = count[owner]
            count[owner] = rank + 1
            for s in range(CAP):
                place = jnp.where(rank == s, owner * MSG, -4 * MSG)
                rows[s][i] = jnp.where(lane_request == r, place, rows[s][i])
    inner = lane // ROWS * TOK_REQ + lane % TOK_REQ
    target = iota((devices * MSG, 2 * ROWS), 0)
    picks = []
    for s in range(CAP):
        chosen = None
        for i in range(hit_count):
            row = rows[s][i] + inner
            places[s * hit_count + i : s * hit_count + i + 1, :] = row
            hit = target == row
            chosen = hit if chosen is None else chosen | hit
        picks.append(jnp.where(chosen, 1.0, 0.0).astype(jnp.bfloat16))
    for copy in copies:
        copy.wait()
    for s in range(CAP):
        here = slice(s * (WIDE + HD), (s + 1) * (WIDE + HD))
        send[:, here] = dot(picks[s], held[...], NN).astype(jnp.bfloat16)


def prep_kernel(devices, hit_count, hits, prefix_len, span, values, busy, prompt, cached, wide):
    me = lax.axis_index("cache")
    total_rows = devices * MSG
    wide[:, :HD] = values[...]
    wide[:, HD:] = jnp.ones((CAP * REGION, HD), jnp.bfloat16)
    for slot in range(CAP):
        seen = jnp.int32(0)
        request = jnp.int32(0)
        which = jnp.int32(0)
        for r in range(REQUESTS):
            for i in range(hit_count):
                mine = hits[r * hit_count + i] == me
                here = mine & (seen == slot)
                request = jnp.where(here, r, request)
                which = jnp.where(here, i, which)
                seen = seen + mine.astype(jnp.int32)
        busy[slot] = (seen > slot).astype(jnp.int32)
        limit = prefix_len[request] - which * REGION
        cached[slot : slot + 1, :] = jnp.where(iota((1, REGION), 1) < limit, 0.0, FLOOR)
        span_row = span[pl.ds(request, 1), :].astype(jnp.float32)
        source = iota((devices, total_rows), 0)
        spread = (iota((devices, total_rows), 1) // MSG == source).astype(jnp.bfloat16)
        spans = jnp.broadcast_to(span_row, (16, devices)).astype(jnp.bfloat16)
        key_span = dot(spans, spread, NN)[:1]
        lane = iota((1, total_rows), 1)
        key_spot = key_span.astype(jnp.int32) * TOK_REQ + lane % TOK_REQ
        is_key = lane % MSG < TOK_REQ
        if hit_count > 1:
            is_key = is_key & (which == 0)
        key_spot = jnp.where(is_key, key_spot, devices * TOK_REQ)
        block = 16 * MSG

        def one_block(at):
            row_source = at * 16 + iota((block, devices), 0) // MSG
            mine = iota((block, devices), 1) == row_source
            row_span = jnp.sum(jnp.where(mine, span_row, 0.0), axis=1, keepdims=True)
            row_spot = row_span.astype(jnp.int32) * TOK_REQ + iota((block, 1), 0) % TOK_REQ
            here = pl.ds(slot * total_rows + at * block, block)
            prompt[here, :] = jnp.where(key_spot <= row_spot, 0.0, FLOOR)

        each_block(devices, one_block)


def each_block(devices, one_block):
    blocks = devices // 16
    if blocks == 1:
        one_block(0)
    else:
        pl.loop(0, blocks)(one_block)


def attend_kernel(devices, hit_count, busy, prompt_mask, cached_mask, got, keys, wide, out, *levels):
    total_rows = devices * MSG
    block = 16 * MSG
    factor = SCALE * math.log2(math.e)
    for slot in range(CAP):
        base = slot * (WIDE + HD)
        region = slice(slot * REGION, (slot + 1) * REGION)
        first = slot * WIDE

        @pl.when(busy[slot] == 0)
        def _():
            out[:, first : first + WIDE] = jnp.zeros((total_rows, WIDE), jnp.bfloat16)
            for lse in levels:
                lse[:, slot * HD : (slot + 1) * HD] = jnp.zeros((total_rows, HD), jnp.float32)

        @pl.when(busy[slot] != 0)
        def _():
            prompt_keys = got[:, base + WIDE : base + WIDE + HD]
            moved = pltpu.roll(prompt_keys.astype(jnp.float32), total_rows - TOK_REQ, 0)
            prompt_values = jnp.concatenate(
                [moved.astype(jnp.bfloat16), jnp.ones((total_rows, HD), jnp.bfloat16)], axis=1
            )

            def one_block(at):
                here = pl.ds(at * block, block)
                prompt_bias = prompt_mask[pl.ds(slot * total_rows + at * block, block), :]
                prompt_bias = jnp.concatenate([prompt_bias, prompt_bias], axis=0)
                lane = iota((block, HD), 1)
                logs = jnp.zeros((block, HD), jnp.float32)
                for c in range(0, HALF, 2):
                    at_c = [base + (c + n) * HD for n in range(2)]
                    pair = jnp.concatenate([got[here, n : n + HD] for n in at_c], axis=0)
                    cached = dot(pair, keys[region, :], NT) + cached_mask[slot : slot + 1, :]
                    prompt = dot(pair, prompt_keys, NT) + prompt_bias
                    top = jnp.maximum(
                        jnp.max(cached, axis=1, keepdims=True),
                        jnp.max(prompt, axis=1, keepdims=True),
                    )
                    if hit_count > 1:
                        top = jnp.maximum(top, 0.1 * FLOOR)
                    cached = jnp.exp2((cached - top) * factor).astype(jnp.bfloat16)
                    prompt = jnp.exp2((prompt - top) * factor).astype(jnp.bfloat16)
                    summed = dot(cached, wide[region, :], NN) + dot(prompt, prompt_values, NN)
                    totals = summed[:, HD:]
                    if hit_count > 1:
                        totals = jnp.maximum(totals, 1.0)
                        level = top * SCALE + jnp.log(totals)
                        logs = jnp.where(lane == c, level[:block], logs)
                        logs = jnp.where(lane == c + 1, level[block:], logs)
                    result = (summed[:, :HD] / totals).astype(jnp.bfloat16)
                    for n in range(2):
                        column = first + (c + n) * HD
                        out[here, column : column + HD] = result[n * block : (n + 1) * block]
                for lse in levels:
                    lse[here, slot * HD : (slot + 1) * HD] = logs

            each_block(devices, one_block)


def unpack_kernel(devices, hit_count, places, *refs):
    outs, logs, result = refs[0], refs[1:-1], refs[-1]
    target = iota((devices * MSG, 2 * ROWS), 0)

    def chosen(s, i, dtype):
        place = s * hit_count + i
        return jnp.where(target == places[place : place + 1, :], 1.0, 0.0).astype(dtype)

    def rows_of(i):
        parts = [
            dot(chosen(s, i, jnp.bfloat16), outs[:, s * WIDE : (s + 1) * WIDE], TN)
            for s in range(CAP)
        ]
        return sum(parts[1:], parts[0])

    def logs_of(i):
        parts = [
            dot(
                chosen(s, i, jnp.float32),
                logs[0][:, s * HD : (s + 1) * HD],
                TN,
                precision=lax.Precision.HIGHEST,
            )
            for s in range(CAP)
        ]
        return sum(parts[1:], parts[0])

    if hit_count == 1:
        joined = rows_of(0)
    else:
        levels = [logs_of(i) for i in range(hit_count)]
        top = functools.reduce(jnp.maximum, levels)
        shares = [jnp.exp(level - top) for level in levels]
        total = sum(shares[1:], shares[0])
        pieces = [rows_of(i) for i in range(hit_count)]
        columns = []
        for c in range(HALF):
            part = sum(
                shares[i][:, c : c + 1] * pieces[i][:, c * HD : (c + 1) * HD]
                for i in range(hit_count)
            )
            columns.append(part / total[:, c : c + 1])
        joined = jnp.concatenate(columns, axis=1)
    joined = joined.astype(jnp.bfloat16)
    result[:, :WIDE] = joined[:ROWS]
    result[:, WIDE:] = joined[ROWS:]


def vmem(count):
    return [pl.BlockSpec(memory_space=pltpu.VMEM)] * count


def smem(count):
    return [pl.BlockSpec(memory_space=pltpu.SMEM)] * count


def hbm(count):
    return [pl.BlockSpec(memory_space=pltpu.HBM)] * count


def body(prefix_len, hits, span_block, queries, fresh_keys, fresh_values, cache_keys, cache_values):
    devices = lax.axis_size("cache")
    hit_count = hits.shape[1]
    rows = devices * MSG
    owners = hits.reshape(REQUESTS * hit_count)

    def exchange(x):
        return lax.all_to_all(x, "cache", split_axis=0, concat_axis=0, tiled=True)

    def call(kernel, out_shape, name, grant=40, **kw):
        return pl.pallas_call(
            functools.partial(kernel, devices, hit_count),
            out_shape=[jax.ShapeDtypeStruct(*leaf) for leaf in out_shape],
            compiler_params=pltpu.CompilerParams(vmem_limit_bytes=grant * 2**20),
            name=name,
            **kw,
        )

    send, places = call(
        pack_kernel,
        [((rows, CAP * (WIDE + HD)), jnp.bfloat16), ((CAP * hit_count, 2 * ROWS), jnp.int32)],
        "pack",
        grant=60,
        in_specs=smem(1) + hbm(3),
        out_specs=vmem(2),
        scratch_shapes=[
            pltpu.VMEM((2 * ROWS, WIDE + HD), jnp.bfloat16),
            pltpu.SMEM((devices,), jnp.int32),
            pltpu.SemaphoreType.DMA((4,)),
        ],
    )(owners, queries, fresh_keys, fresh_values)
    got = exchange(send)
    busy, prompt_mask, cached_mask, wide = call(
        prep_kernel,
        [
            ((CAP,), jnp.int32),
            ((CAP * rows, rows), jnp.float32),
            ((CAP, REGION), jnp.float32),
            ((CAP * REGION, 2 * HD), jnp.bfloat16),
        ],
        "prep",
        in_specs=smem(2) + vmem(2),
        out_specs=smem(1) + vmem(3),
        cost_estimate=pl.CostEstimate(flops=10**6, bytes_accessed=2**22, transcendentals=0),
    )(owners, prefix_len, span_block, cache_values)
    pairs = CAP * rows * HALF * (REGION + rows)
    answers = call(
        attend_kernel,
        [((rows, CAP * WIDE), jnp.bfloat16)]
        + [((rows, CAP * HD), jnp.float32)] * (hit_count > 1),
        "attend",
        in_specs=smem(1) + vmem(5),
        out_specs=vmem(1 + (hit_count > 1)),
        cost_estimate=pl.CostEstimate(
            flops=4 * pairs * HD, bytes_accessed=8 * rows * WIDE, transcendentals=pairs
        ),
    )(busy, prompt_mask, cached_mask, got, cache_keys, wide)
    returned = [exchange(answer) for answer in answers]
    return call(
        unpack_kernel,
        [((ROWS, HEADS * HD), jnp.bfloat16)],
        "unpack",
        in_specs=vmem(1 + len(returned)),
        out_specs=vmem(1),
    )(places, *returned)[0]


def solution(mesh):
    in_specs = (
        P("groups"),
        P("groups", None),
        P("groups", None),
        P(("groups", "cache"), None),
        P(("groups", "cache"), None),
        P(("groups", "cache"), None),
        P(("groups", "cache"), None),
        P(("groups", "cache"), None),
    )
    out_specs = P(("groups", "cache"), None)
    return jax.shard_map(body, mesh=mesh, in_specs=in_specs, out_specs=out_specs, check_vma=False)
```

time: 65 us -> 50.3 us (0.77)
  blocking collectives: 30.7 us -> 17.8 us
  Pallas kernels: 5.11 us -> 9.71 us
  waiting for transfers between devices: 17.5 us -> 14.1 us
  local copies, waits for them, and re-layouts: 3.75 us -> 0.71 us
    all_to_all x2 -> x1, blocking collectives: 30.7 us -> 17.8 us  [exchange(): return lax.all_to_all(x, 'cache', split_axis=0, concat_axis=0, tiled=True)]
    pallas_call x4, Pallas kernels: 5.11 us -> 9.71 us  [the longest x1 4.54 us: body(): call(attend_kernel, [((rows, CAP * WIDE), jnp.bfloat16)] + [((rows, CAP *...]
    all_to_all x2 -> x1, waiting for transfers between devices: 17.5 us -> 14.1 us  [exchange(): return lax.all_to_all(x, 'cache', split_axis=0, concat_axis=0, tiled=True)]
    unnamed x15 -> x12, local copies, waits for them, and re-layouts: 3.75 us -> 0.71 us
    all_to_all x2 -> x1, starting transfers between devices: 7.2 us -> 7.53 us  [exchange(): return lax.all_to_all(x, 'cache', split_axis=0, concat_axis=0, tiled=True)]
  transfers between devices with their start and end apart: 2 -> 1, of which waited for: 2 -> 1; matrix products, arithmetic and copies ran while one was open for 0% -> 0% of each run, Pallas kernels for 4% -> 3%
where the time goes in v2:
time: 50.3 us; the launch traced here: 50 us
  blocking collectives  17.8 us (35%)
  waiting for transfers between devices  14.1 us (28%)
  Pallas kernels  9.71 us (19%)
  starting transfers between devices  7.53 us (15%)
  local copies, waits for them, and re-layouts  0.71 us (1%)
    all_to_all x1, blocking collectives, exchange(): return lax.all_to_all(x, 'cache', split_axis=0, concat_axis=0, tiled=True)  17.8 us
    all_to_all x1, waiting for transfers between devices, exchange(): return lax.all_to_all(x, 'cache', split_axis=0, concat_axis=0, tiled=True)  14.1 us
    all_to_all x1, starting transfers between devices, exchange(): return lax.all_to_all(x, 'cache', split_axis=0, concat_axis=0, tiled=True)  7.53 us
    pallas_call x1, Pallas kernels, body(): call(attend_kernel, [((rows, CAP * WIDE), jnp.bfloat16)] + [((rows, CAP *...  4.54 us
    pallas_call x1, Pallas kernels, body(): call(pack_kernel, [((rows, CAP * (WIDE + HD)), jnp.bfloat16), ((CAP * hit...  2.79 us
    pallas_call x1, Pallas kernels, body(): call(prep_kernel, [((CAP,), jnp.int32), ((CAP * rows, rows), jnp.float32)...  1.35 us
    pallas_call x1, Pallas kernels, body(): call(unpack_kernel, [((ROWS, HEADS * HD), jnp.bfloat16)], 'unpack', in_sp...  1.03 us
  transfers between devices with their start and end apart: 1, of which 1 were waited for; matrix products, arithmetic and copies ran while one was open for 0% of the time, Pallas kernels for 3%

profile of v2, /device:TPU:0, one launch (start us, length us, event | category | flops | bytes accessed | tf_op | source)
XLA Modules:
  0.0 50.0 jit_solution(13092897769508525098)
XLA Ops:
  0.0 2.8 %pack.1 = (bf16[128,2304]{1,0:T(8,128)(2,1)}, s32[2,128]{1,0:T(2,128)}) custom-call(s32[16]{0:T(128)} %bitcast.8, bf16[64,2048]{1,0:T(8,128)(2,1)} %q.1, bf16[64,128]{1,0:T(8,128)(2,1)} %k.1, bf16[64,128]{1,0:T(8,128)(2,1)} %v.1), custom_call_target="tpu_custom_call" | custom-call | tf_op jit(solution)/shard_map/pack/pallas_call | solution.py:273
  2.8 0.0 copy-start
  2.8 0.0 copy-start.1
  2.8 0.0 copy-start.2
  2.8 0.0 copy-start.4
  2.8 7.5 %all-to-all-start = ((bf16[16,8,2304]{2,1,0:T(8,128)(2,1)}), bf16[16,8,2304]{2,1,0:T(8,128)(2,1)S(1)}, u32[]{:S(2)}, u32[]{:S(2)}) async-start(bf16[16,8,2304]{2,1,0:T(8,128)(2,1)} %bitcast.10), calls=%async_computation | async-start | bytes 1179648 | tf_op jit(solution)/shard_map/all_to_all | solution.py:262
  10.4 0.0 copy-done
  10.4 0.0 copy-done.1
  10.4 0.0 copy-done.2
  10.4 0.0 copy-done.4
  10.4 0.0 copy-start.5
  10.4 1.3 %prep.1 = (s32[2]{0:T(128)S(1)}, f32[256,128]{1,0:T(8,128)S(1)}, f32[2,1024]{1,0:T(2,128)S(1)}, bf16[2048,256]{1,0:T(8,128)(2,1)S(1)}) custom-call(s32[16]{0:T(128)S(1)} %bitcast.9, s32[16]{0:T(128)S(1)} %copy-done.4, s32[16,16]{1,0:T(8,128)S(1)} %copy-done.1, bf16[2048,128]{1,0:T(8,128)(2,1)S(1)} %copy-done), custom_call_target="tpu_custom_call" | custom-call | flops 1000000 | bytes 4194304 | tf_op jit(solution)/shard_map/prep/pallas_call | solution.py:287
  11.8 14.1 %all-to-all-done = bf16[16,8,2304]{2,1,0:T(8,128)(2,1)S(1)} async-done(((bf16[16,8,2304]{2,1,0:T(8,128)(2,1)}), bf16[16,8,2304]{2,1,0:T(8,128)(2,1)S(1)}, u32[]{:S(2)}, u32[]{:S(2)}) %all-to-all-start) | async-done | bytes 589856 | tf_op jit(solution)/shard_map/all_to_all | solution.py:262
  25.9 0.0 copy-done.5
  25.9 4.5 %attend.1 = bf16[128,2048]{1,0:T(8,128)(2,1)S(1)} custom-call(s32[2]{0:T(128)S(1)} %get-tuple-element.12.busy, f32[256,128]{1,0:T(8,128)S(1)} %get-tuple-element.13.prompt_mask, f32[2,1024]{1,0:T(2,128)S(1)} %get-tuple-element.14.cached_mask, bf16[128,2304]{1,0:T(8,128)(2,1)S(1)} %bitcast.6, bf16[2048,128]{1,0:T(8,128)(2,1)S(1)} %copy-done.5, ...), custom_call_target="tpu_custom_call" | custom-call | flops 1207959552 | bytes 1048576 | tf_op jit(solution)/shard_map/attend/pallas_call | solution.py:301
  30.5 17.8 %all_to_all.22 = bf16[16,8,2048]{2,1,0:T(8,128)(2,1)S(1)} all-to-all(bf16[16,8,2048]{2,1,0:T(8,128)(2,1)S(1)} %bitcast.7), channel_id=1, replica_groups=mesh['groups'=2,'cache'=16] {'cache'}, dimensions={0} | all-to-all | bytes 1048576 | tf_op jit(solution)/shard_map/all_to_all | solution.py:262
  48.3 0.0 copy-start.3
  48.3 0.7 %copy-done.3 = s32[2,128]{1,0:T(2,128)S(1)} copy-done((s32[2,128]{1,0:T(2,128)S(1)}, s32[2,128]{1,0:T(2,128)}, u32[]{:S(2)}) %copy-start.3) | copy-done | bytes 1048
  49.0 1.0 %unpack.1 = bf16[64,2048]{1,0:T(8,128)(2,1)} custom-call(s32[2,128]{1,0:T(2,128)S(1)} %copy-done.3, bf16[128,2048]{1,0:T(8,128)(2,1)S(1)} %bitcast.5), custom_call_target="tpu_custom_call" | custom-call | tf_op jit(solution)/shard_map/unpack/pallas_call | solution.py:313
Async XLA Ops:
  2.8 7.6 %copy-start = (bf16[2048,128]{1,0:T(8,128)(2,1)S(1)}, bf16[2048,128]{1,0:T(8,128)(2,1)}, u32[]{:S(2)}) copy-start(bf16[2048,128]{1,0:T(8,128)(2,1)} %values.1) | copy-start | bytes 1572868
  2.8 7.6 %copy-start.1 = (s32[16,16]{1,0:T(8,128)S(1)}, s32[16,16]{1,0:T(8,128)}, u32[]{:S(2)}) copy-start(s32[16,16]{1,0:T(8,128)} %span.1) | copy-start | bytes 3076
  2.8 7.6 %copy-start.2 = (s32[16,1]{0,1:T(1,128)S(1)}, s32[16,1]{0,1:T(1,128)}, u32[]{:S(2)}) copy-start(s32[16,1]{0,1:T(1,128)} %param.9) | copy-start | bytes 196
  2.8 7.6 %copy-start.4 = (s32[16]{0:T(128)S(1)}, s32[16]{0:T(128)}, u32[]{:S(2)}) copy-start(s32[16]{0:T(128)} %prefix_len.1) | copy-start | bytes 196
  2.8 23.1 %all-to-all-start = ((bf16[16,8,2304]{2,1,0:T(8,128)(2,1)}), bf16[16,8,2304]{2,1,0:T(8,128)(2,1)S(1)}, u32[]{:S(2)}, u32[]{:S(2)}) async-start(bf16[16,8,2304]{2,1,0:T(8,128)(2,1)} %bitcast.10), calls=%async_computation | async-start | bytes 1179648 | tf_op jit(solution)/shard_map/all_to_all | solution.py:262
  10.4 15.5 %copy-start.5 = (bf16[2048,128]{1,0:T(8,128)(2,1)S(1)}, bf16[2048,128]{1,0:T(8,128)(2,1)}, u32[]{:S(2)}) copy-start(bf16[2048,128]{1,0:T(8,128)(2,1)} %keys.1) | copy-start | bytes 1572868
  48.3 0.7 %copy-start.3 = (s32[2,128]{1,0:T(2,128)S(1)}, s32[2,128]{1,0:T(2,128)}, u32[]{:S(2)}) copy-start(s32[2,128]{1,0:T(2,128)} %get-tuple-element.11.places) | copy-start | bytes 3076

commit v3 on v2

--- a/solution.py
+++ b/solution.py
@@ -36,7 +36,17 @@
     return lax.dot_general(a, b, dims, preferred_element_type=jnp.float32, **kw)
 
 
-def pack_kernel(devices, hit_count, hits, q, k, v, send, places, held, count, sems):
+def pairwise(devices):
+    return devices <= 16
+
+
+def partner(devices, me, order):
+    return order ^ me if pairwise(devices) else order
+
+
+def pack_kernel(devices, hit_count, hits, q, k, v, *refs):
+    *sends, places, held, count, sems = refs
+    me = lax.axis_index("cache")
     copies = [
         pltpu.make_async_copy(source, held.at[pl.ds(row, ROWS), pl.ds(column, width)], sems.at[n])
         for n, (source, row, column, width) in enumerate(
@@ -61,8 +71,9 @@
             owner = hits[r * hit_count + i]
             rank = count[owner]
             count[owner] = rank + 1
+            message = partner(devices, me, owner) * MSG
             for s in range(CAP):
-                place = jnp.where(rank == s, owner * MSG, -4 * MSG)
+                place = jnp.where(rank == s, message, -4 * MSG)
                 rows[s][i] = jnp.where(lane_request == r, place, rows[s][i])
     inner = lane // ROWS * TOK_REQ + lane % TOK_REQ
     target = iota((devices * MSG, 2 * ROWS), 0)
@@ -79,7 +90,10 @@
         copy.wait()
     for s in range(CAP):
         here = slice(s * (WIDE + HD), (s + 1) * (WIDE + HD))
-        send[:, here] = dot(picks[s], held[...], NN).astype(jnp.bfloat16)
+        packed = dot(picks[s], held[...], NN).astype(jnp.bfloat16)
+        height = packed.shape[0] // len(sends)
+        for m, send in enumerate(sends):
+            send[:, here] = packed[m * height : (m + 1) * height]
 
 
 def prep_kernel(devices, hit_count, hits, prefix_len, span, values, busy, prompt, cached, wide):
@@ -102,7 +116,7 @@
         limit = prefix_len[request] - which * REGION
         cached[slot : slot + 1, :] = jnp.where(iota((1, REGION), 1) < limit, 0.0, FLOOR)
         span_row = span[pl.ds(request, 1), :].astype(jnp.float32)
-        source = iota((devices, total_rows), 0)
+        source = partner(devices, me, iota((devices, total_rows), 0))
         spread = (iota((devices, total_rows), 1) // MSG == source).astype(jnp.bfloat16)
         spans = jnp.broadcast_to(span_row, (16, devices)).astype(jnp.bfloat16)
         key_span = dot(spans, spread, NN)[:1]
@@ -115,7 +129,7 @@
         block = 16 * MSG
 
         def one_block(at):
-            row_source = at * 16 + iota((block, devices), 0) // MSG
+            row_source = partner(devices, me, at * 16 + iota((block, devices), 0) // MSG)
             mine = iota((block, devices), 1) == row_source
             row_span = jnp.sum(jnp.where(mine, span_row, 0.0), axis=1, keepdims=True)
             row_spot = row_span.astype(jnp.int32) * TOK_REQ + iota((block, 1), 0) % TOK_REQ
@@ -133,7 +147,15 @@
         pl.loop(0, blocks)(one_block)
 
 
-def attend_kernel(devices, hit_count, busy, prompt_mask, cached_mask, got, keys, wide, out, *levels):
+def attend_kernel(devices, hit_count, busy, prompt_mask, cached_mask, keys, wide, *refs):
+    parts = devices if pairwise(devices) else 1
+    gots, outs, levels, got = refs[:parts], refs[parts : 2 * parts], refs[2 * parts : -1], refs[-1]
+    if parts == 1:
+        got, levels = gots[0], refs[2:]
+    else:
+        for m in range(parts):
+            got[m * MSG : (m + 1) * MSG, :] = gots[m][...]
+    height = devices * MSG // parts
     total_rows = devices * MSG
     block = 16 * MSG
     factor = SCALE * math.log2(math.e)
@@ -144,7 +166,8 @@
 
         @pl.when(busy[slot] == 0)
         def _():
-            out[:, first : first + WIDE] = jnp.zeros((total_rows, WIDE), jnp.bfloat16)
+            for out in outs:
+                out[:, first : first + WIDE] = jnp.zeros((height, WIDE), jnp.bfloat16)
             for lse in levels:
                 lse[:, slot * HD : (slot + 1) * HD] = jnp.zeros((total_rows, HD), jnp.float32)
 
@@ -185,7 +208,12 @@
                     result = (summed[:, :HD] / totals).astype(jnp.bfloat16)
                     for n in range(2):
                         column = first + (c + n) * HD
-                        out[here, column : column + HD] = result[n * block : (n + 1) * block]
+                        if parts == 1:
+                            rows = result[n * block : (n + 1) * block]
+                            outs[0][here, column : column + HD] = rows
+                        for m in range(parts if parts > 1 else 0):
+                            rows = result[n * block + m * MSG : n * block + (m + 1) * MSG]
+                            outs[m][:, column : column + HD] = rows
                 for lse in levels:
                     lse[here, slot * HD : (slot + 1) * HD] = logs
 
@@ -193,7 +221,9 @@
 
 
 def unpack_kernel(devices, hit_count, places, *refs):
-    outs, logs, result = refs[0], refs[1:-1], refs[-1]
+    parts = devices if pairwise(devices) else 1
+    logs, result = refs[parts:-1], refs[-1]
+    outs = jnp.concatenate([part[...] for part in refs[:parts]], axis=0) if parts > 1 else refs[0]
     target = iota((devices * MSG, 2 * ROWS), 0)
 
     def chosen(s, i, dtype):
@@ -258,8 +288,16 @@
     rows = devices * MSG
     owners = hits.reshape(REQUESTS * hit_count)
 
-    def exchange(x):
+    def together(x):
         return lax.all_to_all(x, "cache", split_axis=0, concat_axis=0, tiled=True)
+
+    def exchange(messages):
+        if not pairwise(devices):
+            return [together(x) for x in messages]
+        moved = list(messages)
+        for m in reversed(range(1, devices)):
+            moved[m] = lax.ppermute(messages[m], "cache", [(d, d ^ m) for d in range(devices)])
+        return moved
 
     def call(kernel, out_shape, name, grant=40, **kw):
         return pl.pallas_call(
@@ -270,20 +308,22 @@
             **kw,
         )
 
-    send, places = call(
+    parts = devices if pairwise(devices) else 1
+    *sends, places = call(
         pack_kernel,
-        [((rows, CAP * (WIDE + HD)), jnp.bfloat16), ((CAP * hit_count, 2 * ROWS), jnp.int32)],
+        [((rows // parts, CAP * (WIDE + HD)), jnp.bfloat16)] * parts
+        + [((CAP * hit_count, 2 * ROWS), jnp.int32)],
         "pack",
         grant=60,
         in_specs=smem(1) + hbm(3),
-        out_specs=vmem(2),
+        out_specs=vmem(parts + 1),
         scratch_shapes=[
             pltpu.VMEM((2 * ROWS, WIDE + HD), jnp.bfloat16),
             pltpu.SMEM((devices,), jnp.int32),
             pltpu.SemaphoreType.DMA((4,)),
         ],
     )(owners, queries, fresh_keys, fresh_values)
-    got = exchange(send)
+    got = exchange(sends)
     busy, prompt_mask, cached_mask, wide = call(
         prep_kernel,
         [
@@ -300,16 +340,24 @@
     pairs = CAP * rows * HALF * (REGION + rows)
     answers = call(
         attend_kernel,
-        [((rows, CAP * WIDE), jnp.bfloat16)]
+        [((rows // parts, CAP * WIDE), jnp.bfloat16)] * parts
         + [((rows, CAP * HD), jnp.float32)] * (hit_count > 1),
         "attend",
-        in_specs=smem(1) + vmem(5),
-        out_specs=vmem(1 + (hit_count > 1)),
+        in_specs=smem(1) + vmem(4 + parts),
+        out_specs=vmem(parts + (hit_count > 1)),
+        scratch_shapes=[pltpu.VMEM((rows, CAP * (WIDE + HD)), jnp.bfloat16)] * (parts > 1),
         cost_estimate=pl.CostEstimate(
             flops=4 * pairs * HD, bytes_accessed=8 * rows * WIDE, transcendentals=pairs
         ),
-    )(busy, prompt_mask, cached_mask, got, cache_keys, wide)
-    returned = [exchange(answer) for answer in answers]
+    )(busy, prompt_mask, cached_mask, cache_keys, wide, *got)
+    returned = exchange(answers[:parts])
+    for level in answers[parts:]:
+        if pairwise(devices):
+            blocks = level.reshape(devices, MSG, CAP * HD)
+            level = jnp.concatenate(exchange([blocks[m] for m in range(devices)]), axis=0)
+        else:
+            level = together(level)
+        returned.append(level)
     return call(
         unpack_kernel,
         [((ROWS, HEADS * HD), jnp.bfloat16)],

time: 50.3 us -> 61.6 us (1.22)
  starting transfers between devices: 7.53 us -> 44.1 us
  blocking collectives: 17.8 us -> 0 us
  waiting for transfers between devices: 14.1 us -> 7.04 us
  Pallas kernels: 9.71 us -> 7.76 us
  local copies, waits for them, and re-layouts: 0.71 us -> 2.49 us
    ppermute x0 -> x30, starting transfers between devices: none -> 44.1 us  [exchange(): lax.ppermute(messages[m], 'cache', [(d, d ^ m) for d in range(devices)])]
    all_to_all x1 -> x0, blocking collectives: 17.8 us -> none  [exchange(): return lax.all_to_all(x, 'cache', split_axis=0, concat_axis=0, tiled=True)]
    all_to_all x1 -> x0, waiting for transfers between devices: 14.1 us -> none  [exchange(): return lax.all_to_all(x, 'cache', split_axis=0, concat_axis=0, tiled=True)]
    all_to_all x1 -> x0, starting transfers between devices: 7.53 us -> none  [exchange(): return lax.all_to_all(x, 'cache', split_axis=0, concat_axis=0, tiled=True)]
    ppermute x0 -> x30, waiting for transfers between devices: none -> 7.04 us  [exchange(): lax.ppermute(messages[m], 'cache', [(d, d ^ m) for d in range(devices)])]
    pallas_call x2, Pallas kernels: 7.33 us -> 5.39 us  [the longest x1 2.75 us: body(): call(pack_kernel, [((rows // parts, CAP * (WIDE + HD)), jnp.bfloat16)] *...]
    unnamed x12 -> x14, local copies, waits for them, and re-layouts: 0.71 us -> 2.49 us
  transfers between devices with their start and end apart: 1 -> 30, of which waited for: 1 -> 5; matrix products, arithmetic and copies ran while one was open for 0% -> 0% of each run, Pallas kernels for 3% -> 2%
where the time goes in v3:
time: 61.6 us; the launch traced here: 61.5 us
  starting transfers between devices  44.1 us (72%)
  Pallas kernels  7.76 us (13%)
  waiting for transfers between devices  7.04 us (11%)
  local copies, waits for them, and re-layouts  2.49 us (4%)
    ppermute x30, starting transfers between devices, exchange(): lax.ppermute(messages[m], 'cache', [(d, d ^ m) for d in range(devices)])  44.1 us
    ppermute x30, waiting for transfers between devices, exchange(): lax.ppermute(messages[m], 'cache', [(d, d ^ m) for d in range(devices)])  7.04 us
    pallas_call x1, Pallas kernels, body(): call(pack_kernel, [((rows // parts, CAP * (WIDE + HD)), jnp.bfloat16)] *...  2.75 us
    pallas_call x1, Pallas kernels, body(): call(attend_kernel, [((rows // parts, CAP * WIDE), jnp.bfloat16)] * parts...  2.63 us
    unnamed x14, local copies, waits for them, and re-layouts  2.49 us
    pallas_call x1, Pallas kernels, body(): call(prep_kernel, [((CAP,), jnp.int32), ((CAP * rows, rows), jnp.float32)...  1.35 us
  transfers between devices with their start and end apart: 30, of which 5 were waited for; matrix products, arithmetic and copies ran while one was open for 0% of the time, Pallas kernels for 2%

profile of v3, /device:TPU:0, one launch (start us, length us, event | category | flops | bytes accessed | tf_op | source)
XLA Modules:
  0.0 61.5 jit_solution(7108598838369933757)
XLA Ops:
  0.0 2.8 %pack.1 = (bf16[8,2304]{1,0:T(8,128)(2,1)}, bf16[8,2304]{1,0:T(8,128)(2,1)}, bf16[8,2304]{1,0:T(8,128)(2,1)}, bf16[8,2304]{1,0:T(8,128)(2,1)}, bf16[8,2304]{1,0:...) custom-call(s32[16]{0:T(128)} %bitcast.1, ...), custom_call_target="tpu_custom_call" | custom-call | tf_op jit(solution)/shard_map/pack/pallas_call | solution.py:312
  2.8 0.5 collective-permute-start
  3.3 2.6 %collective-permute-start.1 = (bf16[8,2304]{1,0:T(8,128)(2,1)}, bf16[8,2304]{1,0:T(8,128)(2,1)S(1)}, u32[]{:S(2)}, u32[]{:S(2)}) collective-permute-start(bf16[8,2304]{1,0:T(8,128)(2,1)} %get-tuple-element.49), channel_id=1, source_target_pairs={{0,2},{1,3},{2,0},{3,1},{4,6},{5,7},{6,4},{7,5},{8,10},{9,11},{10,... | collective-permute-start | bytes 110600 | tf_op jit(solution)/shard_map/ppermute | solution.py:299
  5.9 0.1 collective-permute-start.2
  5.9 1.8 %collective-permute-start.3 = (bf16[8,2304]{1,0:T(8,128)(2,1)}, bf16[8,2304]{1,0:T(8,128)(2,1)S(1)}, u32[]{:S(2)}, u32[]{:S(2)}) collective-permute-start(bf16[8,2304]{1,0:T(8,128)(2,1)} %get-tuple-element.51), channel_id=1, source_target_pairs={{0,4},{1,5},{2,6},{3,7},{4,0},{5,1},{6,2},{7,3},{8,12},{9,13},{10,... | collective-permute-start | bytes 110600 | tf_op jit(solution)/shard_map/ppermute | solution.py:299
  7.7 0.0 collective-permute-start.4
  7.7 0.0 collective-permute-done.refs_1_
  7.7 2.6 %collective-permute-start.5 = (bf16[8,2304]{1,0:T(8,128)(2,1)}, bf16[8,2304]{1,0:T(8,128)(2,1)S(1)}, u32[]{:S(2)}, u32[]{:S(2)}) collective-permute-start(bf16[8,2304]{1,0:T(8,128)(2,1)} %get-tuple-element.53), channel_id=1, source_target_pairs={{0,6},{1,7},{2,4},{3,5},{4,2},{5,3},{6,0},{7,1},{8,14},{9,15},{10,... | collective-permute-start | bytes 110600 | tf_op jit(solution)/shard_map/ppermute | solution.py:299
  10.4 0.0 collective-permute-done.1.refs_2_
  10.4 0.1 collective-permute-start.6
  10.5 0.0 collective-permute-done.2.refs_3_
  10.5 2.6 %collective-permute-start.7 = (bf16[8,2304]{1,0:T(8,128)(2,1)}, bf16[8,2304]{1,0:T(8,128)(2,1)S(1)}, u32[]{:S(2)}, u32[]{:S(2)}) collective-permute-start(bf16[8,2304]{1,0:T(8,128)(2,1)} %get-tuple-element.55), channel_id=1, source_target_pairs={{0,8},{1,9},{2,10},{3,11},{4,12},{5,13},{6,14},{7,15},{8,0},{9,1},... | collective-permute-start | bytes 110600 | tf_op jit(solution)/shard_map/ppermute | solution.py:299
  13.1 0.0 collective-permute-done.3.refs_4_
  13.1 0.6 %collective-permute-start.8 = (bf16[8,2304]{1,0:T(8,128)(2,1)}, bf16[8,2304]{1,0:T(8,128)(2,1)S(1)}, u32[]{:S(2)}, u32[]{:S(2)}) collective-permute-start(bf16[8,2304]{1,0:T(8,128)(2,1)} %get-tuple-element.56), channel_id=1, source_target_pairs={{0,9},{1,8},{2,11},{3,10},{4,13},{5,12},{6,15},{7,14},{8,1},{9,0},... | collective-permute-start | bytes 110600 | tf_op jit(solution)/shard_map/ppermute | solution.py:299
  13.8 0.0 collective-permute-done.4.refs_5_
  13.8 2.9 %collective-permute-start.9 = (bf16[8,2304]{1,0:T(8,128)(2,1)}, bf16[8,2304]{1,0:T(8,128)(2,1)S(1)}, u32[]{:S(2)}, u32[]{:S(2)}) collective-permute-start(bf16[8,2304]{1,0:T(8,128)(2,1)} %get-tuple-element.57), channel_id=1, source_target_pairs={{0,10},{1,11},{2,8},{3,9},{4,14},{5,15},{6,12},{7,13},{8,2},{9,3},... | collective-permute-start | bytes 110600 | tf_op jit(solution)/shard_map/ppermute | solution.py:299
  16.7 0.0 collective-permute-done.5.refs_6_
  16.7 0.3 collective-permute-start.10
  17.0 0.0 collective-permute-done.6.refs_7_
  17.0 3.3 %collective-permute-start.11 = (bf16[8,2304]{1,0:T(8,128)(2,1)}, bf16[8,2304]{1,0:T(8,128)(2,1)S(1)}, u32[]{:S(2)}, u32[]{:S(2)}) collective-permute-start(bf16[8,2304]{1,0:T(8,128)(2,1)} %get-tuple-element.59), channel_id=1, source_target_pairs={{0,12},{1,13},{2,14},{3,15},{4,8},{5,9},{6,10},{7,11},{8,4},{9,5},... | collective-permute-start | bytes 110600 | tf_op jit(solution)/shard_map/ppermute | solution.py:299
  20.4 0.0 collective-permute-done.7.refs_8_
  20.4 0.5 collective-permute-start.12
  20.9 0.0 collective-permute-done.8.refs_9_
  20.9 3.9 %collective-permute-start.13 = (bf16[8,2304]{1,0:T(8,128)(2,1)}, bf16[8,2304]{1,0:T(8,128)(2,1)S(1)}, u32[]{:S(2)}, u32[]{:S(2)}) collective-permute-start(bf16[8,2304]{1,0:T(8,128)(2,1)} %get-tuple-element.61), channel_id=1, source_target_pairs={{0,14},{1,15},{2,12},{3,13},{4,10},{5,11},{6,8},{7,9},{8,6},{9,7},... | collective-permute-start | bytes 110600 | tf_op jit(solution)/shard_map/ppermute | solution.py:299
  24.8 0.0 collective-permute-done.9.refs_10_
  24.8 0.3 collective-permute-start.14
  25.2 1.0 %copy-done = bf16[2048,128]{1,0:T(8,128)(2,1)S(1)} copy-done((bf16[2048,128]{1,0:T(8,128)(2,1)S(1)}, bf16[2048,128]{1,0:T(8,128)(2,1)}, u32[]{:S(2)}) %copy-start) | copy-done | bytes 524312
  26.2 1.3 %prep.1 = (s32[2]{0:T(128)S(1)}, f32[256,128]{1,0:T(8,128)S(1)}, f32[2,1024]{1,0:T(2,128)S(1)}, bf16[2048,256]{1,0:T(8,128)(2,1)S(1)}) custom-call(s32[16]{0:T(128)S(1)} %bitcast.2, s32[16]{0:T(128)S(1)} %copy-done.4, s32[16,16]{1,0:T(8,128)S(1)} %copy-done.1, bf16[2048,128]{1,0:T(8,128)(2,1)S(1)} %copy-done), custom_call_target="tpu_custom_call" | custom-call | flops 1000000 | bytes 4194304 | tf_op jit(solution)/shard_map/prep/pallas_call | solution.py:327
  27.6 0.0 collective-permute-done.10.refs_11_
  27.6 0.0 collective-permute-done.11.refs_12_
  27.6 0.0 collective-permute-done.12.refs_13_
  27.6 0.4 collective-permute-done.13.refs_14_
  28.0 3.3 %collective-permute-done.14.refs_15_ = bf16[8,2304]{1,0:T(8,128)(2,1)S(1)} collective-permute-done((bf16[8,2304]{1,0:T(8,128)(2,1)}, bf16[8,2304]{1,0:T(8,128)(2,1)S(1)}, u32[]{:S(2)}, u32[]{:S(2)}) %collective-permute-start.14) | collective-permute-done | bytes 36896 | tf_op jit(solution)/shard_map/ppermute | solution.py:299
  31.3 0.8 %copy-done.6 = bf16[8,2304]{1,0:T(8,128)(2,1)S(1)} copy-done((bf16[8,2304]{1,0:T(8,128)(2,1)S(1)}, bf16[8,2304]{1,0:T(8,128)(2,1)}, u32[]{:S(2)}) %copy-start.6) | copy-done | bytes 36888
  32.0 2.6 %attend.1 = (bf16[8,2048]{1,0:T(8,128)(2,1)S(1)}, bf16[8,2048]{1,0:T(8,128)(2,1)S(1)}, bf16[8,2048]{1,0:T(8,128)(2,1)S(1)}, bf16[8,2048]{1,0:T(8,128)(2,1)S(1)},...) custom-call(s32[2]{0:T(128)S(1)} %get-tuple-element.43.busy, ...), custom_call_target="tpu_custom_call" | custom-call | flops 1207959552 | bytes 1048576 | tf_op jit(solution)/shard_map/attend/pallas_call | solution.py:341
  34.7 2.2 %collective-permute-start.15 = (bf16[8,2048]{1,0:T(8,128)(2,1)S(1)}, bf16[8,2048]{1,0:T(8,128)(2,1)S(1)}, u32[]{:S(2)}, u32[]{:S(2)}) collective-permute-start(bf16[8,2048]{1,0:T(8,128)(2,1)S(1)} %get-tuple-element.64), channel_id=1, source_target_pairs={{0,1},{1,0},{2,3},{3,2},{4,5},{5,4},{6,7},{7,6},{8,9},{9,8},{10,11... | collective-permute-start | bytes 98312 | tf_op jit(solution)/shard_map/ppermute | solution.py:299
  36.9 0.5 collective-permute-start.16
  37.3 1.0 %collective-permute-start.17 = (bf16[8,2048]{1,0:T(8,128)(2,1)S(1)}, bf16[8,2048]{1,0:T(8,128)(2,1)S(1)}, u32[]{:S(2)}, u32[]{:S(2)}) collective-permute-start(bf16[8,2048]{1,0:T(8,128)(2,1)S(1)} %get-tuple-element.66), channel_id=1, source_target_pairs={{0,3},{1,2},{2,1},{3,0},{4,7},{5,6},{6,5},{7,4},{8,11},{9,10},{10,... | collective-permute-start | bytes 98312 | tf_op jit(solution)/shard_map/ppermute | solution.py:299
  38.3 0.0 collective-permute-start.18
  38.3 2.1 %collective-permute-start.19 = (bf16[8,2048]{1,0:T(8,128)(2,1)S(1)}, bf16[8,2048]{1,0:T(8,128)(2,1)S(1)}, u32[]{:S(2)}, u32[]{:S(2)}) collective-permute-start(bf16[8,2048]{1,0:T(8,128)(2,1)S(1)} %get-tuple-element.68), channel_id=1, source_target_pairs={{0,5},{1,4},{2,7},{3,6},{4,1},{5,0},{6,3},{7,2},{8,13},{9,12},{10,... | collective-permute-start | bytes 98312 | tf_op jit(solution)/shard_map/ppermute | solution.py:299
  40.4 0.0 collective-permute-done.15.refs_1_
  40.4 0.2 collective-permute-start.20
  40.6 0.4 collective-permute-done.16.refs_2_
  41.0 1.7 %collective-permute-start.21 = (bf16[8,2048]{1,0:T(8,128)(2,1)S(1)}, bf16[8,2048]{1,0:T(8,128)(2,1)S(1)}, u32[]{:S(2)}, u32[]{:S(2)}) collective-permute-start(bf16[8,2048]{1,0:T(8,128)(2,1)S(1)} %get-tuple-element.70), channel_id=1, source_target_pairs={{0,7},{1,6},{2,5},{3,4},{4,3},{5,2},{6,1},{7,0},{8,15},{9,14},{10,... | collective-permute-start | bytes 98312 | tf_op jit(solution)/shard_map/ppermute | solution.py:299
  42.7 0.0 collective-permute-done.17.refs_3_
  42.7 0.0 collective-permute-start.22
  42.7 0.0 collective-permute-done.18.refs_4_
  42.7 3.0 %collective-permute-start.23 = (bf16[8,2048]{1,0:T(8,128)(2,1)S(1)}, bf16[8,2048]{1,0:T(8,128)(2,1)S(1)}, u32[]{:S(2)}, u32[]{:S(2)}) collective-permute-start(bf16[8,2048]{1,0:T(8,128)(2,1)S(1)} %get-tuple-element.72), channel_id=1, source_target_pairs={{0,9},{1,8},{2,11},{3,10},{4,13},{5,12},{6,15},{7,14},{8,1},{9,0},... | collective-permute-start | bytes 98312 | tf_op jit(solution)/shard_map/ppermute | solution.py:299
  45.7 0.0 collective-permute-done.19.refs_5_
  45.7 0.3 collective-permute-start.24
  46.0 0.0 collective-permute-done.20.refs_6_
  46.0 2.9 %collective-permute-start.25 = (bf16[8,2048]{1,0:T(8,128)(2,1)S(1)}, bf16[8,2048]{1,0:T(8,128)(2,1)S(1)}, u32[]{:S(2)}, u32[]{:S(2)}) collective-permute-start(bf16[8,2048]{1,0:T(8,128)(2,1)S(1)} %get-tuple-element.74), channel_id=1, source_target_pairs={{0,11},{1,10},{2,9},{3,8},{4,15},{5,14},{6,13},{7,12},{8,3},{9,2},... | collective-permute-start | bytes 98312 | tf_op jit(solution)/shard_map/ppermute | solution.py:299
  48.9 0.0 collective-permute-done.21.refs_7_
  48.9 0.2 collective-permute-start.26
  49.1 0.0 collective-permute-done.22.refs_8_
  49.1 3.7 %collective-permute-start.27 = (bf16[8,2048]{1,0:T(8,128)(2,1)S(1)}, bf16[8,2048]{1,0:T(8,128)(2,1)S(1)}, u32[]{:S(2)}, u32[]{:S(2)}) collective-permute-start(bf16[8,2048]{1,0:T(8,128)(2,1)S(1)} %get-tuple-element.76), channel_id=1, source_target_pairs={{0,13},{1,12},{2,15},{3,14},{4,9},{5,8},{6,11},{7,10},{8,5},{9,4},... | collective-permute-start | bytes 98312 | tf_op jit(solution)/shard_map/ppermute | solution.py:299
  52.8 0.0 collective-permute-done.23.refs_9_
  52.8 1.0 %collective-permute-start.28 = (bf16[8,2048]{1,0:T(8,128)(2,1)S(1)}, bf16[8,2048]{1,0:T(8,128)(2,1)S(1)}, u32[]{:S(2)}, u32[]{:S(2)}) collective-permute-start(bf16[8,2048]{1,0:T(8,128)(2,1)S(1)} %get-tuple-element.77), channel_id=1, source_target_pairs={{0,14},{1,15},{2,12},{3,13},{4,10},{5,11},{6,8},{7,9},{8,6},{9,7},... | collective-permute-start | bytes 98312 | tf_op jit(solution)/shard_map/ppermute | solution.py:299
  53.8 3.1 %collective-permute-start.29 = (bf16[8,2048]{1,0:T(8,128)(2,1)S(1)}, bf16[8,2048]{1,0:T(8,128)(2,1)S(1)}, u32[]{:S(2)}, u32[]{:S(2)}) collective-permute-start(bf16[8,2048]{1,0:T(8,128)(2,1)S(1)} %get-tuple-element.78), channel_id=1, source_target_pairs={{0,15},{1,14},{2,13},{3,12},{4,11},{5,10},{6,9},{7,8},{8,7},{9,6},... | collective-permute-start | bytes 98312 | tf_op jit(solution)/shard_map/ppermute | solution.py:299
  56.9 0.0 collective-permute-done.27.refs_13_
  56.9 2.5 %collective-permute-done.28.refs_14_ = bf16[8,2048]{1,0:T(8,128)(2,1)S(1)} collective-permute-done((bf16[8,2048]{1,0:T(8,128)(2,1)S(1)}, bf16[8,2048]{1,0:T(8,128)(2,1)S(1)}, u32[]{:S(2)}, u32[]{:S(2)}) %collective-permute-start.28) | collective-permute-done | bytes 32800 | tf_op jit(solution)/shard_map/ppermute | solution.py:299
  59.4 0.4 collective-permute-done.29.refs_15_
  59.8 0.7 %copy-done.3 = s32[2,128]{1,0:T(2,128)S(1)} copy-done((s32[2,128]{1,0:T(2,128)S(1)}, s32[2,128]{1,0:T(2,128)}, u32[]{:S(2)}) %copy-start.3) | copy-done | bytes 1048
  60.5 1.0 %unpack.1 = bf16[64,2048]{1,0:T(8,128)(2,1)} custom-call(s32[2,128]{1,0:T(2,128)S(1)} %copy-done.3, bf16[8,2048]{1,0:T(8,128)(2,1)S(1)} %get-tuple-element.63.refs_0_, bf16[8,2048]{1,0:T(8,128)(2,1)S(1)} %collective-permute-done.15.refs_1_, bf16[8,2048]{1,0:T(8,128)(2,1)S(1)} %collective-permute-done.16.refs_2_, ...), custom_call_target="tpu_custom_call" | custom-call | tf_op jit(solution)/shard_map/unpack/pallas_call | solution.py:361
  (14 shorter events, 0.0 us)
Async XLA Ops:
  2.8 5.0 %collective-permute-start = (bf16[8,2304]{1,0:T(8,128)(2,1)}, bf16[8,2304]{1,0:T(8,128)(2,1)S(1)}, u32[]{:S(2)}, u32[]{:S(2)}) collective-permute-start(bf16[8,2304]{1,0:T(8,128)(2,1)} %get-tuple-element.48), channel_id=1, source_target_pairs={{0,1},{1,0},{2,3},{3,2},{4,5},{5,4},{6,7},{7,6},{8,9},{9,8},{10,11... | collective-permute-start | bytes 110600 | tf_op jit(solution)/shard_map/ppermute | solution.py:299
  3.3 7.1 %collective-permute-start.1 = (bf16[8,2304]{1,0:T(8,128)(2,1)}, bf16[8,2304]{1,0:T(8,128)(2,1)S(1)}, u32[]{:S(2)}, u32[]{:S(2)}) collective-permute-start(bf16[8,2304]{1,0:T(8,128)(2,1)} %get-tuple-element.49), channel_id=1, source_target_pairs={{0,2},{1,3},{2,0},{3,1},{4,6},{5,7},{6,4},{7,5},{8,10},{9,11},{10,... | collective-permute-start | bytes 110600 | tf_op jit(solution)/shard_map/ppermute | solution.py:299
  5.9 4.6 %collective-permute-start.2 = (bf16[8,2304]{1,0:T(8,128)(2,1)}, bf16[8,2304]{1,0:T(8,128)(2,1)S(1)}, u32[]{:S(2)}, u32[]{:S(2)}) collective-permute-start(bf16[8,2304]{1,0:T(8,128)(2,1)} %get-tuple-element.50), channel_id=1, source_target_pairs={{0,3},{1,2},{2,1},{3,0},{4,7},{5,6},{6,5},{7,4},{8,11},{9,10},{10,... | collective-permute-start | bytes 110600 | tf_op jit(solution)/shard_map/ppermute | solution.py:299
  5.9 7.2 %collective-permute-start.3 = (bf16[8,2304]{1,0:T(8,128)(2,1)}, bf16[8,2304]{1,0:T(8,128)(2,1)S(1)}, u32[]{:S(2)}, u32[]{:S(2)}) collective-permute-start(bf16[8,2304]{1,0:T(8,128)(2,1)} %get-tuple-element.51), channel_id=1, source_target_pairs={{0,4},{1,5},{2,6},{3,7},{4,0},{5,1},{6,2},{7,3},{8,12},{9,13},{10,... | collective-permute-start | bytes 110600 | tf_op jit(solution)/shard_map/ppermute | solution.py:299
  7.7 6.0 %collective-permute-start.4 = (bf16[8,2304]{1,0:T(8,128)(2,1)}, bf16[8,2304]{1,0:T(8,128)(2,1)S(1)}, u32[]{:S(2)}, u32[]{:S(2)}) collective-permute-start(bf16[8,2304]{1,0:T(8,128)(2,1)} %get-tuple-element.52), channel_id=1, source_target_pairs={{0,5},{1,4},{2,7},{3,6},{4,1},{5,0},{6,3},{7,2},{8,13},{9,12},{10,... | collective-permute-start | bytes 110600 | tf_op jit(solution)/shard_map/ppermute | solution.py:299
  7.7 9.0 %collective-permute-start.5 = (bf16[8,2304]{1,0:T(8,128)(2,1)}, bf16[8,2304]{1,0:T(8,128)(2,1)S(1)}, u32[]{:S(2)}, u32[]{:S(2)}) collective-permute-start(bf16[8,2304]{1,0:T(8,128)(2,1)} %get-tuple-element.53), channel_id=1, source_target_pairs={{0,6},{1,7},{2,4},{3,5},{4,2},{5,3},{6,0},{7,1},{8,14},{9,15},{10,... | collective-permute-start | bytes 110600 | tf_op jit(solution)/shard_map/ppermute | solution.py:299
  10.4 14.8 %copy-start.1 = (s32[16,16]{1,0:T(8,128)S(1)}, s32[16,16]{1,0:T(8,128)}, u32[]{:S(2)}) copy-start(s32[16,16]{1,0:T(8,128)} %span.1) | copy-start | bytes 3076
  10.4 6.7 %collective-permute-start.6 = (bf16[8,2304]{1,0:T(8,128)(2,1)}, bf16[8,2304]{1,0:T(8,128)(2,1)S(1)}, u32[]{:S(2)}, u32[]{:S(2)}) collective-permute-start(bf16[8,2304]{1,0:T(8,128)(2,1)} %get-tuple-element.54), channel_id=1, source_target_pairs={{0,7},{1,6},{2,5},{3,4},{4,3},{5,2},{6,1},{7,0},{8,15},{9,14},{10,... | collective-permute-start | bytes 110600 | tf_op jit(solution)/shard_map/ppermute | solution.py:299
  10.5 9.8 %collective-permute-start.7 = (bf16[8,2304]{1,0:T(8,128)(2,1)}, bf16[8,2304]{1,0:T(8,128)(2,1)S(1)}, u32[]{:S(2)}, u32[]{:S(2)}) collective-permute-start(bf16[8,2304]{1,0:T(8,128)(2,1)} %get-tuple-element.55), channel_id=1, source_target_pairs={{0,8},{1,9},{2,10},{3,11},{4,12},{5,13},{6,14},{7,15},{8,0},{9,1},... | collective-permute-start | bytes 110600 | tf_op jit(solution)/shard_map/ppermute | solution.py:299
  13.1 7.7 %collective-permute-start.8 = (bf16[8,2304]{1,0:T(8,128)(2,1)}, bf16[8,2304]{1,0:T(8,128)(2,1)S(1)}, u32[]{:S(2)}, u32[]{:S(2)}) collective-permute-start(bf16[8,2304]{1,0:T(8,128)(2,1)} %get-tuple-element.56), channel_id=1, source_target_pairs={{0,9},{1,8},{2,11},{3,10},{4,13},{5,12},{6,15},{7,14},{8,1},{9,0},... | collective-permute-start | bytes 110600 | tf_op jit(solution)/shard_map/ppermute | solution.py:299
  13.8 11.1 %collective-permute-start.9 = (bf16[8,2304]{1,0:T(8,128)(2,1)}, bf16[8,2304]{1,0:T(8,128)(2,1)S(1)}, u32[]{:S(2)}, u32[]{:S(2)}) collective-permute-start(bf16[8,2304]{1,0:T(8,128)(2,1)} %get-tuple-element.57), channel_id=1, source_target_pairs={{0,10},{1,11},{2,8},{3,9},{4,14},{5,15},{6,12},{7,13},{8,2},{9,3},... | collective-permute-start | bytes 110600 | tf_op jit(solution)/shard_map/ppermute | solution.py:299
  16.7 10.9 %collective-permute-start.10 = (bf16[8,2304]{1,0:T(8,128)(2,1)}, bf16[8,2304]{1,0:T(8,128)(2,1)S(1)}, u32[]{:S(2)}, u32[]{:S(2)}) collective-permute-start(bf16[8,2304]{1,0:T(8,128)(2,1)} %get-tuple-element.58), channel_id=1, source_target_pairs={{0,11},{1,10},{2,9},{3,8},{4,15},{5,14},{6,13},{7,12},{8,3},{9,2},... | collective-permute-start | bytes 110600 | tf_op jit(solution)/shard_map/ppermute | solution.py:299
  17.0 10.5 %collective-permute-start.11 = (bf16[8,2304]{1,0:T(8,128)(2,1)}, bf16[8,2304]{1,0:T(8,128)(2,1)S(1)}, u32[]{:S(2)}, u32[]{:S(2)}) collective-permute-start(bf16[8,2304]{1,0:T(8,128)(2,1)} %get-tuple-element.59), channel_id=1, source_target_pairs={{0,12},{1,13},{2,14},{3,15},{4,8},{5,9},{6,10},{7,11},{8,4},{9,5},... | collective-permute-start | bytes 110600 | tf_op jit(solution)/shard_map/ppermute | solution.py:299
  20.4 7.2 %collective-permute-start.12 = (bf16[8,2304]{1,0:T(8,128)(2,1)}, bf16[8,2304]{1,0:T(8,128)(2,1)S(1)}, u32[]{:S(2)}, u32[]{:S(2)}) collective-permute-start(bf16[8,2304]{1,0:T(8,128)(2,1)} %get-tuple-element.60), channel_id=1, source_target_pairs={{0,13},{1,12},{2,15},{3,14},{4,9},{5,8},{6,11},{7,10},{8,5},{9,4},... | collective-permute-start | bytes 110600 | tf_op jit(solution)/shard_map/ppermute | solution.py:299
  20.9 4.3 %copy-start.2 = (s32[16,1]{0,1:T(1,128)S(1)}, s32[16,1]{0,1:T(1,128)}, u32[]{:S(2)}) copy-start(s32[16,1]{0,1:T(1,128)} %param.9) | copy-start | bytes 196
  20.9 4.3 %copy-start.4 = (s32[16]{0:T(128)S(1)}, s32[16]{0:T(128)}, u32[]{:S(2)}) copy-start(s32[16]{0:T(128)} %prefix_len.1) | copy-start | bytes 196
  20.9 7.1 %collective-permute-start.13 = (bf16[8,2304]{1,0:T(8,128)(2,1)}, bf16[8,2304]{1,0:T(8,128)(2,1)S(1)}, u32[]{:S(2)}, u32[]{:S(2)}) collective-permute-start(bf16[8,2304]{1,0:T(8,128)(2,1)} %get-tuple-element.61), channel_id=1, source_target_pairs={{0,14},{1,15},{2,12},{3,13},{4,10},{5,11},{6,8},{7,9},{8,6},{9,7},... | collective-permute-start | bytes 110600 | tf_op jit(solution)/shard_map/ppermute | solution.py:299
  24.8 6.4 %collective-permute-start.14 = (bf16[8,2304]{1,0:T(8,128)(2,1)}, bf16[8,2304]{1,0:T(8,128)(2,1)S(1)}, u32[]{:S(2)}, u32[]{:S(2)}) collective-permute-start(bf16[8,2304]{1,0:T(8,128)(2,1)} %get-tuple-element.62), channel_id=1, source_target_pairs={{0,15},{1,14},{2,13},{3,12},{4,11},{5,10},{6,9},{7,8},{8,7},{9,6},... | collective-permute-start | bytes 110600 | tf_op jit(solution)/shard_map/ppermute | solution.py:299
  25.2 1.0 %copy-start = (bf16[2048,128]{1,0:T(8,128)(2,1)S(1)}, bf16[2048,128]{1,0:T(8,128)(2,1)}, u32[]{:S(2)}) copy-start(bf16[2048,128]{1,0:T(8,128)(2,1)} %values.1) | copy-start | bytes 1572868
  26.2 5.1 %copy-start.5 = (bf16[2048,128]{1,0:T(8,128)(2,1)S(1)}, bf16[2048,128]{1,0:T(8,128)(2,1)}, u32[]{:S(2)}) copy-start(bf16[2048,128]{1,0:T(8,128)(2,1)} %keys.1) | copy-start | bytes 1572868
  31.3 0.8 %copy-start.6 = (bf16[8,2304]{1,0:T(8,128)(2,1)S(1)}, bf16[8,2304]{1,0:T(8,128)(2,1)}, u32[]{:S(2)}) copy-start(bf16[8,2304]{1,0:T(8,128)(2,1)} %get-tuple-element.47.refs_0_) | copy-start | bytes 110596
  34.7 5.7 %collective-permute-start.15 = (bf16[8,2048]{1,0:T(8,128)(2,1)S(1)}, bf16[8,2048]{1,0:T(8,128)(2,1)S(1)}, u32[]{:S(2)}, u32[]{:S(2)}) collective-permute-start(bf16[8,2048]{1,0:T(8,128)(2,1)S(1)} %get-tuple-element.64), channel_id=1, source_target_pairs={{0,1},{1,0},{2,3},{3,2},{4,5},{5,4},{6,7},{7,6},{8,9},{9,8},{10,11... | collective-permute-start | bytes 98312 | tf_op jit(solution)/shard_map/ppermute | solution.py:299
  36.9 4.2 %collective-permute-start.16 = (bf16[8,2048]{1,0:T(8,128)(2,1)S(1)}, bf16[8,2048]{1,0:T(8,128)(2,1)S(1)}, u32[]{:S(2)}, u32[]{:S(2)}) collective-permute-start(bf16[8,2048]{1,0:T(8,128)(2,1)S(1)} %get-tuple-element.65), channel_id=1, source_target_pairs={{0,2},{1,3},{2,0},{3,1},{4,6},{5,7},{6,4},{7,5},{8,10},{9,11},{10,... | collective-permute-start | bytes 98312 | tf_op jit(solution)/shard_map/ppermute | solution.py:299
  37.3 5.4 %collective-permute-start.17 = (bf16[8,2048]{1,0:T(8,128)(2,1)S(1)}, bf16[8,2048]{1,0:T(8,128)(2,1)S(1)}, u32[]{:S(2)}, u32[]{:S(2)}) collective-permute-start(bf16[8,2048]{1,0:T(8,128)(2,1)S(1)} %get-tuple-element.66), channel_id=1, source_target_pairs={{0,3},{1,2},{2,1},{3,0},{4,7},{5,6},{6,5},{7,4},{8,11},{9,10},{10,... | collective-permute-start | bytes 98312 | tf_op jit(solution)/shard_map/ppermute | solution.py:299
  38.3 4.4 %collective-permute-start.18 = (bf16[8,2048]{1,0:T(8,128)(2,1)S(1)}, bf16[8,2048]{1,0:T(8,128)(2,1)S(1)}, u32[]{:S(2)}, u32[]{:S(2)}) collective-permute-start(bf16[8,2048]{1,0:T(8,128)(2,1)S(1)} %get-tuple-element.67), channel_id=1, source_target_pairs={{0,4},{1,5},{2,6},{3,7},{4,0},{5,1},{6,2},{7,3},{8,12},{9,13},{10,... | collective-permute-start | bytes 98312 | tf_op jit(solution)/shard_map/ppermute | solution.py:299
  38.3 7.4 %collective-permute-start.19 = (bf16[8,2048]{1,0:T(8,128)(2,1)S(1)}, bf16[8,2048]{1,0:T(8,128)(2,1)S(1)}, u32[]{:S(2)}, u32[]{:S(2)}) collective-permute-start(bf16[8,2048]{1,0:T(8,128)(2,1)S(1)} %get-tuple-element.68), channel_id=1, source_target_pairs={{0,5},{1,4},{2,7},{3,6},{4,1},{5,0},{6,3},{7,2},{8,13},{9,12},{10,... | collective-permute-start | bytes 98312 | tf_op jit(solution)/shard_map/ppermute | solution.py:299
  40.4 5.6 %collective-permute-start.20 = (bf16[8,2048]{1,0:T(8,128)(2,1)S(1)}, bf16[8,2048]{1,0:T(8,128)(2,1)S(1)}, u32[]{:S(2)}, u32[]{:S(2)}) collective-permute-start(bf16[8,2048]{1,0:T(8,128)(2,1)S(1)} %get-tuple-element.69), channel_id=1, source_target_pairs={{0,6},{1,7},{2,4},{3,5},{4,2},{5,3},{6,0},{7,1},{8,14},{9,15},{10,... | collective-permute-start | bytes 98312 | tf_op jit(solution)/shard_map/ppermute | solution.py:299
  41.0 7.9 %collective-permute-start.21 = (bf16[8,2048]{1,0:T(8,128)(2,1)S(1)}, bf16[8,2048]{1,0:T(8,128)(2,1)S(1)}, u32[]{:S(2)}, u32[]{:S(2)}) collective-permute-start(bf16[8,2048]{1,0:T(8,128)(2,1)S(1)} %get-tuple-element.70), channel_id=1, source_target_pairs={{0,7},{1,6},{2,5},{3,4},{4,3},{5,2},{6,1},{7,0},{8,15},{9,14},{10,... | collective-permute-start | bytes 98312 | tf_op jit(solution)/shard_map/ppermute | solution.py:299
  42.7 6.4 %collective-permute-start.22 = (bf16[8,2048]{1,0:T(8,128)(2,1)S(1)}, bf16[8,2048]{1,0:T(8,128)(2,1)S(1)}, u32[]{:S(2)}, u32[]{:S(2)}) collective-permute-start(bf16[8,2048]{1,0:T(8,128)(2,1)S(1)} %get-tuple-element.71), channel_id=1, source_target_pairs={{0,8},{1,9},{2,10},{3,11},{4,12},{5,13},{6,14},{7,15},{8,0},{9,1},... | collective-permute-start | bytes 98312 | tf_op jit(solution)/shard_map/ppermute | solution.py:299
  42.7 10.1 %collective-permute-start.23 = (bf16[8,2048]{1,0:T(8,128)(2,1)S(1)}, bf16[8,2048]{1,0:T(8,128)(2,1)S(1)}, u32[]{:S(2)}, u32[]{:S(2)}) collective-permute-start(bf16[8,2048]{1,0:T(8,128)(2,1)S(1)} %get-tuple-element.72), channel_id=1, source_target_pairs={{0,9},{1,8},{2,11},{3,10},{4,13},{5,12},{6,15},{7,14},{8,1},{9,0},... | collective-permute-start | bytes 98312 | tf_op jit(solution)/shard_map/ppermute | solution.py:299
  45.7 8.1 %collective-permute-start.24 = (bf16[8,2048]{1,0:T(8,128)(2,1)S(1)}, bf16[8,2048]{1,0:T(8,128)(2,1)S(1)}, u32[]{:S(2)}, u32[]{:S(2)}) collective-permute-start(bf16[8,2048]{1,0:T(8,128)(2,1)S(1)} %get-tuple-element.73), channel_id=1, source_target_pairs={{0,10},{1,11},{2,8},{3,9},{4,14},{5,15},{6,12},{7,13},{8,2},{9,3},... | collective-permute-start | bytes 98312 | tf_op jit(solution)/shard_map/ppermute | solution.py:299
  46.0 10.9 %collective-permute-start.25 = (bf16[8,2048]{1,0:T(8,128)(2,1)S(1)}, bf16[8,2048]{1,0:T(8,128)(2,1)S(1)}, u32[]{:S(2)}, u32[]{:S(2)}) collective-permute-start(bf16[8,2048]{1,0:T(8,128)(2,1)S(1)} %get-tuple-element.74), channel_id=1, source_target_pairs={{0,11},{1,10},{2,9},{3,8},{4,15},{5,14},{6,13},{7,12},{8,3},{9,2},... | collective-permute-start | bytes 98312 | tf_op jit(solution)/shard_map/ppermute | solution.py:299
  48.9 8.0 %collective-permute-start.26 = (bf16[8,2048]{1,0:T(8,128)(2,1)S(1)}, bf16[8,2048]{1,0:T(8,128)(2,1)S(1)}, u32[]{:S(2)}, u32[]{:S(2)}) collective-permute-start(bf16[8,2048]{1,0:T(8,128)(2,1)S(1)} %get-tuple-element.75), channel_id=1, source_target_pairs={{0,12},{1,13},{2,14},{3,15},{4,8},{5,9},{6,10},{7,11},{8,4},{9,5},... | collective-permute-start | bytes 98312 | tf_op jit(solution)/shard_map/ppermute | solution.py:299
  49.1 7.8 %collective-permute-start.27 = (bf16[8,2048]{1,0:T(8,128)(2,1)S(1)}, bf16[8,2048]{1,0:T(8,128)(2,1)S(1)}, u32[]{:S(2)}, u32[]{:S(2)}) collective-permute-start(bf16[8,2048]{1,0:T(8,128)(2,1)S(1)} %get-tuple-element.76), channel_id=1, source_target_pairs={{0,13},{1,12},{2,15},{3,14},{4,9},{5,8},{6,11},{7,10},{8,5},{9,4},... | collective-permute-start | bytes 98312 | tf_op jit(solution)/shard_map/ppermute | solution.py:299
  52.8 6.6 %collective-permute-start.28 = (bf16[8,2048]{1,0:T(8,128)(2,1)S(1)}, bf16[8,2048]{1,0:T(8,128)(2,1)S(1)}, u32[]{:S(2)}, u32[]{:S(2)}) collective-permute-start(bf16[8,2048]{1,0:T(8,128)(2,1)S(1)} %get-tuple-element.77), channel_id=1, source_target_pairs={{0,14},{1,15},{2,12},{3,13},{4,10},{5,11},{6,8},{7,9},{8,6},{9,7},... | collective-permute-start | bytes 98312 | tf_op jit(solution)/shard_map/ppermute | solution.py:299
  53.8 6.0 %collective-permute-start.29 = (bf16[8,2048]{1,0:T(8,128)(2,1)S(1)}, bf16[8,2048]{1,0:T(8,128)(2,1)S(1)}, u32[]{:S(2)}, u32[]{:S(2)}) collective-permute-start(bf16[8,2048]{1,0:T(8,128)(2,1)S(1)} %get-tuple-element.78), channel_id=1, source_target_pairs={{0,15},{1,14},{2,13},{3,12},{4,11},{5,10},{6,9},{7,8},{8,7},{9,6},... | collective-permute-start | bytes 98312 | tf_op jit(solution)/shard_map/ppermute | solution.py:299
  59.8 0.7 %copy-start.3 = (s32[2,128]{1,0:T(2,128)S(1)}, s32[2,128]{1,0:T(2,128)}, u32[]{:S(2)}) copy-start(s32[2,128]{1,0:T(2,128)} %get-tuple-element.42.places) | copy-start | bytes 3076

commit v4 on v3

--- a/solution.py
+++ b/solution.py
@@ -287,6 +287,7 @@
     hit_count = hits.shape[1]
     rows = devices * MSG
     owners = hits.reshape(REQUESTS * hit_count)
+    fresh = (owners, queries, fresh_keys, fresh_values)
 
     def together(x):
         return lax.all_to_all(x, "cache", split_axis=0, concat_axis=0, tiled=True)
@@ -295,7 +296,7 @@
         if not pairwise(devices):
             return [together(x) for x in messages]
         moved = list(messages)
-        for m in reversed(range(1, devices)):
+        for m in sorted(range(1, devices), key=lambda m: (-m % (devices // 2), -m)):
             moved[m] = lax.ppermute(messages[m], "cache", [(d, d ^ m) for d in range(devices)])
         return moved
 
@@ -314,7 +315,6 @@
         [((rows // parts, CAP * (WIDE + HD)), jnp.bfloat16)] * parts
         + [((CAP * hit_count, 2 * ROWS), jnp.int32)],
         "pack",
-        grant=60,
         in_specs=smem(1) + hbm(3),
         out_specs=vmem(parts + 1),
         scratch_shapes=[
@@ -322,7 +322,7 @@
             pltpu.SMEM((devices,), jnp.int32),
             pltpu.SemaphoreType.DMA((4,)),
         ],
-    )(owners, queries, fresh_keys, fresh_values)
+    )(*(pltpu.with_memory_space_constraint(x, pltpu.HBM) for x in fresh))
     got = exchange(sends)
     busy, prompt_mask, cached_mask, wide = call(
         prep_kernel,

time: 61.6 us -> 58.7 us (0.953)
  starting transfers between devices: 44.1 us -> 42.1 us
  local copies, waits for them, and re-layouts: 2.49 us -> 1.05 us
  Pallas kernels: 7.76 us -> 8.97 us
    ppermute x30, starting transfers between devices: 44.1 us -> 42.1 us  [exchange(): lax.ppermute(messages[m], 'cache', [(d, d ^ m) for d in range(devices)])]
    pallas_call x1, Pallas kernels: 2.63 us -> 4.62 us  [body(): call(attend_kernel, [((rows // parts, CAP * WIDE), jnp.bfloat16)] * parts...]
    unnamed x14 -> x10, local copies, waits for them, and re-layouts: 2.49 us -> 1.05 us
    pallas_call x1, Pallas kernels: 2.75 us -> 1.97 us  [body(): call(pack_kernel, [((rows // parts, CAP * (WIDE + HD)), jnp.bfloat16)] *...]
  transfers between devices with their start and end apart: 30 -> 30, of which waited for: 5 -> 4; matrix products, arithmetic and copies ran while one was open for 0% -> 0% of each run, Pallas kernels for 2% -> 2%
where the time goes in v4:
time: 58.7 us
  starting transfers between devices  42.1 us (72%)
  Pallas kernels  8.97 us (15%)
  waiting for transfers between devices  6.43 us (11%)
  local copies, waits for them, and re-layouts  1.05 us (2%)
    ppermute x30, starting transfers between devices, exchange(): lax.ppermute(messages[m], 'cache', [(d, d ^ m) for d in range(devices)])  42.1 us
    ppermute x30, waiting for transfers between devices, exchange(): lax.ppermute(messages[m], 'cache', [(d, d ^ m) for d in range(devices)])  6.43 us
    pallas_call x1, Pallas kernels, body(): call(attend_kernel, [((rows // parts, CAP * WIDE), jnp.bfloat16)] * parts...  4.62 us
    pallas_call x1, Pallas kernels, body(): call(pack_kernel, [((rows // parts, CAP * (WIDE + HD)), jnp.bfloat16)] *...  1.97 us
    pallas_call x1, Pallas kernels, body(): call(prep_kernel, [((CAP,), jnp.int32), ((CAP * rows, rows), jnp.float32)...  1.35 us
  transfers between devices with their start and end apart: 30, of which 4 were waited for; matrix products, arithmetic and copies ran while one was open for 0% of the time, Pallas kernels for 2%

profile of v4, /device:TPU:0, one launch (start us, length us, event | category | flops | bytes accessed | tf_op | source)
XLA Modules:
  0.0 58.7 jit_solution(9659657683719083013)
XLA Ops:
  0.0 2.0 %pack.1 = (bf16[8,2304]{1,0:T(8,128)(2,1)S(1)}, bf16[8,2304]{1,0:T(8,128)(2,1)S(1)}, bf16[8,2304]{1,0:T(8,128)(2,1)S(1)}, bf16[8,2304]{1,0:T(8,128)(2,1)S(1)}, b...) custom-call(s32[16]{0:T(128)} %bitcast.1, ...), custom_call_target="tpu_custom_call" | custom-call | tf_op jit(solution)/shard_map/pack/pallas_call | solution.py:313
  2.0 0.5 collective-permute-start
  2.5 2.6 %collective-permute-start.1 = (bf16[8,2304]{1,0:T(8,128)(2,1)S(1)}, bf16[8,2304]{1,0:T(8,128)(2,1)S(1)}, u32[]{:S(2)}, u32[]{:S(2)}) collective-permute-start(bf16[8,2304]{1,0:T(8,128)(2,1)S(1)} %get-tuple-element.49), channel_id=1, source_target_pairs={{0,2},{1,3},{2,0},{3,1},{4,6},{5,7},{6,4},{7,5},{8,10},{9,11},{10,... | collective-permute-start | bytes 110600 | tf_op jit(solution)/shard_map/ppermute | solution.py:300
  5.1 0.1 collective-permute-start.2
  5.2 1.8 %collective-permute-start.3 = (bf16[8,2304]{1,0:T(8,128)(2,1)S(1)}, bf16[8,2304]{1,0:T(8,128)(2,1)S(1)}, u32[]{:S(2)}, u32[]{:S(2)}) collective-permute-start(bf16[8,2304]{1,0:T(8,128)(2,1)S(1)} %get-tuple-element.51), channel_id=1, source_target_pairs={{0,4},{1,5},{2,6},{3,7},{4,0},{5,1},{6,2},{7,3},{8,12},{9,13},{10,... | collective-permute-start | bytes 110600 | tf_op jit(solution)/shard_map/ppermute | solution.py:300
  7.0 0.0 collective-permute-start.4
  7.0 0.0 collective-permute-done.refs_1_
  7.0 2.6 %collective-permute-start.5 = (bf16[8,2304]{1,0:T(8,128)(2,1)S(1)}, bf16[8,2304]{1,0:T(8,128)(2,1)S(1)}, u32[]{:S(2)}, u32[]{:S(2)}) collective-permute-start(bf16[8,2304]{1,0:T(8,128)(2,1)S(1)} %get-tuple-element.53), channel_id=1, source_target_pairs={{0,6},{1,7},{2,4},{3,5},{4,2},{5,3},{6,0},{7,1},{8,14},{9,15},{10,... | collective-permute-start | bytes 110600 | tf_op jit(solution)/shard_map/ppermute | solution.py:300
  9.6 0.0 collective-permute-done.1.refs_2_
  9.6 0.1 collective-permute-start.6
  9.7 0.0 collective-permute-done.2.refs_3_
  9.7 2.6 %collective-permute-start.7 = (bf16[8,2304]{1,0:T(8,128)(2,1)S(1)}, bf16[8,2304]{1,0:T(8,128)(2,1)S(1)}, u32[]{:S(2)}, u32[]{:S(2)}) collective-permute-start(bf16[8,2304]{1,0:T(8,128)(2,1)S(1)} %get-tuple-element.55), channel_id=1, source_target_pairs={{0,8},{1,9},{2,10},{3,11},{4,12},{5,13},{6,14},{7,15},{8,0},{9,1},... | collective-permute-start | bytes 110600 | tf_op jit(solution)/shard_map/ppermute | solution.py:300
  12.4 0.0 collective-permute-done.3.refs_4_
  12.4 0.4 collective-permute-start.8
  12.8 0.0 collective-permute-done.4.refs_5_
  12.8 3.1 %collective-permute-start.9 = (bf16[8,2304]{1,0:T(8,128)(2,1)S(1)}, bf16[8,2304]{1,0:T(8,128)(2,1)S(1)}, u32[]{:S(2)}, u32[]{:S(2)}) collective-permute-start(bf16[8,2304]{1,0:T(8,128)(2,1)S(1)} %get-tuple-element.57), channel_id=1, source_target_pairs={{0,10},{1,11},{2,8},{3,9},{4,14},{5,15},{6,12},{7,13},{8,2},{9,3},... | collective-permute-start | bytes 110600 | tf_op jit(solution)/shard_map/ppermute | solution.py:300
  15.9 0.0 collective-permute-done.5.refs_6_
  15.9 0.1 collective-permute-start.10
  16.1 0.0 collective-permute-done.6.refs_7_
  16.1 3.5 %collective-permute-start.11 = (bf16[8,2304]{1,0:T(8,128)(2,1)S(1)}, bf16[8,2304]{1,0:T(8,128)(2,1)S(1)}, u32[]{:S(2)}, u32[]{:S(2)}) collective-permute-start(bf16[8,2304]{1,0:T(8,128)(2,1)S(1)} %get-tuple-element.59), channel_id=1, source_target_pairs={{0,12},{1,13},{2,14},{3,15},{4,8},{5,9},{6,10},{7,11},{8,4},{9,5},... | collective-permute-start | bytes 110600 | tf_op jit(solution)/shard_map/ppermute | solution.py:300
  19.6 0.0 collective-permute-done.7.refs_8_
  19.6 0.3 collective-permute-start.12
  19.9 0.0 collective-permute-done.8.refs_9_
  19.9 4.2 %collective-permute-start.13 = (bf16[8,2304]{1,0:T(8,128)(2,1)S(1)}, bf16[8,2304]{1,0:T(8,128)(2,1)S(1)}, u32[]{:S(2)}, u32[]{:S(2)}) collective-permute-start(bf16[8,2304]{1,0:T(8,128)(2,1)S(1)} %get-tuple-element.61), channel_id=1, source_target_pairs={{0,14},{1,15},{2,12},{3,13},{4,10},{5,11},{6,8},{7,9},{8,6},{9,7},... | collective-permute-start | bytes 110600 | tf_op jit(solution)/shard_map/ppermute | solution.py:300
  24.0 0.0 collective-permute-done.9.refs_10_
  24.0 0.1 collective-permute-start.14
  24.2 1.0 %copy-done = bf16[2048,128]{1,0:T(8,128)(2,1)S(1)} copy-done((bf16[2048,128]{1,0:T(8,128)(2,1)S(1)}, bf16[2048,128]{1,0:T(8,128)(2,1)}, u32[]{:S(2)}) %copy-start) | copy-done | bytes 524312
  25.2 1.3 %prep.1 = (s32[2]{0:T(128)S(1)}, f32[256,128]{1,0:T(8,128)S(1)}, f32[2,1024]{1,0:T(2,128)S(1)}, bf16[2048,256]{1,0:T(8,128)(2,1)S(1)}) custom-call(s32[16]{0:T(128)S(1)} %bitcast.2, s32[16]{0:T(128)S(1)} %copy-done.3, s32[16,16]{1,0:T(8,128)S(1)} %copy-done.1, bf16[2048,128]{1,0:T(8,128)(2,1)S(1)} %copy-done), custom_call_target="tpu_custom_call" | custom-call | flops 1000000 | bytes 4194304 | tf_op jit(solution)/shard_map/prep/pallas_call | solution.py:327
  26.6 0.0 collective-permute-done.10.refs_11_
  26.6 0.0 collective-permute-done.11.refs_12_
  26.6 0.0 collective-permute-done.12.refs_13_
  26.6 0.4 collective-permute-done.13.refs_14_
  27.0 3.2 %collective-permute-done.14.refs_15_ = bf16[8,2304]{1,0:T(8,128)(2,1)S(1)} collective-permute-done((bf16[8,2304]{1,0:T(8,128)(2,1)S(1)}, bf16[8,2304]{1,0:T(8,128)(2,1)S(1)}, u32[]{:S(2)}, u32[]{:S(2)}) %collective-permute-start.14) | collective-permute-done | bytes 36896 | tf_op jit(solution)/shard_map/ppermute | solution.py:300
  30.2 4.6 %attend.1 = (bf16[8,2048]{1,0:T(8,128)(2,1)S(1)}, bf16[8,2048]{1,0:T(8,128)(2,1)S(1)}, bf16[8,2048]{1,0:T(8,128)(2,1)S(1)}, bf16[8,2048]{1,0:T(8,128)(2,1)S(1)},...) custom-call(s32[2]{0:T(128)S(1)} %get-tuple-element.43.busy, ...), custom_call_target="tpu_custom_call" | custom-call | flops 1207959552 | bytes 1048576 | tf_op jit(solution)/shard_map/attend/pallas_call | solution.py:341
  34.8 0.1 collective-permute-start.15
  34.9 0.1 collective-permute-start.16
  35.0 1.8 %collective-permute-start.17 = (bf16[8,2048]{1,0:T(8,128)(2,1)S(1)}, bf16[8,2048]{1,0:T(8,128)(2,1)S(1)}, u32[]{:S(2)}, u32[]{:S(2)}) collective-permute-start(bf16[8,2048]{1,0:T(8,128)(2,1)S(1)} %get-tuple-element.66), channel_id=1, source_target_pairs={{0,3},{1,2},{2,1},{3,0},{4,7},{5,6},{6,5},{7,4},{8,11},{9,10},{10,... | collective-permute-start | bytes 98312 | tf_op jit(solution)/shard_map/ppermute | solution.py:300
  36.7 0.0 collective-permute-start.18
  36.7 1.7 %collective-permute-start.19 = (bf16[8,2048]{1,0:T(8,128)(2,1)S(1)}, bf16[8,2048]{1,0:T(8,128)(2,1)S(1)}, u32[]{:S(2)}, u32[]{:S(2)}) collective-permute-start(bf16[8,2048]{1,0:T(8,128)(2,1)S(1)} %get-tuple-element.68), channel_id=1, source_target_pairs={{0,5},{1,4},{2,7},{3,6},{4,1},{5,0},{6,3},{7,2},{8,13},{9,12},{10,... | collective-permute-start | bytes 98312 | tf_op jit(solution)/shard_map/ppermute | solution.py:300
  38.4 0.0 collective-permute-done.15.refs_1_
  38.4 0.1 collective-permute-start.20
  38.5 0.5 collective-permute-done.16.refs_2_
  39.0 2.1 %collective-permute-start.21 = (bf16[8,2048]{1,0:T(8,128)(2,1)S(1)}, bf16[8,2048]{1,0:T(8,128)(2,1)S(1)}, u32[]{:S(2)}, u32[]{:S(2)}) collective-permute-start(bf16[8,2048]{1,0:T(8,128)(2,1)S(1)} %get-tuple-element.70), channel_id=1, source_target_pairs={{0,7},{1,6},{2,5},{3,4},{4,3},{5,2},{6,1},{7,0},{8,15},{9,14},{10,... | collective-permute-start | bytes 98312 | tf_op jit(solution)/shard_map/ppermute | solution.py:300
  41.2 0.0 collective-permute-done.17.refs_3_
  41.2 0.0 collective-permute-start.22
  41.2 0.0 collective-permute-done.18.refs_4_
  41.2 2.6 %collective-permute-start.23 = (bf16[8,2048]{1,0:T(8,128)(2,1)S(1)}, bf16[8,2048]{1,0:T(8,128)(2,1)S(1)}, u32[]{:S(2)}, u32[]{:S(2)}) collective-permute-start(bf16[8,2048]{1,0:T(8,128)(2,1)S(1)} %get-tuple-element.72), channel_id=1, source_target_pairs={{0,9},{1,8},{2,11},{3,10},{4,13},{5,12},{6,15},{7,14},{8,1},{9,0},... | collective-permute-start | bytes 98312 | tf_op jit(solution)/shard_map/ppermute | solution.py:300
  43.7 0.0 collective-permute-done.19.refs_5_
  43.8 0.1 collective-permute-start.24
  43.9 0.0 collective-permute-done.20.refs_6_
  43.9 3.5 %collective-permute-start.25 = (bf16[8,2048]{1,0:T(8,128)(2,1)S(1)}, bf16[8,2048]{1,0:T(8,128)(2,1)S(1)}, u32[]{:S(2)}, u32[]{:S(2)}) collective-permute-start(bf16[8,2048]{1,0:T(8,128)(2,1)S(1)} %get-tuple-element.74), channel_id=1, source_target_pairs={{0,11},{1,10},{2,9},{3,8},{4,15},{5,14},{6,13},{7,12},{8,3},{9,2},... | collective-permute-start | bytes 98312 | tf_op jit(solution)/shard_map/ppermute | solution.py:300
  47.4 0.0 collective-permute-done.21.refs_7_
  47.4 0.6 %collective-permute-start.26 = (bf16[8,2048]{1,0:T(8,128)(2,1)S(1)}, bf16[8,2048]{1,0:T(8,128)(2,1)S(1)}, u32[]{:S(2)}, u32[]{:S(2)}) collective-permute-start(bf16[8,2048]{1,0:T(8,128)(2,1)S(1)} %get-tuple-element.75), channel_id=1, source_target_pairs={{0,12},{1,13},{2,14},{3,15},{4,8},{5,9},{6,10},{7,11},{8,4},{9,5},... | collective-permute-start | bytes 98312 | tf_op jit(solution)/shard_map/ppermute | solution.py:300
  48.0 0.0 collective-permute-done.22.refs_8_
  48.0 2.9 %collective-permute-start.27 = (bf16[8,2048]{1,0:T(8,128)(2,1)S(1)}, bf16[8,2048]{1,0:T(8,128)(2,1)S(1)}, u32[]{:S(2)}, u32[]{:S(2)}) collective-permute-start(bf16[8,2048]{1,0:T(8,128)(2,1)S(1)} %get-tuple-element.76), channel_id=1, source_target_pairs={{0,13},{1,12},{2,15},{3,14},{4,9},{5,8},{6,11},{7,10},{8,5},{9,4},... | collective-permute-start | bytes 98312 | tf_op jit(solution)/shard_map/ppermute | solution.py:300
  50.9 0.0 collective-permute-done.23.refs_9_
  50.9 0.4 collective-permute-start.28
  51.2 0.0 collective-permute-done.24.refs_10_
  51.2 4.1 %collective-permute-start.29 = (bf16[8,2048]{1,0:T(8,128)(2,1)S(1)}, bf16[8,2048]{1,0:T(8,128)(2,1)S(1)}, u32[]{:S(2)}, u32[]{:S(2)}) collective-permute-start(bf16[8,2048]{1,0:T(8,128)(2,1)S(1)} %get-tuple-element.78), channel_id=1, source_target_pairs={{0,15},{1,14},{2,13},{3,12},{4,11},{5,10},{6,9},{7,8},{8,7},{9,6},... | collective-permute-start | bytes 98312 | tf_op jit(solution)/shard_map/ppermute | solution.py:300
  55.4 0.0 collective-permute-done.25.refs_11_
  55.4 0.0 collective-permute-done.26.refs_12_
  55.4 0.0 collective-permute-done.27.refs_13_
  55.4 2.3 %collective-permute-done.28.refs_14_ = bf16[8,2048]{1,0:T(8,128)(2,1)S(1)} collective-permute-done((bf16[8,2048]{1,0:T(8,128)(2,1)S(1)}, bf16[8,2048]{1,0:T(8,128)(2,1)S(1)}, u32[]{:S(2)}, u32[]{:S(2)}) %collective-permute-start.28) | collective-permute-done | bytes 32800 | tf_op jit(solution)/shard_map/ppermute | solution.py:300
  57.7 1.0 %unpack.1 = bf16[64,2048]{1,0:T(8,128)(2,1)} custom-call(s32[2,128]{1,0:T(2,128)S(1)} %get-tuple-element.42.places, bf16[8,2048]{1,0:T(8,128)(2,1)S(1)} %get-tuple-element.63.refs_0_, bf16[8,2048]{1,0:T(8,128)(2,1)S(1)} %collective-permute-done.15.refs_1_, bf16[8,2048]{1,0:T(8,128)(2,1)S(1)} %collective-permute-done.16.refs_2_, ...), custom_call_target="tpu_custom_call" | custom-call | tf_op jit(solution)/shard_map/unpack/pallas_call | solution.py:361
  (10 shorter events, 0.0 us)
Async XLA Ops:
  2.0 5.0 %collective-permute-start = (bf16[8,2304]{1,0:T(8,128)(2,1)S(1)}, bf16[8,2304]{1,0:T(8,128)(2,1)S(1)}, u32[]{:S(2)}, u32[]{:S(2)}) collective-permute-start(bf16[8,2304]{1,0:T(8,128)(2,1)S(1)} %get-tuple-element.48), channel_id=1, source_target_pairs={{0,1},{1,0},{2,3},{3,2},{4,5},{5,4},{6,7},{7,6},{8,9},{9,8},{10,11... | collective-permute-start | bytes 110600 | tf_op jit(solution)/shard_map/ppermute | solution.py:300
  2.5 7.1 %collective-permute-start.1 = (bf16[8,2304]{1,0:T(8,128)(2,1)S(1)}, bf16[8,2304]{1,0:T(8,128)(2,1)S(1)}, u32[]{:S(2)}, u32[]{:S(2)}) collective-permute-start(bf16[8,2304]{1,0:T(8,128)(2,1)S(1)} %get-tuple-element.49), channel_id=1, source_target_pairs={{0,2},{1,3},{2,0},{3,1},{4,6},{5,7},{6,4},{7,5},{8,10},{9,11},{10,... | collective-permute-start | bytes 110600 | tf_op jit(solution)/shard_map/ppermute | solution.py:300
  5.1 4.7 %collective-permute-start.2 = (bf16[8,2304]{1,0:T(8,128)(2,1)S(1)}, bf16[8,2304]{1,0:T(8,128)(2,1)S(1)}, u32[]{:S(2)}, u32[]{:S(2)}) collective-permute-start(bf16[8,2304]{1,0:T(8,128)(2,1)S(1)} %get-tuple-element.50), channel_id=1, source_target_pairs={{0,3},{1,2},{2,1},{3,0},{4,7},{5,6},{6,5},{7,4},{8,11},{9,10},{10,... | collective-permute-start | bytes 110600 | tf_op jit(solution)/shard_map/ppermute | solution.py:300
  5.2 7.2 %collective-permute-start.3 = (bf16[8,2304]{1,0:T(8,128)(2,1)S(1)}, bf16[8,2304]{1,0:T(8,128)(2,1)S(1)}, u32[]{:S(2)}, u32[]{:S(2)}) collective-permute-start(bf16[8,2304]{1,0:T(8,128)(2,1)S(1)} %get-tuple-element.51), channel_id=1, source_target_pairs={{0,4},{1,5},{2,6},{3,7},{4,0},{5,1},{6,2},{7,3},{8,12},{9,13},{10,... | collective-permute-start | bytes 110600 | tf_op jit(solution)/shard_map/ppermute | solution.py:300
  7.0 5.8 %collective-permute-start.4 = (bf16[8,2304]{1,0:T(8,128)(2,1)S(1)}, bf16[8,2304]{1,0:T(8,128)(2,1)S(1)}, u32[]{:S(2)}, u32[]{:S(2)}) collective-permute-start(bf16[8,2304]{1,0:T(8,128)(2,1)S(1)} %get-tuple-element.52), channel_id=1, source_target_pairs={{0,5},{1,4},{2,7},{3,6},{4,1},{5,0},{6,3},{7,2},{8,13},{9,12},{10,... | collective-permute-start | bytes 110600 | tf_op jit(solution)/shard_map/ppermute | solution.py:300
  7.0 9.0 %collective-permute-start.5 = (bf16[8,2304]{1,0:T(8,128)(2,1)S(1)}, bf16[8,2304]{1,0:T(8,128)(2,1)S(1)}, u32[]{:S(2)}, u32[]{:S(2)}) collective-permute-start(bf16[8,2304]{1,0:T(8,128)(2,1)S(1)} %get-tuple-element.53), channel_id=1, source_target_pairs={{0,6},{1,7},{2,4},{3,5},{4,2},{5,3},{6,0},{7,1},{8,14},{9,15},{10,... | collective-permute-start | bytes 110600 | tf_op jit(solution)/shard_map/ppermute | solution.py:300
  9.6 14.6 %copy-start.1 = (s32[16,16]{1,0:T(8,128)S(1)}, s32[16,16]{1,0:T(8,128)}, u32[]{:S(2)}) copy-start(s32[16,16]{1,0:T(8,128)} %span.1) | copy-start | bytes 3076
  9.6 6.5 %collective-permute-start.6 = (bf16[8,2304]{1,0:T(8,128)(2,1)S(1)}, bf16[8,2304]{1,0:T(8,128)(2,1)S(1)}, u32[]{:S(2)}, u32[]{:S(2)}) collective-permute-start(bf16[8,2304]{1,0:T(8,128)(2,1)S(1)} %get-tuple-element.54), channel_id=1, source_target_pairs={{0,7},{1,6},{2,5},{3,4},{4,3},{5,2},{6,1},{7,0},{8,15},{9,14},{10,... | collective-permute-start | bytes 110600 | tf_op jit(solution)/shard_map/ppermute | solution.py:300
  9.7 9.8 %collective-permute-start.7 = (bf16[8,2304]{1,0:T(8,128)(2,1)S(1)}, bf16[8,2304]{1,0:T(8,128)(2,1)S(1)}, u32[]{:S(2)}, u32[]{:S(2)}) collective-permute-start(bf16[8,2304]{1,0:T(8,128)(2,1)S(1)} %get-tuple-element.55), channel_id=1, source_target_pairs={{0,8},{1,9},{2,10},{3,11},{4,12},{5,13},{6,14},{7,15},{8,0},{9,1},... | collective-permute-start | bytes 110600 | tf_op jit(solution)/shard_map/ppermute | solution.py:300
  12.4 7.5 %collective-permute-start.8 = (bf16[8,2304]{1,0:T(8,128)(2,1)S(1)}, bf16[8,2304]{1,0:T(8,128)(2,1)S(1)}, u32[]{:S(2)}, u32[]{:S(2)}) collective-permute-start(bf16[8,2304]{1,0:T(8,128)(2,1)S(1)} %get-tuple-element.56), channel_id=1, source_target_pairs={{0,9},{1,8},{2,11},{3,10},{4,13},{5,12},{6,15},{7,14},{8,1},{9,0},... | collective-permute-start | bytes 110600 | tf_op jit(solution)/shard_map/ppermute | solution.py:300
  12.8 11.3 %collective-permute-start.9 = (bf16[8,2304]{1,0:T(8,128)(2,1)S(1)}, bf16[8,2304]{1,0:T(8,128)(2,1)S(1)}, u32[]{:S(2)}, u32[]{:S(2)}) collective-permute-start(bf16[8,2304]{1,0:T(8,128)(2,1)S(1)} %get-tuple-element.57), channel_id=1, source_target_pairs={{0,10},{1,11},{2,8},{3,9},{4,14},{5,15},{6,12},{7,13},{8,2},{9,3},... | collective-permute-start | bytes 110600 | tf_op jit(solution)/shard_map/ppermute | solution.py:300
  15.9 10.7 %collective-permute-start.10 = (bf16[8,2304]{1,0:T(8,128)(2,1)S(1)}, bf16[8,2304]{1,0:T(8,128)(2,1)S(1)}, u32[]{:S(2)}, u32[]{:S(2)}) collective-permute-start(bf16[8,2304]{1,0:T(8,128)(2,1)S(1)} %get-tuple-element.58), channel_id=1, source_target_pairs={{0,11},{1,10},{2,9},{3,8},{4,15},{5,14},{6,13},{7,12},{8,3},{9,2},... | collective-permute-start | bytes 110600 | tf_op jit(solution)/shard_map/ppermute | solution.py:300
  16.1 10.5 %collective-permute-start.11 = (bf16[8,2304]{1,0:T(8,128)(2,1)S(1)}, bf16[8,2304]{1,0:T(8,128)(2,1)S(1)}, u32[]{:S(2)}, u32[]{:S(2)}) collective-permute-start(bf16[8,2304]{1,0:T(8,128)(2,1)S(1)} %get-tuple-element.59), channel_id=1, source_target_pairs={{0,12},{1,13},{2,14},{3,15},{4,8},{5,9},{6,10},{7,11},{8,4},{9,5},... | collective-permute-start | bytes 110600 | tf_op jit(solution)/shard_map/ppermute | solution.py:300
  19.6 7.0 %collective-permute-start.12 = (bf16[8,2304]{1,0:T(8,128)(2,1)S(1)}, bf16[8,2304]{1,0:T(8,128)(2,1)S(1)}, u32[]{:S(2)}, u32[]{:S(2)}) collective-permute-start(bf16[8,2304]{1,0:T(8,128)(2,1)S(1)} %get-tuple-element.60), channel_id=1, source_target_pairs={{0,13},{1,12},{2,15},{3,14},{4,9},{5,8},{6,11},{7,10},{8,5},{9,4},... | collective-permute-start | bytes 110600 | tf_op jit(solution)/shard_map/ppermute | solution.py:300
  19.9 4.3 %copy-start.2 = (s32[16,1]{0,1:T(1,128)S(1)}, s32[16,1]{0,1:T(1,128)}, u32[]{:S(2)}) copy-start(s32[16,1]{0,1:T(1,128)} %param.9) | copy-start | bytes 196
  19.9 4.3 %copy-start.3 = (s32[16]{0:T(128)S(1)}, s32[16]{0:T(128)}, u32[]{:S(2)}) copy-start(s32[16]{0:T(128)} %prefix_len.1) | copy-start | bytes 196
  19.9 7.1 %collective-permute-start.13 = (bf16[8,2304]{1,0:T(8,128)(2,1)S(1)}, bf16[8,2304]{1,0:T(8,128)(2,1)S(1)}, u32[]{:S(2)}, u32[]{:S(2)}) collective-permute-start(bf16[8,2304]{1,0:T(8,128)(2,1)S(1)} %get-tuple-element.61), channel_id=1, source_target_pairs={{0,14},{1,15},{2,12},{3,13},{4,10},{5,11},{6,8},{7,9},{8,6},{9,7},... | collective-permute-start | bytes 110600 | tf_op jit(solution)/shard_map/ppermute | solution.py:300
  24.0 6.1 %collective-permute-start.14 = (bf16[8,2304]{1,0:T(8,128)(2,1)S(1)}, bf16[8,2304]{1,0:T(8,128)(2,1)S(1)}, u32[]{:S(2)}, u32[]{:S(2)}) collective-permute-start(bf16[8,2304]{1,0:T(8,128)(2,1)S(1)} %get-tuple-element.62), channel_id=1, source_target_pairs={{0,15},{1,14},{2,13},{3,12},{4,11},{5,10},{6,9},{7,8},{8,7},{9,6},... | collective-permute-start | bytes 110600 | tf_op jit(solution)/shard_map/ppermute | solution.py:300
  24.2 1.0 %copy-start = (bf16[2048,128]{1,0:T(8,128)(2,1)S(1)}, bf16[2048,128]{1,0:T(8,128)(2,1)}, u32[]{:S(2)}) copy-start(bf16[2048,128]{1,0:T(8,128)(2,1)} %values.1) | copy-start | bytes 1572868
  25.2 5.0 %copy-start.4 = (bf16[2048,128]{1,0:T(8,128)(2,1)S(1)}, bf16[2048,128]{1,0:T(8,128)(2,1)}, u32[]{:S(2)}) copy-start(bf16[2048,128]{1,0:T(8,128)(2,1)} %keys.1) | copy-start | bytes 1572868
  34.8 3.6 %collective-permute-start.15 = (bf16[8,2048]{1,0:T(8,128)(2,1)S(1)}, bf16[8,2048]{1,0:T(8,128)(2,1)S(1)}, u32[]{:S(2)}, u32[]{:S(2)}) collective-permute-start(bf16[8,2048]{1,0:T(8,128)(2,1)S(1)} %get-tuple-element.64), channel_id=1, source_target_pairs={{0,1},{1,0},{2,3},{3,2},{4,5},{5,4},{6,7},{7,6},{8,9},{9,8},{10,11... | collective-permute-start | bytes 98312 | tf_op jit(solution)/shard_map/ppermute | solution.py:300
  34.9 4.2 %collective-permute-start.16 = (bf16[8,2048]{1,0:T(8,128)(2,1)S(1)}, bf16[8,2048]{1,0:T(8,128)(2,1)S(1)}, u32[]{:S(2)}, u32[]{:S(2)}) collective-permute-start(bf16[8,2048]{1,0:T(8,128)(2,1)S(1)} %get-tuple-element.65), channel_id=1, source_target_pairs={{0,2},{1,3},{2,0},{3,1},{4,6},{5,7},{6,4},{7,5},{8,10},{9,11},{10,... | collective-permute-start | bytes 98312 | tf_op jit(solution)/shard_map/ppermute | solution.py:300
  35.0 6.2 %collective-permute-start.17 = (bf16[8,2048]{1,0:T(8,128)(2,1)S(1)}, bf16[8,2048]{1,0:T(8,128)(2,1)S(1)}, u32[]{:S(2)}, u32[]{:S(2)}) collective-permute-start(bf16[8,2048]{1,0:T(8,128)(2,1)S(1)} %get-tuple-element.66), channel_id=1, source_target_pairs={{0,3},{1,2},{2,1},{3,0},{4,7},{5,6},{6,5},{7,4},{8,11},{9,10},{10,... | collective-permute-start | bytes 98312 | tf_op jit(solution)/shard_map/ppermute | solution.py:300
  36.7 4.4 %collective-permute-start.18 = (bf16[8,2048]{1,0:T(8,128)(2,1)S(1)}, bf16[8,2048]{1,0:T(8,128)(2,1)S(1)}, u32[]{:S(2)}, u32[]{:S(2)}) collective-permute-start(bf16[8,2048]{1,0:T(8,128)(2,1)S(1)} %get-tuple-element.67), channel_id=1, source_target_pairs={{0,4},{1,5},{2,6},{3,7},{4,0},{5,1},{6,2},{7,3},{8,12},{9,13},{10,... | collective-permute-start | bytes 98312 | tf_op jit(solution)/shard_map/ppermute | solution.py:300
  36.7 7.0 %collective-permute-start.19 = (bf16[8,2048]{1,0:T(8,128)(2,1)S(1)}, bf16[8,2048]{1,0:T(8,128)(2,1)S(1)}, u32[]{:S(2)}, u32[]{:S(2)}) collective-permute-start(bf16[8,2048]{1,0:T(8,128)(2,1)S(1)} %get-tuple-element.68), channel_id=1, source_target_pairs={{0,5},{1,4},{2,7},{3,6},{4,1},{5,0},{6,3},{7,2},{8,13},{9,12},{10,... | collective-permute-start | bytes 98312 | tf_op jit(solution)/shard_map/ppermute | solution.py:300
  38.4 5.4 %collective-permute-start.20 = (bf16[8,2048]{1,0:T(8,128)(2,1)S(1)}, bf16[8,2048]{1,0:T(8,128)(2,1)S(1)}, u32[]{:S(2)}, u32[]{:S(2)}) collective-permute-start(bf16[8,2048]{1,0:T(8,128)(2,1)S(1)} %get-tuple-element.69), channel_id=1, source_target_pairs={{0,6},{1,7},{2,4},{3,5},{4,2},{5,3},{6,0},{7,1},{8,14},{9,15},{10,... | collective-permute-start | bytes 98312 | tf_op jit(solution)/shard_map/ppermute | solution.py:300
  39.0 8.3 %collective-permute-start.21 = (bf16[8,2048]{1,0:T(8,128)(2,1)S(1)}, bf16[8,2048]{1,0:T(8,128)(2,1)S(1)}, u32[]{:S(2)}, u32[]{:S(2)}) collective-permute-start(bf16[8,2048]{1,0:T(8,128)(2,1)S(1)} %get-tuple-element.70), channel_id=1, source_target_pairs={{0,7},{1,6},{2,5},{3,4},{4,3},{5,2},{6,1},{7,0},{8,15},{9,14},{10,... | collective-permute-start | bytes 98312 | tf_op jit(solution)/shard_map/ppermute | solution.py:300
  41.2 6.8 %collective-permute-start.22 = (bf16[8,2048]{1,0:T(8,128)(2,1)S(1)}, bf16[8,2048]{1,0:T(8,128)(2,1)S(1)}, u32[]{:S(2)}, u32[]{:S(2)}) collective-permute-start(bf16[8,2048]{1,0:T(8,128)(2,1)S(1)} %get-tuple-element.71), channel_id=1, source_target_pairs={{0,8},{1,9},{2,10},{3,11},{4,12},{5,13},{6,14},{7,15},{8,0},{9,1},... | collective-permute-start | bytes 98312 | tf_op jit(solution)/shard_map/ppermute | solution.py:300
  41.2 9.7 %collective-permute-start.23 = (bf16[8,2048]{1,0:T(8,128)(2,1)S(1)}, bf16[8,2048]{1,0:T(8,128)(2,1)S(1)}, u32[]{:S(2)}, u32[]{:S(2)}) collective-permute-start(bf16[8,2048]{1,0:T(8,128)(2,1)S(1)} %get-tuple-element.72), channel_id=1, source_target_pairs={{0,9},{1,8},{2,11},{3,10},{4,13},{5,12},{6,15},{7,14},{8,1},{9,0},... | collective-permute-start | bytes 98312 | tf_op jit(solution)/shard_map/ppermute | solution.py:300
  43.8 7.5 %collective-permute-start.24 = (bf16[8,2048]{1,0:T(8,128)(2,1)S(1)}, bf16[8,2048]{1,0:T(8,128)(2,1)S(1)}, u32[]{:S(2)}, u32[]{:S(2)}) collective-permute-start(bf16[8,2048]{1,0:T(8,128)(2,1)S(1)} %get-tuple-element.73), channel_id=1, source_target_pairs={{0,10},{1,11},{2,8},{3,9},{4,14},{5,15},{6,12},{7,13},{8,2},{9,3},... | collective-permute-start | bytes 98312 | tf_op jit(solution)/shard_map/ppermute | solution.py:300
  43.9 11.5 %collective-permute-start.25 = (bf16[8,2048]{1,0:T(8,128)(2,1)S(1)}, bf16[8,2048]{1,0:T(8,128)(2,1)S(1)}, u32[]{:S(2)}, u32[]{:S(2)}) collective-permute-start(bf16[8,2048]{1,0:T(8,128)(2,1)S(1)} %get-tuple-element.74), channel_id=1, source_target_pairs={{0,11},{1,10},{2,9},{3,8},{4,15},{5,14},{6,13},{7,12},{8,3},{9,2},... | collective-permute-start | bytes 98312 | tf_op jit(solution)/shard_map/ppermute | solution.py:300
  47.4 8.0 %collective-permute-start.26 = (bf16[8,2048]{1,0:T(8,128)(2,1)S(1)}, bf16[8,2048]{1,0:T(8,128)(2,1)S(1)}, u32[]{:S(2)}, u32[]{:S(2)}) collective-permute-start(bf16[8,2048]{1,0:T(8,128)(2,1)S(1)} %get-tuple-element.75), channel_id=1, source_target_pairs={{0,12},{1,13},{2,14},{3,15},{4,8},{5,9},{6,10},{7,11},{8,4},{9,5},... | collective-permute-start | bytes 98312 | tf_op jit(solution)/shard_map/ppermute | solution.py:300
  48.0 7.4 %collective-permute-start.27 = (bf16[8,2048]{1,0:T(8,128)(2,1)S(1)}, bf16[8,2048]{1,0:T(8,128)(2,1)S(1)}, u32[]{:S(2)}, u32[]{:S(2)}) collective-permute-start(bf16[8,2048]{1,0:T(8,128)(2,1)S(1)} %get-tuple-element.76), channel_id=1, source_target_pairs={{0,13},{1,12},{2,15},{3,14},{4,9},{5,8},{6,11},{7,10},{8,5},{9,4},... | collective-permute-start | bytes 98312 | tf_op jit(solution)/shard_map/ppermute | solution.py:300
  50.9 6.8 %collective-permute-start.28 = (bf16[8,2048]{1,0:T(8,128)(2,1)S(1)}, bf16[8,2048]{1,0:T(8,128)(2,1)S(1)}, u32[]{:S(2)}, u32[]{:S(2)}) collective-permute-start(bf16[8,2048]{1,0:T(8,128)(2,1)S(1)} %get-tuple-element.77), channel_id=1, source_target_pairs={{0,14},{1,15},{2,12},{3,13},{4,10},{5,11},{6,8},{7,9},{8,6},{9,7},... | collective-permute-start | bytes 98312 | tf_op jit(solution)/shard_map/ppermute | solution.py:300
  51.2 6.4 %collective-permute-start.29 = (bf16[8,2048]{1,0:T(8,128)(2,1)S(1)}, bf16[8,2048]{1,0:T(8,128)(2,1)S(1)}, u32[]{:S(2)}, u32[]{:S(2)}) collective-permute-start(bf16[8,2048]{1,0:T(8,128)(2,1)S(1)} %get-tuple-element.78), channel_id=1, source_target_pairs={{0,15},{1,14},{2,13},{3,12},{4,11},{5,10},{6,9},{7,8},{8,7},{9,6},... | collective-permute-start | bytes 98312 | tf_op jit(solution)/shard_map/ppermute | solution.py:300

commit v5 on v4

--- a/solution.py
+++ b/solution.py
@@ -40,8 +40,20 @@
     return devices <= 16
 
 
-def partner(devices, me, order):
-    return order ^ me if pairwise(devices) else order
+def step(devices):
+    return devices // 2 - 1
+
+
+def message_for(devices, me, device):
+    if not pairwise(devices):
+        return device
+    return (step(devices) * (device - me + devices)) % devices
+
+
+def source_of(devices, me, message):
+    if not pairwise(devices):
+        return message
+    return (me + step(devices) * (devices - message)) % devices
 
 
 def pack_kernel(devices, hit_count, hits, q, k, v, *refs):
@@ -71,7 +83,7 @@
             owner = hits[r * hit_count + i]
             rank = count[owner]
             count[owner] = rank + 1
-            message = partner(devices, me, owner) * MSG
+            message = message_for(devices, me, owner) * MSG
             for s in range(CAP):
                 place = jnp.where(rank == s, message, -4 * MSG)
                 rows[s][i] = jnp.where(lane_request == r, place, rows[s][i])
@@ -116,8 +128,8 @@
         limit = prefix_len[request] - which * REGION
         cached[slot : slot + 1, :] = jnp.where(iota((1, REGION), 1) < limit, 0.0, FLOOR)
         span_row = span[pl.ds(request, 1), :].astype(jnp.float32)
-        source = partner(devices, me, iota((devices, total_rows), 0))
-        spread = (iota((devices, total_rows), 1) // MSG == source).astype(jnp.bfloat16)
+        source = source_of(devices, me, iota((devices, total_rows), 1) // MSG)
+        spread = (iota((devices, total_rows), 0) == source).astype(jnp.bfloat16)
         spans = jnp.broadcast_to(span_row, (16, devices)).astype(jnp.bfloat16)
         key_span = dot(spans, spread, NN)[:1]
         lane = iota((1, total_rows), 1)
@@ -129,7 +141,7 @@
         block = 16 * MSG
 
         def one_block(at):
-            row_source = partner(devices, me, at * 16 + iota((block, devices), 0) // MSG)
+            row_source = source_of(devices, me, at * 16 + iota((block, devices), 0) // MSG)
             mine = iota((block, devices), 1) == row_source
             row_span = jnp.sum(jnp.where(mine, span_row, 0.0), axis=1, keepdims=True)
             row_spot = row_span.astype(jnp.int32) * TOK_REQ + iota((block, 1), 0) % TOK_REQ
@@ -292,12 +304,14 @@
     def together(x):
         return lax.all_to_all(x, "cache", split_axis=0, concat_axis=0, tiled=True)
 
-    def exchange(messages):
+    def exchange(messages, sign):
         if not pairwise(devices):
             return [together(x) for x in messages]
         moved = list(messages)
-        for m in sorted(range(1, devices), key=lambda m: (-m % (devices // 2), -m)):
-            moved[m] = lax.ppermute(messages[m], "cache", [(d, d ^ m) for d in range(devices)])
+        for m in range(1, devices):
+            far = sign * m * step(devices)
+            pairs = [(d, (d + far) % devices) for d in range(devices)]
+            moved[m] = lax.ppermute(messages[m], "cache", pairs)
         return moved
 
     def call(kernel, out_shape, name, grant=40, **kw):
@@ -323,7 +337,7 @@
             pltpu.SemaphoreType.DMA((4,)),
         ],
     )(*(pltpu.with_memory_space_constraint(x, pltpu.HBM) for x in fresh))
-    got = exchange(sends)
+    got = exchange(sends, 1)
     busy, prompt_mask, cached_mask, wide = call(
         prep_kernel,
         [
@@ -350,11 +364,11 @@
             flops=4 * pairs * HD, bytes_accessed=8 * rows * WIDE, transcendentals=pairs
         ),
     )(busy, prompt_mask, cached_mask, cache_keys, wide, *got)
-    returned = exchange(answers[:parts])
+    returned = exchange(answers[:parts], -1)
     for level in answers[parts:]:
         if pairwise(devices):
             blocks = level.reshape(devices, MSG, CAP * HD)
-            level = jnp.concatenate(exchange([blocks[m] for m in range(devices)]), axis=0)
+            level = jnp.concatenate(exchange([blocks[m] for m in range(devices)], -1), axis=0)
         else:
             level = together(level)
         returned.append(level)

time: 58.7 us -> 61.8 us (1.053)
  starting transfers between devices: 42.1 us -> 45.1 us
  waiting for transfers between devices: 6.43 us -> 8.45 us
  Pallas kernels: 8.97 us -> 6.98 us
    ppermute x30, starting transfers between devices: 42.1 us -> 45.1 us  [exchange(): moved[m] = lax.ppermute(messages[m], 'cache', pairs)]
    ppermute x30, waiting for transfers between devices: 6.43 us -> 8.45 us  [exchange(): moved[m] = lax.ppermute(messages[m], 'cache', pairs)]
    pallas_call x1, Pallas kernels: 4.62 us -> 2.63 us  [body(): call(attend_kernel, [((rows // parts, CAP * WIDE), jnp.bfloat16)] * parts...]
  transfers between devices with their start and end apart: 30 -> 30, of which waited for: 4 -> 8; matrix products, arithmetic and copies ran while one was open for 0% -> 0% of each run, Pallas kernels for 2% -> 2%
where the time goes in v5:
time: 61.8 us
  starting transfers between devices  45.1 us (73%)
  waiting for transfers between devices  8.45 us (14%)
  Pallas kernels  6.98 us (11%)
  local copies, waits for them, and re-layouts  1.05 us (2%)
    ppermute x30, starting transfers between devices, exchange(): moved[m] = lax.ppermute(messages[m], 'cache', pairs)  45.1 us
    ppermute x30, waiting for transfers between devices, exchange(): moved[m] = lax.ppermute(messages[m], 'cache', pairs)  8.45 us
    pallas_call x1, Pallas kernels, body(): call(attend_kernel, [((rows // parts, CAP * WIDE), jnp.bfloat16)] * parts...  2.63 us
    pallas_call x1, Pallas kernels, body(): call(pack_kernel, [((rows // parts, CAP * (WIDE + HD)), jnp.bfloat16)] *...  1.97 us
    pallas_call x1, Pallas kernels, body(): call(prep_kernel, [((CAP,), jnp.int32), ((CAP * rows, rows), jnp.float32)...  1.35 us
  transfers between devices with their start and end apart: 30, of which 8 were waited for; matrix products, arithmetic and copies ran while one was open for 0% of the time, Pallas kernels for 2%

profile of v5, /device:TPU:0, one launch (start us, length us, event | category | flops | bytes accessed | tf_op | source)
XLA Modules:
  0.0 61.8 jit_solution(16375141219649168992)
XLA Ops:
  0.0 2.0 %pack.1 = (bf16[8,2304]{1,0:T(8,128)(2,1)S(1)}, bf16[8,2304]{1,0:T(8,128)(2,1)S(1)}, bf16[8,2304]{1,0:T(8,128)(2,1)S(1)}, bf16[8,2304]{1,0:T(8,128)(2,1)S(1)}, b...) custom-call(s32[16]{0:T(128)} %bitcast.1, ...), custom_call_target="tpu_custom_call" | custom-call | tf_op jit(solution)/shard_map/pack/pallas_call | solution.py:327
  2.0 3.5 %collective-permute-start = (bf16[8,2304]{1,0:T(8,128)(2,1)S(1)}, bf16[8,2304]{1,0:T(8,128)(2,1)S(1)}, u32[]{:S(2)}, u32[]{:S(2)}) collective-permute-start(bf16[8,2304]{1,0:T(8,128)(2,1)S(1)} %get-tuple-element.48), channel_id=1, source_target_pairs={{0,7},{1,8},{2,9},{3,10},{4,11},{5,12},{6,13},{7,14},{8,15},{9,0},... | collective-permute-start | bytes 110600 | tf_op jit(solution)/shard_map/ppermute | solution.py:314
  5.5 2.7 %collective-permute-start.1 = (bf16[8,2304]{1,0:T(8,128)(2,1)S(1)}, bf16[8,2304]{1,0:T(8,128)(2,1)S(1)}, u32[]{:S(2)}, u32[]{:S(2)}) collective-permute-start(bf16[8,2304]{1,0:T(8,128)(2,1)S(1)} %get-tuple-element.49), channel_id=1, source_target_pairs={{0,14},{1,15},{2,0},{3,1},{4,2},{5,3},{6,4},{7,5},{8,6},{9,7},{10,... | collective-permute-start | bytes 110600 | tf_op jit(solution)/shard_map/ppermute | solution.py:314
  8.1 0.4 collective-permute-start.2
  8.5 3.1 %collective-permute-start.3 = (bf16[8,2304]{1,0:T(8,128)(2,1)S(1)}, bf16[8,2304]{1,0:T(8,128)(2,1)S(1)}, u32[]{:S(2)}, u32[]{:S(2)}) collective-permute-start(bf16[8,2304]{1,0:T(8,128)(2,1)S(1)} %get-tuple-element.51), channel_id=1, source_target_pairs={{0,12},{1,13},{2,14},{3,15},{4,0},{5,1},{6,2},{7,3},{8,4},{9,5},{1... | collective-permute-start | bytes 110600 | tf_op jit(solution)/shard_map/ppermute | solution.py:314
  11.6 0.1 collective-permute-start.4
  11.7 0.0 collective-permute-done.refs_1_
  11.7 0.5 collective-permute-start.5
  12.2 0.0 collective-permute-done.1.refs_2_
  12.2 0.0 collective-permute-start.6
  12.2 1.4 %collective-permute-done.2.refs_3_ = bf16[8,2304]{1,0:T(8,128)(2,1)S(1)} collective-permute-done((bf16[8,2304]{1,0:T(8,128)(2,1)S(1)}, bf16[8,2304]{1,0:T(8,128)(2,1)S(1)}, u32[]{:S(2)}, u32[]{:S(2)}) %collective-permute-start.2) | collective-permute-done | bytes 36896 | tf_op jit(solution)/shard_map/ppermute | solution.py:314
  13.6 1.0 %collective-permute-start.7 = (bf16[8,2304]{1,0:T(8,128)(2,1)S(1)}, bf16[8,2304]{1,0:T(8,128)(2,1)S(1)}, u32[]{:S(2)}, u32[]{:S(2)}) collective-permute-start(bf16[8,2304]{1,0:T(8,128)(2,1)S(1)} %get-tuple-element.55), channel_id=1, source_target_pairs={{0,8},{1,9},{2,10},{3,11},{4,12},{5,13},{6,14},{7,15},{8,0},{9,1},... | collective-permute-start | bytes 110600 | tf_op jit(solution)/shard_map/ppermute | solution.py:314
  14.6 0.0 collective-permute-done.3.refs_4_
  14.6 2.4 %collective-permute-start.8 = (bf16[8,2304]{1,0:T(8,128)(2,1)S(1)}, bf16[8,2304]{1,0:T(8,128)(2,1)S(1)}, u32[]{:S(2)}, u32[]{:S(2)}) collective-permute-start(bf16[8,2304]{1,0:T(8,128)(2,1)S(1)} %get-tuple-element.56), channel_id=1, source_target_pairs={{0,15},{1,0},{2,1},{3,2},{4,3},{5,4},{6,5},{7,6},{8,7},{9,8},{10,9... | collective-permute-start | bytes 110600 | tf_op jit(solution)/shard_map/ppermute | solution.py:314
  17.1 0.1 collective-permute-done.4.refs_5_
  17.1 0.0 collective-permute-start.9
  17.1 0.0 collective-permute-done.5.refs_6_
  17.1 3.7 %collective-permute-start.10 = (bf16[8,2304]{1,0:T(8,128)(2,1)S(1)}, bf16[8,2304]{1,0:T(8,128)(2,1)S(1)}, u32[]{:S(2)}, u32[]{:S(2)}) collective-permute-start(bf16[8,2304]{1,0:T(8,128)(2,1)S(1)} %get-tuple-element.58), channel_id=1, source_target_pairs={{0,13},{1,14},{2,15},{3,0},{4,1},{5,2},{6,3},{7,4},{8,5},{9,6},{10... | collective-permute-start | bytes 110600 | tf_op jit(solution)/shard_map/ppermute | solution.py:314
  20.8 0.0 collective-permute-done.6.refs_7_
  20.8 0.0 collective-permute-start.11
  20.8 0.0 collective-permute-done.7.refs_8_
  20.8 1.0 %collective-permute-start.12 = (bf16[8,2304]{1,0:T(8,128)(2,1)S(1)}, bf16[8,2304]{1,0:T(8,128)(2,1)S(1)}, u32[]{:S(2)}, u32[]{:S(2)}) collective-permute-start(bf16[8,2304]{1,0:T(8,128)(2,1)S(1)} %get-tuple-element.60), channel_id=1, source_target_pairs={{0,11},{1,12},{2,13},{3,14},{4,15},{5,0},{6,1},{7,2},{8,3},{9,4},{... | collective-permute-start | bytes 110600 | tf_op jit(solution)/shard_map/ppermute | solution.py:314
  21.8 0.0 collective-permute-done.8.refs_9_
  21.8 4.7 %collective-permute-start.13 = (bf16[8,2304]{1,0:T(8,128)(2,1)S(1)}, bf16[8,2304]{1,0:T(8,128)(2,1)S(1)}, u32[]{:S(2)}, u32[]{:S(2)}) collective-permute-start(bf16[8,2304]{1,0:T(8,128)(2,1)S(1)} %get-tuple-element.61), channel_id=1, source_target_pairs={{0,2},{1,3},{2,4},{3,5},{4,6},{5,7},{6,8},{7,9},{8,10},{9,11},{10,... | collective-permute-start | bytes 110600 | tf_op jit(solution)/shard_map/ppermute | solution.py:314
  26.5 0.0 collective-permute-done.9.refs_10_
  26.5 0.0 collective-permute-start.14
  26.5 0.0 copy-start
  26.5 1.0 %copy-done = bf16[2048,128]{1,0:T(8,128)(2,1)S(1)} copy-done((bf16[2048,128]{1,0:T(8,128)(2,1)S(1)}, bf16[2048,128]{1,0:T(8,128)(2,1)}, u32[]{:S(2)}) %copy-start) | copy-done | bytes 524312
  27.5 1.3 %prep.1 = (s32[2]{0:T(128)S(1)}, f32[256,128]{1,0:T(8,128)S(1)}, f32[2,1024]{1,0:T(2,128)S(1)}, bf16[2048,256]{1,0:T(8,128)(2,1)S(1)}) custom-call(s32[16]{0:T(128)S(1)} %bitcast.2, s32[16]{0:T(128)S(1)} %copy-done.3, s32[16,16]{1,0:T(8,128)S(1)} %copy-done.1, bf16[2048,128]{1,0:T(8,128)(2,1)S(1)} %copy-done), custom_call_target="tpu_custom_call" | custom-call | flops 1000000 | bytes 4194304 | tf_op jit(solution)/shard_map/prep/pallas_call | solution.py:341
  28.9 0.0 collective-permute-done.10.refs_11_
  28.9 0.0 collective-permute-done.11.refs_12_
  28.9 0.0 collective-permute-done.12.refs_13_
  28.9 0.0 collective-permute-done.13.refs_14_
  28.9 1.9 %collective-permute-done.14.refs_15_ = bf16[8,2304]{1,0:T(8,128)(2,1)S(1)} collective-permute-done((bf16[8,2304]{1,0:T(8,128)(2,1)S(1)}, bf16[8,2304]{1,0:T(8,128)(2,1)S(1)}, u32[]{:S(2)}, u32[]{:S(2)}) %collective-permute-start.14) | collective-permute-done | bytes 36896 | tf_op jit(solution)/shard_map/ppermute | solution.py:314
  30.8 2.6 %attend.1 = (bf16[8,2048]{1,0:T(8,128)(2,1)S(1)}, bf16[8,2048]{1,0:T(8,128)(2,1)S(1)}, bf16[8,2048]{1,0:T(8,128)(2,1)S(1)}, bf16[8,2048]{1,0:T(8,128)(2,1)S(1)},...) custom-call(s32[2]{0:T(128)S(1)} %get-tuple-element.43.busy, ...), custom_call_target="tpu_custom_call" | custom-call | flops 1207959552 | bytes 1048576 | tf_op jit(solution)/shard_map/attend/pallas_call | solution.py:355
  33.5 0.4 collective-permute-start.15
  33.8 2.6 %collective-permute-start.16 = (bf16[8,2048]{1,0:T(8,128)(2,1)S(1)}, bf16[8,2048]{1,0:T(8,128)(2,1)S(1)}, u32[]{:S(2)}, u32[]{:S(2)}) collective-permute-start(bf16[8,2048]{1,0:T(8,128)(2,1)S(1)} %get-tuple-element.65), channel_id=1, source_target_pairs={{0,2},{1,3},{2,4},{3,5},{4,6},{5,7},{6,8},{7,9},{8,10},{9,11},{10,... | collective-permute-start | bytes 98312 | tf_op jit(solution)/shard_map/ppermute | solution.py:314
  36.5 3.4 %collective-permute-start.17 = (bf16[8,2048]{1,0:T(8,128)(2,1)S(1)}, bf16[8,2048]{1,0:T(8,128)(2,1)S(1)}, u32[]{:S(2)}, u32[]{:S(2)}) collective-permute-start(bf16[8,2048]{1,0:T(8,128)(2,1)S(1)} %get-tuple-element.66), channel_id=1, source_target_pairs={{0,11},{1,12},{2,13},{3,14},{4,15},{5,0},{6,1},{7,2},{8,3},{9,4},{... | collective-permute-start | bytes 98312 | tf_op jit(solution)/shard_map/ppermute | solution.py:314
  39.8 0.0 collective-permute-start.18
  39.8 1.9 %collective-permute-start.19 = (bf16[8,2048]{1,0:T(8,128)(2,1)S(1)}, bf16[8,2048]{1,0:T(8,128)(2,1)S(1)}, u32[]{:S(2)}, u32[]{:S(2)}) collective-permute-start(bf16[8,2048]{1,0:T(8,128)(2,1)S(1)} %get-tuple-element.68), channel_id=1, source_target_pairs={{0,13},{1,14},{2,15},{3,0},{4,1},{5,2},{6,3},{7,4},{8,5},{9,6},{10... | collective-permute-start | bytes 98312 | tf_op jit(solution)/shard_map/ppermute | solution.py:314
  41.7 0.0 collective-permute-done.15.refs_1_
  41.7 0.1 collective-permute-start.20
  41.8 0.0 collective-permute-done.16.refs_2_
  41.8 4.0 %collective-permute-start.21 = (bf16[8,2048]{1,0:T(8,128)(2,1)S(1)}, bf16[8,2048]{1,0:T(8,128)(2,1)S(1)}, u32[]{:S(2)}, u32[]{:S(2)}) collective-permute-start(bf16[8,2048]{1,0:T(8,128)(2,1)S(1)} %get-tuple-element.70), channel_id=1, source_target_pairs={{0,15},{1,0},{2,1},{3,2},{4,3},{5,4},{6,5},{7,6},{8,7},{9,8},{10,9... | collective-permute-start | bytes 98312 | tf_op jit(solution)/shard_map/ppermute | solution.py:314
  45.8 0.0 collective-permute-done.17.refs_3_
  45.8 0.0 collective-permute-start.22
  45.8 0.0 collective-permute-done.18.refs_4_
  45.8 0.1 collective-permute-start.23
  45.9 0.0 collective-permute-done.19.refs_5_
  45.9 1.7 %collective-permute-start.24 = (bf16[8,2048]{1,0:T(8,128)(2,1)S(1)}, bf16[8,2048]{1,0:T(8,128)(2,1)S(1)}, u32[]{:S(2)}, u32[]{:S(2)}) collective-permute-start(bf16[8,2048]{1,0:T(8,128)(2,1)S(1)} %get-tuple-element.73), channel_id=1, source_target_pairs={{0,10},{1,11},{2,12},{3,13},{4,14},{5,15},{6,0},{7,1},{8,2},{9,3},... | collective-permute-start | bytes 98312 | tf_op jit(solution)/shard_map/ppermute | solution.py:314
  47.6 0.1 collective-permute-done.20.refs_6_
  47.8 2.2 %collective-permute-start.25 = (bf16[8,2048]{1,0:T(8,128)(2,1)S(1)}, bf16[8,2048]{1,0:T(8,128)(2,1)S(1)}, u32[]{:S(2)}, u32[]{:S(2)}) collective-permute-start(bf16[8,2048]{1,0:T(8,128)(2,1)S(1)} %get-tuple-element.74), channel_id=1, source_target_pairs={{0,3},{1,4},{2,5},{3,6},{4,7},{5,8},{6,9},{7,10},{8,11},{9,12},{10... | collective-permute-start | bytes 98312 | tf_op jit(solution)/shard_map/ppermute | solution.py:314
  49.9 0.0 collective-permute-done.21.refs_7_
  49.9 1.0 %collective-permute-start.26 = (bf16[8,2048]{1,0:T(8,128)(2,1)S(1)}, bf16[8,2048]{1,0:T(8,128)(2,1)S(1)}, u32[]{:S(2)}, u32[]{:S(2)}) collective-permute-start(bf16[8,2048]{1,0:T(8,128)(2,1)S(1)} %get-tuple-element.75), channel_id=1, source_target_pairs={{0,12},{1,13},{2,14},{3,15},{4,0},{5,1},{6,2},{7,3},{8,4},{9,5},{1... | collective-permute-start | bytes 98312 | tf_op jit(solution)/shard_map/ppermute | solution.py:314
  51.0 0.1 collective-permute-done.22.refs_8_
  51.1 0.4 collective-permute-start.27
  51.5 0.4 collective-permute-done.23.refs_9_
  51.9 4.3 %collective-permute-start.28 = (bf16[8,2048]{1,0:T(8,128)(2,1)S(1)}, bf16[8,2048]{1,0:T(8,128)(2,1)S(1)}, u32[]{:S(2)}, u32[]{:S(2)}) collective-permute-start(bf16[8,2048]{1,0:T(8,128)(2,1)S(1)} %get-tuple-element.77), channel_id=1, source_target_pairs={{0,14},{1,15},{2,0},{3,1},{4,2},{5,3},{6,4},{7,5},{8,6},{9,7},{10,... | collective-permute-start | bytes 98312 | tf_op jit(solution)/shard_map/ppermute | solution.py:314
  56.3 0.0 collective-permute-done.24.refs_10_
  56.3 0.1 collective-permute-start.29
  56.4 0.0 collective-permute-done.27.refs_13_
  56.4 1.5 %collective-permute-done.28.refs_14_ = bf16[8,2048]{1,0:T(8,128)(2,1)S(1)} collective-permute-done((bf16[8,2048]{1,0:T(8,128)(2,1)S(1)}, bf16[8,2048]{1,0:T(8,128)(2,1)S(1)}, u32[]{:S(2)}, u32[]{:S(2)}) %collective-permute-start.28) | collective-permute-done | bytes 32800 | tf_op jit(solution)/shard_map/ppermute | solution.py:314
  57.9 2.9 %collective-permute-done.29.refs_15_ = bf16[8,2048]{1,0:T(8,128)(2,1)S(1)} collective-permute-done((bf16[8,2048]{1,0:T(8,128)(2,1)S(1)}, bf16[8,2048]{1,0:T(8,128)(2,1)S(1)}, u32[]{:S(2)}, u32[]{:S(2)}) %collective-permute-start.29) | collective-permute-done | bytes 32800 | tf_op jit(solution)/shard_map/ppermute | solution.py:314
  60.7 1.0 %unpack.1 = bf16[64,2048]{1,0:T(8,128)(2,1)} custom-call(s32[2,128]{1,0:T(2,128)S(1)} %get-tuple-element.42.places, bf16[8,2048]{1,0:T(8,128)(2,1)S(1)} %get-tuple-element.63.refs_0_, bf16[8,2048]{1,0:T(8,128)(2,1)S(1)} %collective-permute-done.15.refs_1_, bf16[8,2048]{1,0:T(8,128)(2,1)S(1)} %collective-permute-done.16.refs_2_, ...), custom_call_target="tpu_custom_call" | custom-call | tf_op jit(solution)/shard_map/unpack/pallas_call | solution.py:375
  (10 shorter events, 0.0 us)
Async XLA Ops:
  2.0 9.7 %collective-permute-start = (bf16[8,2304]{1,0:T(8,128)(2,1)S(1)}, bf16[8,2304]{1,0:T(8,128)(2,1)S(1)}, u32[]{:S(2)}, u32[]{:S(2)}) collective-permute-start(bf16[8,2304]{1,0:T(8,128)(2,1)S(1)} %get-tuple-element.48), channel_id=1, source_target_pairs={{0,7},{1,8},{2,9},{3,10},{4,11},{5,12},{6,13},{7,14},{8,15},{9,0},... | collective-permute-start | bytes 110600 | tf_op jit(solution)/shard_map/ppermute | solution.py:314
  5.5 6.7 %collective-permute-start.1 = (bf16[8,2304]{1,0:T(8,128)(2,1)S(1)}, bf16[8,2304]{1,0:T(8,128)(2,1)S(1)}, u32[]{:S(2)}, u32[]{:S(2)}) collective-permute-start(bf16[8,2304]{1,0:T(8,128)(2,1)S(1)} %get-tuple-element.49), channel_id=1, source_target_pairs={{0,14},{1,15},{2,0},{3,1},{4,2},{5,3},{6,4},{7,5},{8,6},{9,7},{10,... | collective-permute-start | bytes 110600 | tf_op jit(solution)/shard_map/ppermute | solution.py:314
  8.1 5.5 %collective-permute-start.2 = (bf16[8,2304]{1,0:T(8,128)(2,1)S(1)}, bf16[8,2304]{1,0:T(8,128)(2,1)S(1)}, u32[]{:S(2)}, u32[]{:S(2)}) collective-permute-start(bf16[8,2304]{1,0:T(8,128)(2,1)S(1)} %get-tuple-element.50), channel_id=1, source_target_pairs={{0,5},{1,6},{2,7},{3,8},{4,9},{5,10},{6,11},{7,12},{8,13},{9,14},{... | collective-permute-start | bytes 110600 | tf_op jit(solution)/shard_map/ppermute | solution.py:314
  8.5 6.1 %collective-permute-start.3 = (bf16[8,2304]{1,0:T(8,128)(2,1)S(1)}, bf16[8,2304]{1,0:T(8,128)(2,1)S(1)}, u32[]{:S(2)}, u32[]{:S(2)}) collective-permute-start(bf16[8,2304]{1,0:T(8,128)(2,1)S(1)} %get-tuple-element.51), channel_id=1, source_target_pairs={{0,12},{1,13},{2,14},{3,15},{4,0},{5,1},{6,2},{7,3},{8,4},{9,5},{1... | collective-permute-start | bytes 110600 | tf_op jit(solution)/shard_map/ppermute | solution.py:314
  11.6 5.5 %collective-permute-start.4 = (bf16[8,2304]{1,0:T(8,128)(2,1)S(1)}, bf16[8,2304]{1,0:T(8,128)(2,1)S(1)}, u32[]{:S(2)}, u32[]{:S(2)}) collective-permute-start(bf16[8,2304]{1,0:T(8,128)(2,1)S(1)} %get-tuple-element.52), channel_id=1, source_target_pairs={{0,3},{1,4},{2,5},{3,6},{4,7},{5,8},{6,9},{7,10},{8,11},{9,12},{10... | collective-permute-start | bytes 110600 | tf_op jit(solution)/shard_map/ppermute | solution.py:314
  11.7 5.4 %collective-permute-start.5 = (bf16[8,2304]{1,0:T(8,128)(2,1)S(1)}, bf16[8,2304]{1,0:T(8,128)(2,1)S(1)}, u32[]{:S(2)}, u32[]{:S(2)}) collective-permute-start(bf16[8,2304]{1,0:T(8,128)(2,1)S(1)} %get-tuple-element.53), channel_id=1, source_target_pairs={{0,10},{1,11},{2,12},{3,13},{4,14},{5,15},{6,0},{7,1},{8,2},{9,3},... | collective-permute-start | bytes 110600 | tf_op jit(solution)/shard_map/ppermute | solution.py:314
  12.2 14.3 %copy-start.1 = (s32[16,16]{1,0:T(8,128)S(1)}, s32[16,16]{1,0:T(8,128)}, u32[]{:S(2)}) copy-start(s32[16,16]{1,0:T(8,128)} %span.1) | copy-start | bytes 3076
  12.2 8.6 %collective-permute-start.6 = (bf16[8,2304]{1,0:T(8,128)(2,1)S(1)}, bf16[8,2304]{1,0:T(8,128)(2,1)S(1)}, u32[]{:S(2)}, u32[]{:S(2)}) collective-permute-start(bf16[8,2304]{1,0:T(8,128)(2,1)S(1)} %get-tuple-element.54), channel_id=1, source_target_pairs={{0,1},{1,2},{2,3},{3,4},{4,5},{5,6},{6,7},{7,8},{8,9},{9,10},{10,1... | collective-permute-start | bytes 110600 | tf_op jit(solution)/shard_map/ppermute | solution.py:314
  13.6 7.2 %collective-permute-start.7 = (bf16[8,2304]{1,0:T(8,128)(2,1)S(1)}, bf16[8,2304]{1,0:T(8,128)(2,1)S(1)}, u32[]{:S(2)}, u32[]{:S(2)}) collective-permute-start(bf16[8,2304]{1,0:T(8,128)(2,1)S(1)} %get-tuple-element.55), channel_id=1, source_target_pairs={{0,8},{1,9},{2,10},{3,11},{4,12},{5,13},{6,14},{7,15},{8,0},{9,1},... | collective-permute-start | bytes 110600 | tf_op jit(solution)/shard_map/ppermute | solution.py:314
  14.6 7.1 %collective-permute-start.8 = (bf16[8,2304]{1,0:T(8,128)(2,1)S(1)}, bf16[8,2304]{1,0:T(8,128)(2,1)S(1)}, u32[]{:S(2)}, u32[]{:S(2)}) collective-permute-start(bf16[8,2304]{1,0:T(8,128)(2,1)S(1)} %get-tuple-element.56), channel_id=1, source_target_pairs={{0,15},{1,0},{2,1},{3,2},{4,3},{5,4},{6,5},{7,6},{8,7},{9,8},{10,9... | collective-permute-start | bytes 110600 | tf_op jit(solution)/shard_map/ppermute | solution.py:314
  17.1 9.3 %collective-permute-start.9 = (bf16[8,2304]{1,0:T(8,128)(2,1)S(1)}, bf16[8,2304]{1,0:T(8,128)(2,1)S(1)}, u32[]{:S(2)}, u32[]{:S(2)}) collective-permute-start(bf16[8,2304]{1,0:T(8,128)(2,1)S(1)} %get-tuple-element.57), channel_id=1, source_target_pairs={{0,6},{1,7},{2,8},{3,9},{4,10},{5,11},{6,12},{7,13},{8,14},{9,15},... | collective-permute-start | bytes 110600 | tf_op jit(solution)/shard_map/ppermute | solution.py:314
  17.1 11.8 %collective-permute-start.10 = (bf16[8,2304]{1,0:T(8,128)(2,1)S(1)}, bf16[8,2304]{1,0:T(8,128)(2,1)S(1)}, u32[]{:S(2)}, u32[]{:S(2)}) collective-permute-start(bf16[8,2304]{1,0:T(8,128)(2,1)S(1)} %get-tuple-element.58), channel_id=1, source_target_pairs={{0,13},{1,14},{2,15},{3,0},{4,1},{5,2},{6,3},{7,4},{8,5},{9,6},{10... | collective-permute-start | bytes 110600 | tf_op jit(solution)/shard_map/ppermute | solution.py:314
  20.8 8.1 %collective-permute-start.11 = (bf16[8,2304]{1,0:T(8,128)(2,1)S(1)}, bf16[8,2304]{1,0:T(8,128)(2,1)S(1)}, u32[]{:S(2)}, u32[]{:S(2)}) collective-permute-start(bf16[8,2304]{1,0:T(8,128)(2,1)S(1)} %get-tuple-element.59), channel_id=1, source_target_pairs={{0,4},{1,5},{2,6},{3,7},{4,8},{5,9},{6,10},{7,11},{8,12},{9,13},{1... | collective-permute-start | bytes 110600 | tf_op jit(solution)/shard_map/ppermute | solution.py:314
  20.8 8.1 %collective-permute-start.12 = (bf16[8,2304]{1,0:T(8,128)(2,1)S(1)}, bf16[8,2304]{1,0:T(8,128)(2,1)S(1)}, u32[]{:S(2)}, u32[]{:S(2)}) collective-permute-start(bf16[8,2304]{1,0:T(8,128)(2,1)S(1)} %get-tuple-element.60), channel_id=1, source_target_pairs={{0,11},{1,12},{2,13},{3,14},{4,15},{5,0},{6,1},{7,2},{8,3},{9,4},{... | collective-permute-start | bytes 110600 | tf_op jit(solution)/shard_map/ppermute | solution.py:314
  21.8 4.7 %copy-start.2 = (s32[16,1]{0,1:T(1,128)S(1)}, s32[16,1]{0,1:T(1,128)}, u32[]{:S(2)}) copy-start(s32[16,1]{0,1:T(1,128)} %param.9) | copy-start | bytes 196
  21.8 4.7 %copy-start.3 = (s32[16]{0:T(128)S(1)}, s32[16]{0:T(128)}, u32[]{:S(2)}) copy-start(s32[16]{0:T(128)} %prefix_len.1) | copy-start | bytes 196
  21.8 7.2 %collective-permute-start.13 = (bf16[8,2304]{1,0:T(8,128)(2,1)S(1)}, bf16[8,2304]{1,0:T(8,128)(2,1)S(1)}, u32[]{:S(2)}, u32[]{:S(2)}) collective-permute-start(bf16[8,2304]{1,0:T(8,128)(2,1)S(1)} %get-tuple-element.61), channel_id=1, source_target_pairs={{0,2},{1,3},{2,4},{3,5},{4,6},{5,7},{6,8},{7,9},{8,10},{9,11},{10,... | collective-permute-start | bytes 110600 | tf_op jit(solution)/shard_map/ppermute | solution.py:314
  26.5 4.3 %collective-permute-start.14 = (bf16[8,2304]{1,0:T(8,128)(2,1)S(1)}, bf16[8,2304]{1,0:T(8,128)(2,1)S(1)}, u32[]{:S(2)}, u32[]{:S(2)}) collective-permute-start(bf16[8,2304]{1,0:T(8,128)(2,1)S(1)} %get-tuple-element.62), channel_id=1, source_target_pairs={{0,9},{1,10},{2,11},{3,12},{4,13},{5,14},{6,15},{7,0},{8,1},{9,2},... | collective-permute-start | bytes 110600 | tf_op jit(solution)/shard_map/ppermute | solution.py:314
  26.5 1.0 %copy-start = (bf16[2048,128]{1,0:T(8,128)(2,1)S(1)}, bf16[2048,128]{1,0:T(8,128)(2,1)}, u32[]{:S(2)}) copy-start(bf16[2048,128]{1,0:T(8,128)(2,1)} %values.1) | copy-start | bytes 1572868
  27.5 3.3 %copy-start.4 = (bf16[2048,128]{1,0:T(8,128)(2,1)S(1)}, bf16[2048,128]{1,0:T(8,128)(2,1)}, u32[]{:S(2)}) copy-start(bf16[2048,128]{1,0:T(8,128)(2,1)} %keys.1) | copy-start | bytes 1572868
  33.5 8.3 %collective-permute-start.15 = (bf16[8,2048]{1,0:T(8,128)(2,1)S(1)}, bf16[8,2048]{1,0:T(8,128)(2,1)S(1)}, u32[]{:S(2)}, u32[]{:S(2)}) collective-permute-start(bf16[8,2048]{1,0:T(8,128)(2,1)S(1)} %get-tuple-element.64), channel_id=1, source_target_pairs={{0,9},{1,10},{2,11},{3,12},{4,13},{5,14},{6,15},{7,0},{8,1},{9,2},... | collective-permute-start | bytes 98312 | tf_op jit(solution)/shard_map/ppermute | solution.py:314
  33.8 8.0 %collective-permute-start.16 = (bf16[8,2048]{1,0:T(8,128)(2,1)S(1)}, bf16[8,2048]{1,0:T(8,128)(2,1)S(1)}, u32[]{:S(2)}, u32[]{:S(2)}) collective-permute-start(bf16[8,2048]{1,0:T(8,128)(2,1)S(1)} %get-tuple-element.65), channel_id=1, source_target_pairs={{0,2},{1,3},{2,4},{3,5},{4,6},{5,7},{6,8},{7,9},{8,10},{9,11},{10,... | collective-permute-start | bytes 98312 | tf_op jit(solution)/shard_map/ppermute | solution.py:314
  36.5 9.4 %collective-permute-start.17 = (bf16[8,2048]{1,0:T(8,128)(2,1)S(1)}, bf16[8,2048]{1,0:T(8,128)(2,1)S(1)}, u32[]{:S(2)}, u32[]{:S(2)}) collective-permute-start(bf16[8,2048]{1,0:T(8,128)(2,1)S(1)} %get-tuple-element.66), channel_id=1, source_target_pairs={{0,11},{1,12},{2,13},{3,14},{4,15},{5,0},{6,1},{7,2},{8,3},{9,4},{... | collective-permute-start | bytes 98312 | tf_op jit(solution)/shard_map/ppermute | solution.py:314
  39.8 6.0 %collective-permute-start.18 = (bf16[8,2048]{1,0:T(8,128)(2,1)S(1)}, bf16[8,2048]{1,0:T(8,128)(2,1)S(1)}, u32[]{:S(2)}, u32[]{:S(2)}) collective-permute-start(bf16[8,2048]{1,0:T(8,128)(2,1)S(1)} %get-tuple-element.67), channel_id=1, source_target_pairs={{0,4},{1,5},{2,6},{3,7},{4,8},{5,9},{6,10},{7,11},{8,12},{9,13},{1... | collective-permute-start | bytes 98312 | tf_op jit(solution)/shard_map/ppermute | solution.py:314
  39.8 6.1 %collective-permute-start.19 = (bf16[8,2048]{1,0:T(8,128)(2,1)S(1)}, bf16[8,2048]{1,0:T(8,128)(2,1)S(1)}, u32[]{:S(2)}, u32[]{:S(2)}) collective-permute-start(bf16[8,2048]{1,0:T(8,128)(2,1)S(1)} %get-tuple-element.68), channel_id=1, source_target_pairs={{0,13},{1,14},{2,15},{3,0},{4,1},{5,2},{6,3},{7,4},{8,5},{9,6},{10... | collective-permute-start | bytes 98312 | tf_op jit(solution)/shard_map/ppermute | solution.py:314
  41.7 6.0 %collective-permute-start.20 = (bf16[8,2048]{1,0:T(8,128)(2,1)S(1)}, bf16[8,2048]{1,0:T(8,128)(2,1)S(1)}, u32[]{:S(2)}, u32[]{:S(2)}) collective-permute-start(bf16[8,2048]{1,0:T(8,128)(2,1)S(1)} %get-tuple-element.69), channel_id=1, source_target_pairs={{0,6},{1,7},{2,8},{3,9},{4,10},{5,11},{6,12},{7,13},{8,14},{9,15},... | collective-permute-start | bytes 98312 | tf_op jit(solution)/shard_map/ppermute | solution.py:314
  41.8 8.1 %collective-permute-start.21 = (bf16[8,2048]{1,0:T(8,128)(2,1)S(1)}, bf16[8,2048]{1,0:T(8,128)(2,1)S(1)}, u32[]{:S(2)}, u32[]{:S(2)}) collective-permute-start(bf16[8,2048]{1,0:T(8,128)(2,1)S(1)} %get-tuple-element.70), channel_id=1, source_target_pairs={{0,15},{1,0},{2,1},{3,2},{4,3},{5,4},{6,5},{7,6},{8,7},{9,8},{10,9... | collective-permute-start | bytes 98312 | tf_op jit(solution)/shard_map/ppermute | solution.py:314
  45.8 5.2 %collective-permute-start.22 = (bf16[8,2048]{1,0:T(8,128)(2,1)S(1)}, bf16[8,2048]{1,0:T(8,128)(2,1)S(1)}, u32[]{:S(2)}, u32[]{:S(2)}) collective-permute-start(bf16[8,2048]{1,0:T(8,128)(2,1)S(1)} %get-tuple-element.71), channel_id=1, source_target_pairs={{0,8},{1,9},{2,10},{3,11},{4,12},{5,13},{6,14},{7,15},{8,0},{9,1},... | collective-permute-start | bytes 98312 | tf_op jit(solution)/shard_map/ppermute | solution.py:314
  45.8 6.1 %collective-permute-start.23 = (bf16[8,2048]{1,0:T(8,128)(2,1)S(1)}, bf16[8,2048]{1,0:T(8,128)(2,1)S(1)}, u32[]{:S(2)}, u32[]{:S(2)}) collective-permute-start(bf16[8,2048]{1,0:T(8,128)(2,1)S(1)} %get-tuple-element.72), channel_id=1, source_target_pairs={{0,1},{1,2},{2,3},{3,4},{4,5},{5,6},{6,7},{7,8},{8,9},{9,10},{10,1... | collective-permute-start | bytes 98312 | tf_op jit(solution)/shard_map/ppermute | solution.py:314
  45.9 10.3 %collective-permute-start.24 = (bf16[8,2048]{1,0:T(8,128)(2,1)S(1)}, bf16[8,2048]{1,0:T(8,128)(2,1)S(1)}, u32[]{:S(2)}, u32[]{:S(2)}) collective-permute-start(bf16[8,2048]{1,0:T(8,128)(2,1)S(1)} %get-tuple-element.73), channel_id=1, source_target_pairs={{0,10},{1,11},{2,12},{3,13},{4,14},{5,15},{6,0},{7,1},{8,2},{9,3},... | collective-permute-start | bytes 98312 | tf_op jit(solution)/shard_map/ppermute | solution.py:314
  47.8 8.6 %collective-permute-start.25 = (bf16[8,2048]{1,0:T(8,128)(2,1)S(1)}, bf16[8,2048]{1,0:T(8,128)(2,1)S(1)}, u32[]{:S(2)}, u32[]{:S(2)}) collective-permute-start(bf16[8,2048]{1,0:T(8,128)(2,1)S(1)} %get-tuple-element.74), channel_id=1, source_target_pairs={{0,3},{1,4},{2,5},{3,6},{4,7},{5,8},{6,9},{7,10},{8,11},{9,12},{10... | collective-permute-start | bytes 98312 | tf_op jit(solution)/shard_map/ppermute | solution.py:314
  49.9 6.4 %collective-permute-start.26 = (bf16[8,2048]{1,0:T(8,128)(2,1)S(1)}, bf16[8,2048]{1,0:T(8,128)(2,1)S(1)}, u32[]{:S(2)}, u32[]{:S(2)}) collective-permute-start(bf16[8,2048]{1,0:T(8,128)(2,1)S(1)} %get-tuple-element.75), channel_id=1, source_target_pairs={{0,12},{1,13},{2,14},{3,15},{4,0},{5,1},{6,2},{7,3},{8,4},{9,5},{1... | collective-permute-start | bytes 98312 | tf_op jit(solution)/shard_map/ppermute | solution.py:314
  51.1 5.3 %collective-permute-start.27 = (bf16[8,2048]{1,0:T(8,128)(2,1)S(1)}, bf16[8,2048]{1,0:T(8,128)(2,1)S(1)}, u32[]{:S(2)}, u32[]{:S(2)}) collective-permute-start(bf16[8,2048]{1,0:T(8,128)(2,1)S(1)} %get-tuple-element.76), channel_id=1, source_target_pairs={{0,5},{1,6},{2,7},{3,8},{4,9},{5,10},{6,11},{7,12},{8,13},{9,14},{... | collective-permute-start | bytes 98312 | tf_op jit(solution)/shard_map/ppermute | solution.py:314
  51.9 5.9 %collective-permute-start.28 = (bf16[8,2048]{1,0:T(8,128)(2,1)S(1)}, bf16[8,2048]{1,0:T(8,128)(2,1)S(1)}, u32[]{:S(2)}, u32[]{:S(2)}) collective-permute-start(bf16[8,2048]{1,0:T(8,128)(2,1)S(1)} %get-tuple-element.77), channel_id=1, source_target_pairs={{0,14},{1,15},{2,0},{3,1},{4,2},{5,3},{6,4},{7,5},{8,6},{9,7},{10,... | collective-permute-start | bytes 98312 | tf_op jit(solution)/shard_map/ppermute | solution.py:314
  56.3 4.5 %collective-permute-start.29 = (bf16[8,2048]{1,0:T(8,128)(2,1)S(1)}, bf16[8,2048]{1,0:T(8,128)(2,1)S(1)}, u32[]{:S(2)}, u32[]{:S(2)}) collective-permute-start(bf16[8,2048]{1,0:T(8,128)(2,1)S(1)} %get-tuple-element.78), channel_id=1, source_target_pairs={{0,7},{1,8},{2,9},{3,10},{4,11},{5,12},{6,13},{7,14},{8,15},{9,0},... | collective-permute-start | bytes 98312 | tf_op jit(solution)/shard_map/ppermute | solution.py:314

commit v6 on v2

--- a/solution.py
+++ b/solution.py
@@ -21,6 +21,7 @@
 MSG = 2 * TOK_REQ
 WIDE = HALF * HD
 ROWS = REQUESTS * TOK_REQ
+STRIP = 256
 SCALE = HD**-0.5
 FLOOR = -1e30
 NT = (((1,), (1,)), ((), ()))
@@ -36,7 +37,7 @@
     return lax.dot_general(a, b, dims, preferred_element_type=jnp.float32, **kw)
 
 
-def pack_kernel(devices, hit_count, hits, q, k, v, send, places, held, count, sems):
+def pack_kernel(devices, hit_count, owners, q, k, v, send, places, held, hits, count, sems):
     copies = [
         pltpu.make_async_copy(source, held.at[pl.ds(row, ROWS), pl.ds(column, width)], sems.at[n])
         for n, (source, row, column, width) in enumerate(
@@ -48,10 +49,13 @@
             ]
         )
     ]
+    first = pltpu.make_async_copy(owners, hits, sems.at[4])
+    first.start()
     for copy in copies:
         copy.start()
     lane = iota((1, 2 * ROWS), 1)
     lane_request = (lane % ROWS) // TOK_REQ
+    first.wait()
     for r in range(REQUESTS):
         for i in range(hit_count):
             count[hits[r * hit_count + i]] = 0
@@ -98,8 +102,9 @@
                 request = jnp.where(here, r, request)
                 which = jnp.where(here, i, which)
                 seen = seen + mine.astype(jnp.int32)
-        busy[slot] = (seen > slot).astype(jnp.int32)
         limit = prefix_len[request] - which * REGION
+        blocks = jnp.clip((limit + STRIP - 1) // STRIP, 1, REGION // STRIP)
+        busy[slot] = jnp.where(seen > slot, blocks, 0)
         cached[slot : slot + 1, :] = jnp.where(iota((1, REGION), 1) < limit, 0.0, FLOOR)
         span_row = span[pl.ds(request, 1), :].astype(jnp.float32)
         source = iota((devices, total_rows), 0)
@@ -133,63 +138,82 @@
         pl.loop(0, blocks)(one_block)
 
 
+def lanes_max(parts):
+    pieces = [part[:, n : n + HD] for part in parts for n in range(0, part.shape[1], HD)]
+    return jnp.max(functools.reduce(jnp.maximum, pieces), axis=1, keepdims=True)
+
+
 def attend_kernel(devices, hit_count, busy, prompt_mask, cached_mask, got, keys, wide, out, *levels):
     total_rows = devices * MSG
     block = 16 * MSG
     factor = SCALE * math.log2(math.e)
-    for slot in range(CAP):
-        base = slot * (WIDE + HD)
-        region = slice(slot * REGION, (slot + 1) * REGION)
-        first = slot * WIDE
-
-        @pl.when(busy[slot] == 0)
-        def _():
-            out[:, first : first + WIDE] = jnp.zeros((total_rows, WIDE), jnp.bfloat16)
+
+    def nothing(slot):
+        out[:, pl.ds(slot * WIDE, WIDE)] = jnp.zeros((total_rows, WIDE), jnp.bfloat16)
+        for lse in levels:
+            lse[:, pl.ds(slot * HD, HD)] = jnp.zeros((total_rows, HD), jnp.float32)
+
+    def attend(slot, strips):
+        whole = (strips - 1) * STRIP
+        base = pl.multiple_of(slot * (WIDE + HD), HD)
+        region = pl.multiple_of(slot * REGION, REGION)
+        head = pl.ds(region, whole) if whole else None
+        tail = pl.ds(pl.multiple_of(region + whole, STRIP), STRIP)
+        tail_mask = cached_mask[pl.ds(slot, 1), whole : whole + STRIP]
+        prompt_keys = got[:, pl.ds(base + WIDE, HD)]
+        moved = pltpu.roll(prompt_keys.astype(jnp.float32), total_rows - TOK_REQ, 0)
+        prompt_values = jnp.concatenate(
+            [moved.astype(jnp.bfloat16), jnp.ones((total_rows, HD), jnp.bfloat16)], axis=1
+        )
+
+        def one_block(at):
+            here = pl.ds(at * block, block)
+            prompt_bias = prompt_mask[pl.ds(slot * total_rows + at * block, block), :]
+            prompt_bias = jnp.concatenate([prompt_bias, prompt_bias], axis=0)
+            lane = iota((block, HD), 1)
+
+            def scores(c):
+                pair = jnp.concatenate(
+                    [got[here, pl.ds(base + (c + n) * HD, HD)] for n in range(2)], axis=0
+                )
+                parts = [dot(pair, keys[head, :], NT)] if whole else []
+                parts.append(dot(pair, keys[tail, :], NT) + tail_mask)
+                parts.append(dot(pair, prompt_keys, NT) + prompt_bias)
+                return parts
+
+            logs = jnp.zeros((block, HD), jnp.float32)
+            parts = scores(0)
+            for c in range(0, HALF, 2):
+                later = scores(c + 2) if c + 2 < HALF else None
+                top = lanes_max(parts)
+                if hit_count > 1:
+                    top = jnp.maximum(top, 0.1 * FLOOR)
+                parts = [jnp.exp2((x - top) * factor).astype(jnp.bfloat16) for x in parts]
+                summed = dot(parts[-1], prompt_values, NN) + dot(parts[-2], wide[tail, :], NN)
+                if whole:
+                    summed = summed + dot(parts[0], wide[head, :], NN)
+                totals = summed[:, HD:]
+                if hit_count > 1:
+                    totals = jnp.maximum(totals, 1.0)
+                    level = top * SCALE + jnp.log(totals)
+                    logs = jnp.where(lane == c, level[:block], logs)
+                    logs = jnp.where(lane == c + 1, level[block:], logs)
+                result = (summed[:, :HD] / totals).astype(jnp.bfloat16)
+                for n in range(2):
+                    column = pl.multiple_of(slot * WIDE + (c + n) * HD, HD)
+                    out[here, pl.ds(column, HD)] = result[n * block : (n + 1) * block]
+                parts = later
             for lse in levels:
-                lse[:, slot * HD : (slot + 1) * HD] = jnp.zeros((total_rows, HD), jnp.float32)
-
-        @pl.when(busy[slot] != 0)
-        def _():
-            prompt_keys = got[:, base + WIDE : base + WIDE + HD]
-            moved = pltpu.roll(prompt_keys.astype(jnp.float32), total_rows - TOK_REQ, 0)
-            prompt_values = jnp.concatenate(
-                [moved.astype(jnp.bfloat16), jnp.ones((total_rows, HD), jnp.bfloat16)], axis=1
-            )
-
-            def one_block(at):
-                here = pl.ds(at * block, block)
-                prompt_bias = prompt_mask[pl.ds(slot * total_rows + at * block, block), :]
-                prompt_bias = jnp.concatenate([prompt_bias, prompt_bias], axis=0)
-                lane = iota((block, HD), 1)
-                logs = jnp.zeros((block, HD), jnp.float32)
-                for c in range(0, HALF, 2):
-                    at_c = [base + (c + n) * HD for n in range(2)]
-                    pair = jnp.concatenate([got[here, n : n + HD] for n in at_c], axis=0)
-                    cached = dot(pair, keys[region, :], NT) + cached_mask[slot : slot + 1, :]
-                    prompt = dot(pair, prompt_keys, NT) + prompt_bias
-                    top = jnp.maximum(
-                        jnp.max(cached, axis=1, keepdims=True),
-                        jnp.max(prompt, axis=1, keepdims=True),
-                    )
-                    if hit_count > 1:
-                        top = jnp.maximum(top, 0.1 * FLOOR)
-                    cached = jnp.exp2((cached - top) * factor).astype(jnp.bfloat16)
-                    prompt = jnp.exp2((prompt - top) * factor).astype(jnp.bfloat16)
-                    summed = dot(cached, wide[region, :], NN) + dot(prompt, prompt_values, NN)
-                    totals = summed[:, HD:]
-                    if hit_count > 1:
-                        totals = jnp.maximum(totals, 1.0)
-                        level = top * SCALE + jnp.log(totals)
-                        logs = jnp.where(lane == c, level[:block], logs)
-                        logs = jnp.where(lane == c + 1, level[block:], logs)
-                    result = (summed[:, :HD] / totals).astype(jnp.bfloat16)
-                    for n in range(2):
-                        column = first + (c + n) * HD
-                        out[here, column : column + HD] = result[n * block : (n + 1) * block]
-                for lse in levels:
-                    lse[here, slot * HD : (slot + 1) * HD] = logs
-
-            each_block(devices, one_block)
+                lse[here, pl.ds(pl.multiple_of(slot * HD, HD), HD)] = logs
+
+        each_block(devices, one_block)
+
+    @pl.loop(0, CAP)
+    def _(slot):
+        strips = busy[slot]
+        pl.when(strips == 0)(lambda: nothing(slot))
+        for count in range(1, REGION // STRIP + 1):
+            pl.when(strips == count)(functools.partial(attend, slot, count))
 
 
 def unpack_kernel(devices, hit_count, places, *refs):
@@ -257,6 +281,7 @@
     hit_count = hits.shape[1]
     rows = devices * MSG
     owners = hits.reshape(REQUESTS * hit_count)
+    fresh = (owners, queries, fresh_keys, fresh_values)
 
     def exchange(x):
         return lax.all_to_all(x, "cache", split_axis=0, concat_axis=0, tiled=True)
@@ -274,15 +299,15 @@
         pack_kernel,
         [((rows, CAP * (WIDE + HD)), jnp.bfloat16), ((CAP * hit_count, 2 * ROWS), jnp.int32)],
         "pack",
-        grant=60,
-        in_specs=smem(1) + hbm(3),
+        in_specs=hbm(4),
         out_specs=vmem(2),
         scratch_shapes=[
             pltpu.VMEM((2 * ROWS, WIDE + HD), jnp.bfloat16),
+            pltpu.SMEM((REQUESTS * hit_count,), jnp.int32),
             pltpu.SMEM((devices,), jnp.int32),
-            pltpu.SemaphoreType.DMA((4,)),
+            pltpu.SemaphoreType.DMA((5,)),
         ],
-    )(owners, queries, fresh_keys, fresh_values)
+    )(*(pltpu.with_memory_space_constraint(x, pltpu.HBM) for x in fresh))
     got = exchange(send)
     busy, prompt_mask, cached_mask, wide = call(
         prep_kernel,

time: 50.3 us -> 48.6 us (0.966); the launches traced: 50 us -> 47.7 us
  Pallas kernels: 9.71 us -> 7.21 us
  blocking collectives: 17.8 us -> 18.7 us
  local copies, waits for them, and re-layouts: 0.71 us -> 0.03 us
    pallas_call x1, Pallas kernels: 4.54 us -> 2.68 us  [body(): call(attend_kernel, [((rows, CAP * WIDE), jnp.bfloat16)] + [((rows, CAP *...]
    all_to_all x1, blocking collectives: 17.8 us -> 18.7 us  [exchange(): return lax.all_to_all(x, 'cache', split_axis=0, concat_axis=0, tiled=True)]
    unnamed x12 -> x10, local copies, waits for them, and re-layouts: 0.71 us -> 0.03 us
    pallas_call x1, Pallas kernels: 2.79 us -> 2.13 us  [body(): call(pack_kernel, [((rows, CAP * (WIDE + HD)), jnp.bfloat16), ((CAP * hit...]
where the time goes in v6:
time: 48.6 us; the launch traced here: 47.7 us
  blocking collectives  18.7 us (38%)
  waiting for transfers between devices  14.1 us (29%)
  starting transfers between devices  7.53 us (15%)
  Pallas kernels  7.21 us (15%)
    all_to_all x1, blocking collectives, exchange(): return lax.all_to_all(x, 'cache', split_axis=0, concat_axis=0, tiled=True)  18.7 us
    all_to_all x1, waiting for transfers between devices, exchange(): return lax.all_to_all(x, 'cache', split_axis=0, concat_axis=0, tiled=True)  14.1 us
    all_to_all x1, starting transfers between devices, exchange(): return lax.all_to_all(x, 'cache', split_axis=0, concat_axis=0, tiled=True)  7.53 us
    pallas_call x1, Pallas kernels, body(): call(attend_kernel, [((rows, CAP * WIDE), jnp.bfloat16)] + [((rows, CAP *...  2.68 us
    pallas_call x1, Pallas kernels, body(): call(pack_kernel, [((rows, CAP * (WIDE + HD)), jnp.bfloat16), ((CAP * hit...  2.13 us
    pallas_call x1, Pallas kernels, body(): call(prep_kernel, [((CAP,), jnp.int32), ((CAP * rows, rows), jnp.float32)...  1.36 us
    pallas_call x1, Pallas kernels, body(): call(unpack_kernel, [((ROWS, HEADS * HD), jnp.bfloat16)], 'unpack', in_sp...  1.04 us
  transfers between devices with their start and end apart: 1, of which 1 were waited for; matrix products, arithmetic and copies ran while one was open for 0% of the time, Pallas kernels for 3%

profile of v6, /device:TPU:0, one launch (start us, length us, event | category | flops | bytes accessed | tf_op | source)
XLA Modules:
  0.0 47.7 jit_solution(2933020242505737998)
XLA Ops:
  0.0 2.1 %pack.1 = (bf16[128,2304]{1,0:T(8,128)(2,1)}, s32[2,128]{1,0:T(2,128)S(1)}) custom-call(s32[16]{0:T(128)} %bitcast.8, bf16[64,2048]{1,0:T(8,128)(2,1)} %q.1, bf16[64,128]{1,0:T(8,128)(2,1)} %k.1, bf16[64,128]{1,0:T(8,128)(2,1)} %v.1), custom_call_target="tpu_custom_call" | custom-call | tf_op jit(solution)/shard_map/pack/pallas_call | solution.py:298
  2.1 0.0 copy-start
  2.2 0.0 copy-start.1
  2.2 0.0 copy-start.2
  2.2 0.0 copy-start.3
  2.2 7.5 %all-to-all-start = ((bf16[16,8,2304]{2,1,0:T(8,128)(2,1)}), bf16[16,8,2304]{2,1,0:T(8,128)(2,1)S(1)}, u32[]{:S(2)}, u32[]{:S(2)}) async-start(bf16[16,8,2304]{2,1,0:T(8,128)(2,1)} %bitcast.1), calls=%async_computation | async-start | bytes 1179648 | tf_op jit(solution)/shard_map/all_to_all | solution.py:287
  9.7 0.0 copy-done
  9.7 0.0 copy-done.1
  9.8 0.0 copy-done.2
  9.8 0.0 copy-done.3
  9.8 0.0 copy-start.4
  9.8 1.4 %prep.1 = (s32[2]{0:T(128)S(1)}, f32[256,128]{1,0:T(8,128)S(1)}, f32[2,1024]{1,0:T(2,128)S(1)}, bf16[2048,256]{1,0:T(8,128)(2,1)S(1)}) custom-call(s32[16]{0:T(128)S(1)} %bitcast.9, s32[16]{0:T(128)S(1)} %copy-done.3, s32[16,16]{1,0:T(8,128)S(1)} %copy-done.1, bf16[2048,128]{1,0:T(8,128)(2,1)S(1)} %copy-done), custom_call_target="tpu_custom_call" | custom-call | flops 1000000 | bytes 4194304 | tf_op jit(solution)/shard_map/prep/pallas_call | solution.py:312
  11.2 14.1 %all-to-all-done = bf16[16,8,2304]{2,1,0:T(8,128)(2,1)S(1)} async-done(((bf16[16,8,2304]{2,1,0:T(8,128)(2,1)}), bf16[16,8,2304]{2,1,0:T(8,128)(2,1)S(1)}, u32[]{:S(2)}, u32[]{:S(2)}) %all-to-all-start) | async-done | bytes 589856 | tf_op jit(solution)/shard_map/all_to_all | solution.py:287
  25.3 0.0 copy-done.4
  25.3 2.7 %attend.1 = bf16[128,2048]{1,0:T(8,128)(2,1)S(1)} custom-call(s32[2]{0:T(128)S(1)} %get-tuple-element.12.busy, f32[256,128]{1,0:T(8,128)S(1)} %get-tuple-element.13.prompt_mask, f32[2,1024]{1,0:T(2,128)S(1)} %get-tuple-element.14.cached_mask, bf16[128,2304]{1,0:T(8,128)(2,1)S(1)} %bitcast.6, bf16[2048,128]{1,0:T(8,128)(2,1)S(1)} %copy-done.4, ...), custom_call_target="tpu_custom_call" | custom-call | flops 1207959552 | bytes 1048576 | tf_op jit(solution)/shard_map/attend/pallas_call | solution.py:326
  28.0 18.7 %all_to_all.22 = bf16[16,8,2048]{2,1,0:T(8,128)(2,1)S(1)} all-to-all(bf16[16,8,2048]{2,1,0:T(8,128)(2,1)S(1)} %bitcast.7), channel_id=1, replica_groups=mesh['groups'=2,'cache'=16] {'cache'}, dimensions={0} | all-to-all | bytes 1048576 | tf_op jit(solution)/shard_map/all_to_all | solution.py:287
  46.7 1.0 %unpack.1 = bf16[64,2048]{1,0:T(8,128)(2,1)} custom-call(s32[2,128]{1,0:T(2,128)S(1)} %get-tuple-element.11.places, bf16[128,2048]{1,0:T(8,128)(2,1)S(1)} %bitcast.5), custom_call_target="tpu_custom_call" | custom-call | tf_op jit(solution)/shard_map/unpack/pallas_call | solution.py:338
Async XLA Ops:
  2.1 7.6 %copy-start = (bf16[2048,128]{1,0:T(8,128)(2,1)S(1)}, bf16[2048,128]{1,0:T(8,128)(2,1)}, u32[]{:S(2)}) copy-start(bf16[2048,128]{1,0:T(8,128)(2,1)} %values.1) | copy-start | bytes 1572868
  2.2 7.6 %copy-start.1 = (s32[16,16]{1,0:T(8,128)S(1)}, s32[16,16]{1,0:T(8,128)}, u32[]{:S(2)}) copy-start(s32[16,16]{1,0:T(8,128)} %span.1) | copy-start | bytes 3076
  2.2 7.6 %copy-start.2 = (s32[16,1]{0,1:T(1,128)S(1)}, s32[16,1]{0,1:T(1,128)}, u32[]{:S(2)}) copy-start(s32[16,1]{0,1:T(1,128)} %param.9) | copy-start | bytes 196
  2.2 7.6 %copy-start.3 = (s32[16]{0:T(128)S(1)}, s32[16]{0:T(128)}, u32[]{:S(2)}) copy-start(s32[16]{0:T(128)} %prefix_len.1) | copy-start | bytes 196
  2.2 23.1 %all-to-all-start = ((bf16[16,8,2304]{2,1,0:T(8,128)(2,1)}), bf16[16,8,2304]{2,1,0:T(8,128)(2,1)S(1)}, u32[]{:S(2)}, u32[]{:S(2)}) async-start(bf16[16,8,2304]{2,1,0:T(8,128)(2,1)} %bitcast.1), calls=%async_computation | async-start | bytes 1179648 | tf_op jit(solution)/shard_map/all_to_all | solution.py:287
  9.8 15.5 %copy-start.4 = (bf16[2048,128]{1,0:T(8,128)(2,1)S(1)}, bf16[2048,128]{1,0:T(8,128)(2,1)}, u32[]{:S(2)}) copy-start(bf16[2048,128]{1,0:T(8,128)(2,1)} %keys.1) | copy-start | bytes 1572868

commit v7 on v6

--- a/solution.py
+++ b/solution.py
@@ -35,6 +35,14 @@
 
 def dot(a, b, dims, **kw):
     return lax.dot_general(a, b, dims, preferred_element_type=jnp.float32, **kw)
+
+
+def place_of(devices, device):
+    return device % (devices // 2) * 2 + device // (devices // 2)
+
+
+def device_at(devices, place):
+    return place % 2 * (devices // 2) + place // 2
 
 
 def pack_kernel(devices, hit_count, owners, q, k, v, send, places, held, hits, count, sems):
@@ -65,8 +73,9 @@
             owner = hits[r * hit_count + i]
             rank = count[owner]
             count[owner] = rank + 1
+            message = place_of(devices, owner) * MSG
             for s in range(CAP):
-                place = jnp.where(rank == s, owner * MSG, -4 * MSG)
+                place = jnp.where(rank == s, message, -4 * MSG)
                 rows[s][i] = jnp.where(lane_request == r, place, rows[s][i])
     inner = lane // ROWS * TOK_REQ + lane % TOK_REQ
     target = iota((devices * MSG, 2 * ROWS), 0)
@@ -107,8 +116,8 @@
         busy[slot] = jnp.where(seen > slot, blocks, 0)
         cached[slot : slot + 1, :] = jnp.where(iota((1, REGION), 1) < limit, 0.0, FLOOR)
         span_row = span[pl.ds(request, 1), :].astype(jnp.float32)
-        source = iota((devices, total_rows), 0)
-        spread = (iota((devices, total_rows), 1) // MSG == source).astype(jnp.bfloat16)
+        source = device_at(devices, iota((devices, total_rows), 1) // MSG)
+        spread = (iota((devices, total_rows), 0) == source).astype(jnp.bfloat16)
         spans = jnp.broadcast_to(span_row, (16, devices)).astype(jnp.bfloat16)
         key_span = dot(spans, spread, NN)[:1]
         lane = iota((1, total_rows), 1)
@@ -120,7 +129,7 @@
         block = 16 * MSG
 
         def one_block(at):
-            row_source = at * 16 + iota((block, devices), 0) // MSG
+            row_source = device_at(devices, at * 16 + iota((block, devices), 0) // MSG)
             mine = iota((block, devices), 1) == row_source
             row_span = jnp.sum(jnp.where(mine, span_row, 0.0), axis=1, keepdims=True)
             row_spot = row_span.astype(jnp.int32) * TOK_REQ + iota((block, 1), 0) % TOK_REQ
@@ -283,8 +292,12 @@
     owners = hits.reshape(REQUESTS * hit_count)
     fresh = (owners, queries, fresh_keys, fresh_values)
 
+    order = [[device_at(devices, place) for place in range(devices)]]
+
     def exchange(x):
-        return lax.all_to_all(x, "cache", split_axis=0, concat_axis=0, tiled=True)
+        return lax.all_to_all(
+            x, "cache", split_axis=0, concat_axis=0, axis_index_groups=order, tiled=True
+        )
 
     def call(kernel, out_shape, name, grant=40, **kw):
         return pl.pallas_call(

time: 48.6 us -> 49.9 us (1.027); the launches traced: 47.7 us -> 50.2 us
  blocking collectives: 18.7 us -> 20.4 us
  waiting for transfers between devices: 14.1 us -> 15.3 us
    all_to_all x1, blocking collectives: 18.7 us -> 20.4 us  [exchange(): lax.all_to_all(x, 'cache', split_axis=0, concat_axis=0, axis_index_groups...]
    all_to_all x1, waiting for transfers between devices: 14.1 us -> 15.3 us  [exchange(): lax.all_to_all(x, 'cache', split_axis=0, concat_axis=0, axis_index_groups...]
where the time goes in v7:
time: 49.9 us; the launch traced here: 50.2 us
  blocking collectives  20.4 us (41%)
  waiting for transfers between devices  15.3 us (31%)
  starting transfers between devices  7.53 us (15%)
  Pallas kernels  6.8 us (14%)
    all_to_all x1, blocking collectives, exchange(): lax.all_to_all(x, 'cache', split_axis=0, concat_axis=0, axis_index_groups...  20.4 us
    all_to_all x1, waiting for transfers between devices, exchange(): lax.all_to_all(x, 'cache', split_axis=0, concat_axis=0, axis_index_groups...  15.3 us
    all_to_all x1, starting transfers between devices, exchange(): lax.all_to_all(x, 'cache', split_axis=0, concat_axis=0, axis_index_groups...  7.53 us
    pallas_call x1, Pallas kernels, body(): call(attend_kernel, [((rows, CAP * WIDE), jnp.bfloat16)] + [((rows, CAP *...  2.28 us
    pallas_call x1, Pallas kernels, body(): call(pack_kernel, [((rows, CAP * (WIDE + HD)), jnp.bfloat16), ((CAP * hit...  2.13 us
    pallas_call x1, Pallas kernels, body(): call(prep_kernel, [((CAP,), jnp.int32), ((CAP * rows, rows), jnp.float32)...  1.36 us
    pallas_call x1, Pallas kernels, body(): call(unpack_kernel, [((ROWS, HEADS * HD), jnp.bfloat16)], 'unpack', in_sp...  1.03 us
  transfers between devices with their start and end apart: 1, of which 1 were waited for; matrix products, arithmetic and copies ran while one was open for 0% of the time, Pallas kernels for 3%

profile of v7, /device:TPU:0, one launch (start us, length us, event | category | flops | bytes accessed | tf_op | source)
XLA Modules:
  0.0 50.2 jit_solution(18279116901228661111)
XLA Ops:
  0.0 2.1 %pack.1 = (bf16[128,2304]{1,0:T(8,128)(2,1)}, s32[2,128]{1,0:T(2,128)S(1)}) custom-call(s32[16]{0:T(128)} %bitcast.8, bf16[64,2048]{1,0:T(8,128)(2,1)} %q.1, bf16[64,128]{1,0:T(8,128)(2,1)} %k.1, bf16[64,128]{1,0:T(8,128)(2,1)} %v.1), custom_call_target="tpu_custom_call" | custom-call | tf_op jit(solution)/shard_map/pack/pallas_call | solution.py:311
  2.1 0.0 copy-start
  2.2 0.0 copy-start.1
  2.2 0.0 copy-start.2
  2.2 0.0 copy-start.3
  2.2 7.5 %all-to-all-start = ((bf16[16,8,2304]{2,1,0:T(8,128)(2,1)}), bf16[16,8,2304]{2,1,0:T(8,128)(2,1)S(1)}, u32[]{:S(2)}, u32[]{:S(2)}) async-start(bf16[16,8,2304]{2,1,0:T(8,128)(2,1)} %bitcast.1), calls=%async_computation | async-start | bytes 1179648 | tf_op jit(solution)/shard_map/all_to_all | solution.py:298
  9.7 0.0 copy-done
  9.7 0.0 copy-done.1
  9.8 0.0 copy-done.2
  9.8 0.0 copy-done.3
  9.8 0.0 copy-start.4
  9.8 1.4 %prep.1 = (s32[2]{0:T(128)S(1)}, f32[256,128]{1,0:T(8,128)S(1)}, f32[2,1024]{1,0:T(2,128)S(1)}, bf16[2048,256]{1,0:T(8,128)(2,1)S(1)}) custom-call(s32[16]{0:T(128)S(1)} %bitcast.9, s32[16]{0:T(128)S(1)} %copy-done.3, s32[16,16]{1,0:T(8,128)S(1)} %copy-done.1, bf16[2048,128]{1,0:T(8,128)(2,1)S(1)} %copy-done), custom_call_target="tpu_custom_call" | custom-call | flops 1000000 | bytes 4194304 | tf_op jit(solution)/shard_map/prep/pallas_call | solution.py:325
  11.1 15.3 %all-to-all-done = bf16[16,8,2304]{2,1,0:T(8,128)(2,1)S(1)} async-done(((bf16[16,8,2304]{2,1,0:T(8,128)(2,1)}), bf16[16,8,2304]{2,1,0:T(8,128)(2,1)S(1)}, u32[]{:S(2)}, u32[]{:S(2)}) %all-to-all-start) | async-done | bytes 589856 | tf_op jit(solution)/shard_map/all_to_all | solution.py:298
  26.4 0.0 copy-done.4
  26.4 2.3 %attend.1 = bf16[128,2048]{1,0:T(8,128)(2,1)S(1)} custom-call(s32[2]{0:T(128)S(1)} %get-tuple-element.12.busy, f32[256,128]{1,0:T(8,128)S(1)} %get-tuple-element.13.prompt_mask, f32[2,1024]{1,0:T(2,128)S(1)} %get-tuple-element.14.cached_mask, bf16[128,2304]{1,0:T(8,128)(2,1)S(1)} %bitcast.6, bf16[2048,128]{1,0:T(8,128)(2,1)S(1)} %copy-done.4, ...), custom_call_target="tpu_custom_call" | custom-call | flops 1207959552 | bytes 1048576 | tf_op jit(solution)/shard_map/attend/pallas_call | solution.py:339
  28.7 20.4 %all_to_all.22 = bf16[16,8,2048]{2,1,0:T(8,128)(2,1)S(1)} all-to-all(bf16[16,8,2048]{2,1,0:T(8,128)(2,1)S(1)} %bitcast.7), channel_id=1, replica_groups={{0,8,1,9,2,10,3,11,4,12,5,13,6,14,7,15},{16,24,17,25,18,26,19,27,20,28,..., dimensions={0} | all-to-all | bytes 1048576 | tf_op jit(solution)/shard_map/all_to_all | solution.py:298
  49.2 1.0 %unpack.1 = bf16[64,2048]{1,0:T(8,128)(2,1)} custom-call(s32[2,128]{1,0:T(2,128)S(1)} %get-tuple-element.11.places, bf16[128,2048]{1,0:T(8,128)(2,1)S(1)} %bitcast.5), custom_call_target="tpu_custom_call" | custom-call | tf_op jit(solution)/shard_map/unpack/pallas_call | solution.py:351
Async XLA Ops:
  2.1 7.6 %copy-start = (bf16[2048,128]{1,0:T(8,128)(2,1)S(1)}, bf16[2048,128]{1,0:T(8,128)(2,1)}, u32[]{:S(2)}) copy-start(bf16[2048,128]{1,0:T(8,128)(2,1)} %values.1) | copy-start | bytes 1572868
  2.2 7.6 %copy-start.1 = (s32[16,16]{1,0:T(8,128)S(1)}, s32[16,16]{1,0:T(8,128)}, u32[]{:S(2)}) copy-start(s32[16,16]{1,0:T(8,128)} %span.1) | copy-start | bytes 3076
  2.2 7.6 %copy-start.2 = (s32[16,1]{0,1:T(1,128)S(1)}, s32[16,1]{0,1:T(1,128)}, u32[]{:S(2)}) copy-start(s32[16,1]{0,1:T(1,128)} %param.9) | copy-start | bytes 196
  2.2 7.6 %copy-start.3 = (s32[16]{0:T(128)S(1)}, s32[16]{0:T(128)}, u32[]{:S(2)}) copy-start(s32[16]{0:T(128)} %prefix_len.1) | copy-start | bytes 196
  2.2 24.3 %all-to-all-start = ((bf16[16,8,2304]{2,1,0:T(8,128)(2,1)}), bf16[16,8,2304]{2,1,0:T(8,128)(2,1)S(1)}, u32[]{:S(2)}, u32[]{:S(2)}) async-start(bf16[16,8,2304]{2,1,0:T(8,128)(2,1)} %bitcast.1), calls=%async_computation | async-start | bytes 1179648 | tf_op jit(solution)/shard_map/all_to_all | solution.py:298
  9.8 16.7 %copy-start.4 = (bf16[2048,128]{1,0:T(8,128)(2,1)S(1)}, bf16[2048,128]{1,0:T(8,128)(2,1)}, u32[]{:S(2)}) copy-start(bf16[2048,128]{1,0:T(8,128)(2,1)} %keys.1) | copy-start | bytes 1572868

commit v8 on v7

--- a/solution.py
+++ b/solution.py
@@ -38,11 +38,10 @@
 
 
 def place_of(devices, device):
-    return device % (devices // 2) * 2 + device // (devices // 2)
-
-
-def device_at(devices, place):
-    return place % 2 * (devices // 2) + place // 2
+    return device * (devices // 2 - 1) % devices
+
+
+device_at = place_of
 
 
 def pack_kernel(devices, hit_count, owners, q, k, v, send, places, held, hits, count, sems):

time: 49.9 us -> 48.7 us (0.976); the launches traced: 50.2 us -> 47.8 us
  waiting for transfers between devices: 15.3 us -> 14.1 us
  Pallas kernels: 6.8 us -> 6.12 us
  blocking collectives: 20.4 us -> 19.9 us
    all_to_all x1, waiting for transfers between devices: 15.3 us -> 14.1 us  [exchange(): lax.all_to_all(x, 'cache', split_axis=0, concat_axis=0, axis_index_groups...]
    pallas_call x1, Pallas kernels: 2.28 us -> 1.6 us  [body(): call(attend_kernel, [((rows, CAP * WIDE), jnp.bfloat16)] + [((rows, CAP *...]
where the time goes in v8:
time: 48.7 us; the launch traced here: 47.8 us
  blocking collectives  19.9 us (41%)
  waiting for transfers between devices  14.1 us (29%)
  starting transfers between devices  7.53 us (15%)
  Pallas kernels  6.12 us (13%)
    all_to_all x1, blocking collectives, exchange(): lax.all_to_all(x, 'cache', split_axis=0, concat_axis=0, axis_index_groups...  19.9 us
    all_to_all x1, waiting for transfers between devices, exchange(): lax.all_to_all(x, 'cache', split_axis=0, concat_axis=0, axis_index_groups...  14.1 us
    all_to_all x1, starting transfers between devices, exchange(): lax.all_to_all(x, 'cache', split_axis=0, concat_axis=0, axis_index_groups...  7.53 us
    pallas_call x1, Pallas kernels, body(): call(pack_kernel, [((rows, CAP * (WIDE + HD)), jnp.bfloat16), ((CAP * hit...  2.13 us
    pallas_call x1, Pallas kernels, body(): call(attend_kernel, [((rows, CAP * WIDE), jnp.bfloat16)] + [((rows, CAP *...  1.6 us
    pallas_call x1, Pallas kernels, body(): call(prep_kernel, [((CAP,), jnp.int32), ((CAP * rows, rows), jnp.float32)...  1.36 us
    pallas_call x1, Pallas kernels, body(): call(unpack_kernel, [((ROWS, HEADS * HD), jnp.bfloat16)], 'unpack', in_sp...  1.03 us
  transfers between devices with their start and end apart: 1, of which 1 were waited for; matrix products, arithmetic and copies ran while one was open for 0% of the time, Pallas kernels for 3%

profile of v8, /device:TPU:0, one launch (start us, length us, event | category | flops | bytes accessed | tf_op | source)
XLA Modules:
  0.0 47.8 jit_solution(7480903032795057406)
XLA Ops:
  0.0 2.1 %pack.1 = (bf16[128,2304]{1,0:T(8,128)(2,1)}, s32[2,128]{1,0:T(2,128)S(1)}) custom-call(s32[16]{0:T(128)} %bitcast.8, bf16[64,2048]{1,0:T(8,128)(2,1)} %q.1, bf16[64,128]{1,0:T(8,128)(2,1)} %k.1, bf16[64,128]{1,0:T(8,128)(2,1)} %v.1), custom_call_target="tpu_custom_call" | custom-call | tf_op jit(solution)/shard_map/pack/pallas_call | solution.py:310
  2.1 0.0 copy-start
  2.2 0.0 copy-start.1
  2.2 0.0 copy-start.2
  2.2 0.0 copy-start.3
  2.2 7.5 %all-to-all-start = ((bf16[16,8,2304]{2,1,0:T(8,128)(2,1)}), bf16[16,8,2304]{2,1,0:T(8,128)(2,1)S(1)}, u32[]{:S(2)}, u32[]{:S(2)}) async-start(bf16[16,8,2304]{2,1,0:T(8,128)(2,1)} %bitcast.1), calls=%async_computation | async-start | bytes 1179648 | tf_op jit(solution)/shard_map/all_to_all | solution.py:297
  9.7 0.0 copy-done
  9.7 0.0 copy-done.1
  9.8 0.0 copy-done.2
  9.8 0.0 copy-done.3
  9.8 0.0 copy-start.4
  9.8 1.4 %prep.1 = (s32[2]{0:T(128)S(1)}, f32[256,128]{1,0:T(8,128)S(1)}, f32[2,1024]{1,0:T(2,128)S(1)}, bf16[2048,256]{1,0:T(8,128)(2,1)S(1)}) custom-call(s32[16]{0:T(128)S(1)} %bitcast.9, s32[16]{0:T(128)S(1)} %copy-done.3, s32[16,16]{1,0:T(8,128)S(1)} %copy-done.1, bf16[2048,128]{1,0:T(8,128)(2,1)S(1)} %copy-done), custom_call_target="tpu_custom_call" | custom-call | flops 1000000 | bytes 4194304 | tf_op jit(solution)/shard_map/prep/pallas_call | solution.py:324
  11.2 14.1 %all-to-all-done = bf16[16,8,2304]{2,1,0:T(8,128)(2,1)S(1)} async-done(((bf16[16,8,2304]{2,1,0:T(8,128)(2,1)}), bf16[16,8,2304]{2,1,0:T(8,128)(2,1)S(1)}, u32[]{:S(2)}, u32[]{:S(2)}) %all-to-all-start) | async-done | bytes 589856 | tf_op jit(solution)/shard_map/all_to_all | solution.py:297
  25.2 0.0 copy-done.4
  25.2 1.6 %attend.1 = bf16[128,2048]{1,0:T(8,128)(2,1)S(1)} custom-call(s32[2]{0:T(128)S(1)} %get-tuple-element.12.busy, f32[256,128]{1,0:T(8,128)S(1)} %get-tuple-element.13.prompt_mask, f32[2,1024]{1,0:T(2,128)S(1)} %get-tuple-element.14.cached_mask, bf16[128,2304]{1,0:T(8,128)(2,1)S(1)} %bitcast.6, bf16[2048,128]{1,0:T(8,128)(2,1)S(1)} %copy-done.4, ...), custom_call_target="tpu_custom_call" | custom-call | flops 1207959552 | bytes 1048576 | tf_op jit(solution)/shard_map/attend/pallas_call | solution.py:338
  26.8 19.9 %all_to_all.22 = bf16[16,8,2048]{2,1,0:T(8,128)(2,1)S(1)} all-to-all(bf16[16,8,2048]{2,1,0:T(8,128)(2,1)S(1)} %bitcast.7), channel_id=1, replica_groups={{0,7,14,5,12,3,10,1,8,15,6,13,4,11,2,9},{16,23,30,21,28,19,26,17,24,31,..., dimensions={0} | all-to-all | bytes 1048576 | tf_op jit(solution)/shard_map/all_to_all | solution.py:297
  46.8 1.0 %unpack.1 = bf16[64,2048]{1,0:T(8,128)(2,1)} custom-call(s32[2,128]{1,0:T(2,128)S(1)} %get-tuple-element.11.places, bf16[128,2048]{1,0:T(8,128)(2,1)S(1)} %bitcast.5), custom_call_target="tpu_custom_call" | custom-call | tf_op jit(solution)/shard_map/unpack/pallas_call | solution.py:350
Async XLA Ops:
  2.1 7.6 %copy-start = (bf16[2048,128]{1,0:T(8,128)(2,1)S(1)}, bf16[2048,128]{1,0:T(8,128)(2,1)}, u32[]{:S(2)}) copy-start(bf16[2048,128]{1,0:T(8,128)(2,1)} %values.1) | copy-start | bytes 1572868
  2.2 7.6 %copy-start.1 = (s32[16,16]{1,0:T(8,128)S(1)}, s32[16,16]{1,0:T(8,128)}, u32[]{:S(2)}) copy-start(s32[16,16]{1,0:T(8,128)} %span.1) | copy-start | bytes 3076
  2.2 7.6 %copy-start.2 = (s32[16,1]{0,1:T(1,128)S(1)}, s32[16,1]{0,1:T(1,128)}, u32[]{:S(2)}) copy-start(s32[16,1]{0,1:T(1,128)} %param.9) | copy-start | bytes 196
  2.2 7.6 %copy-start.3 = (s32[16]{0:T(128)S(1)}, s32[16]{0:T(128)}, u32[]{:S(2)}) copy-start(s32[16]{0:T(128)} %prefix_len.1) | copy-start | bytes 196
  2.2 23.0 %all-to-all-start = ((bf16[16,8,2304]{2,1,0:T(8,128)(2,1)}), bf16[16,8,2304]{2,1,0:T(8,128)(2,1)S(1)}, u32[]{:S(2)}, u32[]{:S(2)}) async-start(bf16[16,8,2304]{2,1,0:T(8,128)(2,1)} %bitcast.1), calls=%async_computation | async-start | bytes 1179648 | tf_op jit(solution)/shard_map/all_to_all | solution.py:297
  9.8 15.5 %copy-start.4 = (bf16[2048,128]{1,0:T(8,128)(2,1)S(1)}, bf16[2048,128]{1,0:T(8,128)(2,1)}, u32[]{:S(2)}) copy-start(bf16[2048,128]{1,0:T(8,128)(2,1)} %keys.1) | copy-start | bytes 1572868

commit v9 on v6

--- a/solution.py
+++ b/solution.py
@@ -24,9 +24,7 @@
 STRIP = 256
 SCALE = HD**-0.5
 FLOOR = -1e30
-NT = (((1,), (1,)), ((), ()))
 NN = (((1,), (0,)), ((), ()))
-TN = (((0,), (0,)), ((), ()))
 
 
 def iota(shape, axis):
@@ -81,12 +79,22 @@
         picks.append(jnp.where(chosen, 1.0, 0.0).astype(jnp.bfloat16))
     for copy in copies:
         copy.wait()
+    packed = dot(jnp.concatenate(picks, axis=0), held[...], NN).astype(jnp.bfloat16)
     for s in range(CAP):
-        here = slice(s * (WIDE + HD), (s + 1) * (WIDE + HD))
-        send[:, here] = dot(picks[s], held[...], NN).astype(jnp.bfloat16)
-
-
-def prep_kernel(devices, hit_count, hits, prefix_len, span, values, busy, prompt, cached, wide):
+        rows = slice(s * devices * MSG, (s + 1) * devices * MSG)
+        send[:, s * (WIDE + HD) : (s + 1) * (WIDE + HD)] = packed[rows]
+
+
+def prep_kernel(
+    devices, hit_count, hits, prefix_len, span, places, keys, values, *outs
+):
+    busy, prompt, cached, turned, wide, picks = outs
+    rows = iota((devices * MSG, 2 * ROWS), 0)
+    for n in range(CAP * hit_count):
+        chosen = jnp.where(rows == places[n : n + 1, :], 1.0, 0.0)
+        picks[n * 2 * ROWS : (n + 1) * 2 * ROWS, :] = chosen.T.astype(jnp.bfloat16)
+    for n in range(0, CAP * REGION, STRIP):
+        turned[:, n : n + STRIP] = keys[n : n + STRIP, :].T
     me = lax.axis_index("cache")
     total_rows = devices * MSG
     wide[:, :HD] = values[...]
@@ -143,7 +151,9 @@
     return jnp.max(functools.reduce(jnp.maximum, pieces), axis=1, keepdims=True)
 
 
-def attend_kernel(devices, hit_count, busy, prompt_mask, cached_mask, got, keys, wide, out, *levels):
+def attend_kernel(
+    devices, hit_count, busy, prompt_mask, cached_mask, got, turned, wide, out, *levels
+):
     total_rows = devices * MSG
     block = 16 * MSG
     factor = SCALE * math.log2(math.e)
@@ -160,8 +170,9 @@
         head = pl.ds(region, whole) if whole else None
         tail = pl.ds(pl.multiple_of(region + whole, STRIP), STRIP)
         tail_mask = cached_mask[pl.ds(slot, 1), whole : whole + STRIP]
-        prompt_keys = got[:, pl.ds(base + WIDE, HD)]
-        moved = pltpu.roll(prompt_keys.astype(jnp.float32), total_rows - TOK_REQ, 0)
+        prompt_keys = got[:, pl.ds(base + WIDE, HD)].astype(jnp.float32)
+        moved = pltpu.roll(prompt_keys, total_rows - TOK_REQ, 0)
+        prompt_keys = prompt_keys.T.astype(jnp.bfloat16)
         prompt_values = jnp.concatenate(
             [moved.astype(jnp.bfloat16), jnp.ones((total_rows, HD), jnp.bfloat16)], axis=1
         )
@@ -176,9 +187,9 @@
                 pair = jnp.concatenate(
                     [got[here, pl.ds(base + (c + n) * HD, HD)] for n in range(2)], axis=0
                 )
-                parts = [dot(pair, keys[head, :], NT)] if whole else []
-                parts.append(dot(pair, keys[tail, :], NT) + tail_mask)
-                parts.append(dot(pair, prompt_keys, NT) + prompt_bias)
+                parts = [dot(pair, turned[:, head], NN)] if whole else []
+                parts.append(dot(pair, turned[:, tail], NN) + tail_mask)
+                parts.append(dot(pair, prompt_keys, NN) + prompt_bias)
                 return parts
 
             logs = jnp.zeros((block, HD), jnp.float32)
@@ -216,17 +227,16 @@
             pl.when(strips == count)(functools.partial(attend, slot, count))
 
 
-def unpack_kernel(devices, hit_count, places, *refs):
+def unpack_kernel(devices, hit_count, picks, *refs):
     outs, logs, result = refs[0], refs[1:-1], refs[-1]
-    target = iota((devices * MSG, 2 * ROWS), 0)
-
-    def chosen(s, i, dtype):
+
+    def chosen(s, i):
         place = s * hit_count + i
-        return jnp.where(target == places[place : place + 1, :], 1.0, 0.0).astype(dtype)
+        return picks[place * 2 * ROWS : (place + 1) * 2 * ROWS, :]
 
     def rows_of(i):
         parts = [
-            dot(chosen(s, i, jnp.bfloat16), outs[:, s * WIDE : (s + 1) * WIDE], TN)
+            dot(chosen(s, i), outs[:, s * WIDE : (s + 1) * WIDE], NN)
             for s in range(CAP)
         ]
         return sum(parts[1:], parts[0])
@@ -234,9 +244,9 @@
     def logs_of(i):
         parts = [
             dot(
-                chosen(s, i, jnp.float32),
+                chosen(s, i).astype(jnp.float32),
                 logs[0][:, s * HD : (s + 1) * HD],
-                TN,
+                NN,
                 precision=lax.Precision.HIGHEST,
             )
             for s in range(CAP)
@@ -309,19 +319,21 @@
         ],
     )(*(pltpu.with_memory_space_constraint(x, pltpu.HBM) for x in fresh))
     got = exchange(send)
-    busy, prompt_mask, cached_mask, wide = call(
+    busy, prompt_mask, cached_mask, turned, wide, picks = call(
         prep_kernel,
         [
             ((CAP,), jnp.int32),
             ((CAP * rows, rows), jnp.float32),
             ((CAP, REGION), jnp.float32),
+            ((HD, CAP * REGION), jnp.bfloat16),
             ((CAP * REGION, 2 * HD), jnp.bfloat16),
+            ((CAP * hit_count * 2 * ROWS, rows), jnp.bfloat16),
         ],
         "prep",
-        in_specs=smem(2) + vmem(2),
-        out_specs=smem(1) + vmem(3),
+        in_specs=smem(2) + vmem(4),
+        out_specs=smem(1) + vmem(5),
         cost_estimate=pl.CostEstimate(flops=10**6, bytes_accessed=2**22, transcendentals=0),
-    )(owners, prefix_len, span_block, cache_values)
+    )(owners, prefix_len, span_block, places, cache_keys, cache_values)
     pairs = CAP * rows * HALF * (REGION + rows)
     answers = call(
         attend_kernel,
@@ -333,7 +345,7 @@
         cost_estimate=pl.CostEstimate(
             flops=4 * pairs * HD, bytes_accessed=8 * rows * WIDE, transcendentals=pairs
         ),
-    )(busy, prompt_mask, cached_mask, got, cache_keys, wide)
+    )(busy, prompt_mask, cached_mask, got, turned, wide)
     returned = [exchange(answer) for answer in answers]
     return call(
         unpack_kernel,
@@ -341,7 +353,7 @@
         "unpack",
         in_specs=vmem(1 + len(returned)),
         out_specs=vmem(1),
-    )(places, *returned)[0]
+    )(picks, *returned)[0]
 
 
 def solution(mesh):

time: 48.6 us -> 48.8 us (level)
  waiting for transfers between devices: 14.1 us -> 13.4 us
  local copies, waits for them, and re-layouts: 0.03 us -> 0.65 us
    all_to_all x1, waiting for transfers between devices: 14.1 us -> 13.4 us  [exchange(): return lax.all_to_all(x, 'cache', split_axis=0, concat_axis=0, tiled=True)]
    unnamed x10, local copies, waits for them, and re-layouts: 0.03 us -> 0.65 us
where the time goes in v9:
time: 48.8 us; the launch traced here: 47.9 us
  blocking collectives  19 us (39%)
  waiting for transfers between devices  13.4 us (27%)
  starting transfers between devices  7.53 us (15%)
  Pallas kernels  7.18 us (15%)
  local copies, waits for them, and re-layouts  0.65 us (1%)
    all_to_all x1, blocking collectives, exchange(): return lax.all_to_all(x, 'cache', split_axis=0, concat_axis=0, tiled=True)  19 us
    all_to_all x1, waiting for transfers between devices, exchange(): return lax.all_to_all(x, 'cache', split_axis=0, concat_axis=0, tiled=True)  13.4 us
    all_to_all x1, starting transfers between devices, exchange(): return lax.all_to_all(x, 'cache', split_axis=0, concat_axis=0, tiled=True)  7.53 us
    pallas_call x1, Pallas kernels, body(): call(attend_kernel, [((rows, CAP * WIDE), jnp.bfloat16)] + [((rows, CAP *...  2.63 us
    pallas_call x1, Pallas kernels, body(): call(pack_kernel, [((rows, CAP * (WIDE + HD)), jnp.bfloat16), ((CAP * hit...  2.14 us
    pallas_call x1, Pallas kernels, body(): call(prep_kernel, [((CAP,), jnp.int32), ((CAP * rows, rows), jnp.float32)...  1.42 us
    pallas_call x1, Pallas kernels, body(): call(unpack_kernel, [((ROWS, HEADS * HD), jnp.bfloat16)], 'unpack', in_sp...  0.99 us
  transfers between devices with their start and end apart: 1, of which 1 were waited for; matrix products, arithmetic and copies ran while one was open for 0% of the time, Pallas kernels for 3%

profile of v9, /device:TPU:0, one launch (start us, length us, event | category | flops | bytes accessed | tf_op | source)
XLA Modules:
  0.0 47.9 jit_solution(2619267891087308065)
XLA Ops:
  0.0 2.1 %pack.1 = (bf16[128,2304]{1,0:T(8,128)(2,1)}, s32[2,128]{1,0:T(2,128)S(1)}) custom-call(s32[16]{0:T(128)} %bitcast.8, bf16[64,2048]{1,0:T(8,128)(2,1)} %q.1, bf16[64,128]{1,0:T(8,128)(2,1)} %k.1, bf16[64,128]{1,0:T(8,128)(2,1)} %v.1), custom_call_target="tpu_custom_call" | custom-call | tf_op jit(solution)/shard_map/pack/pallas_call | solution.py:308
  2.1 0.0 copy-start
  2.2 0.0 copy-start.1
  2.2 0.0 copy-start.2
  2.2 7.5 %all-to-all-start = ((bf16[16,8,2304]{2,1,0:T(8,128)(2,1)}), bf16[16,8,2304]{2,1,0:T(8,128)(2,1)S(1)}, u32[]{:S(2)}, u32[]{:S(2)}) async-start(bf16[16,8,2304]{2,1,0:T(8,128)(2,1)} %bitcast.1), calls=%async_computation | async-start | bytes 1179648 | tf_op jit(solution)/shard_map/all_to_all | solution.py:297
  9.7 0.0 copy-start.3
  9.7 0.0 copy-start.4
  9.7 0.0 copy-done
  9.8 0.0 copy-done.1
  9.8 0.0 copy-done.2
  9.8 0.6 %copy-done.3 = s32[16,1]{0,1:T(1,128)S(1)} copy-done((s32[16,1]{0,1:T(1,128)S(1)}, s32[16,1]{0,1:T(1,128)}, u32[]{:S(2)}) %copy-start.3) | copy-done | bytes 88
  10.4 0.0 copy-done.4
  10.4 1.4 %prep.1 = (s32[2]{0:T(128)S(1)}, f32[256,128]{1,0:T(8,128)S(1)}, f32[2,1024]{1,0:T(2,128)S(1)}, bf16[128,2048]{1,0:T(8,128)(2,1)S(1)}, bf16[2048,256]{1,0:T(8,128)(2,1)S(1)}, /*index=5*/bf16[256,128]{1,0:T(8,128)(2,1)S(1)}) custom-call(s32[16]{0:T(128)S(1)} %bitcast.9, s32[16]{0:T(128)S(1)} %copy-done.4, s32[16,16]{1,0:T(8,128)S(1)} %copy-done.2, ...), custom_call_target="tpu_custom_call" | custom-call | flops 1000000 | bytes 4194304 | tf_op jit(solution)/shard_map/prep/pallas_call | solution.py:322
  11.8 13.4 %all-to-all-done = bf16[16,8,2304]{2,1,0:T(8,128)(2,1)S(1)} async-done(((bf16[16,8,2304]{2,1,0:T(8,128)(2,1)}), bf16[16,8,2304]{2,1,0:T(8,128)(2,1)S(1)}, u32[]{:S(2)}, u32[]{:S(2)}) %all-to-all-start) | async-done | bytes 589856 | tf_op jit(solution)/shard_map/all_to_all | solution.py:297
  25.3 2.6 %attend.1 = bf16[128,2048]{1,0:T(8,128)(2,1)S(1)} custom-call(s32[2]{0:T(128)S(1)} %get-tuple-element.15.busy, f32[256,128]{1,0:T(8,128)S(1)} %get-tuple-element.16.prompt_mask, f32[2,1024]{1,0:T(2,128)S(1)} %get-tuple-element.17.cached_mask, bf16[128,2304]{1,0:T(8,128)(2,1)S(1)} %bitcast.6, bf16[128,2048]{1,0:T(8,128)(2,1)S(1)} %get-tuple-element.19.turned, ...), custom_call_target="tpu_custom_call" | custom-call | flops 1207959552 | bytes 1048576 | tf_op jit(solution)/shard_map/attend/pallas_call | solution.py:338
  27.9 19.0 %all_to_all.22 = bf16[16,8,2048]{2,1,0:T(8,128)(2,1)S(1)} all-to-all(bf16[16,8,2048]{2,1,0:T(8,128)(2,1)S(1)} %bitcast.7), channel_id=1, replica_groups=mesh['groups'=2,'cache'=16] {'cache'}, dimensions={0} | all-to-all | bytes 1048576 | tf_op jit(solution)/shard_map/all_to_all | solution.py:297
  46.9 1.0 %unpack.1 = bf16[64,2048]{1,0:T(8,128)(2,1)} custom-call(bf16[256,128]{1,0:T(8,128)(2,1)S(1)} %get-tuple-element.14.picks, bf16[128,2048]{1,0:T(8,128)(2,1)S(1)} %bitcast.5), custom_call_target="tpu_custom_call" | custom-call | tf_op jit(solution)/shard_map/unpack/pallas_call | solution.py:350
Async XLA Ops:
  2.1 7.6 %copy-start = (bf16[2048,128]{1,0:T(8,128)(2,1)S(1)}, bf16[2048,128]{1,0:T(8,128)(2,1)}, u32[]{:S(2)}) copy-start(bf16[2048,128]{1,0:T(8,128)(2,1)} %keys.1) | copy-start | bytes 1572868
  2.2 7.6 %copy-start.1 = (bf16[2048,128]{1,0:T(8,128)(2,1)S(1)}, bf16[2048,128]{1,0:T(8,128)(2,1)}, u32[]{:S(2)}) copy-start(bf16[2048,128]{1,0:T(8,128)(2,1)} %values.1) | copy-start | bytes 1572868
  2.2 7.6 %copy-start.2 = (s32[16,16]{1,0:T(8,128)S(1)}, s32[16,16]{1,0:T(8,128)}, u32[]{:S(2)}) copy-start(s32[16,16]{1,0:T(8,128)} %span.1) | copy-start | bytes 3076
  2.2 23.1 %all-to-all-start = ((bf16[16,8,2304]{2,1,0:T(8,128)(2,1)}), bf16[16,8,2304]{2,1,0:T(8,128)(2,1)S(1)}, u32[]{:S(2)}, u32[]{:S(2)}) async-start(bf16[16,8,2304]{2,1,0:T(8,128)(2,1)} %bitcast.1), calls=%async_computation | async-start | bytes 1179648 | tf_op jit(solution)/shard_map/all_to_all | solution.py:297
  9.7 0.7 %copy-start.3 = (s32[16,1]{0,1:T(1,128)S(1)}, s32[16,1]{0,1:T(1,128)}, u32[]{:S(2)}) copy-start(s32[16,1]{0,1:T(1,128)} %param.9) | copy-start | bytes 196
  9.7 0.7 %copy-start.4 = (s32[16]{0:T(128)S(1)}, s32[16]{0:T(128)}, u32[]{:S(2)}) copy-start(s32[16]{0:T(128)} %prefix_len.1) | copy-start | bytes 196

commit v10 on v9

--- a/solution.py
+++ b/solution.py
@@ -22,6 +22,7 @@
 WIDE = HALF * HD
 ROWS = REQUESTS * TOK_REQ
 STRIP = 256
+GUEST_MSG = WIDE + HD + WIDE // 2 + HD
 SCALE = HD**-0.5
 FLOOR = -1e30
 NN = (((1,), (0,)), ((), ()))
@@ -96,7 +97,6 @@
     for n in range(0, CAP * REGION, STRIP):
         turned[:, n : n + STRIP] = keys[n : n + STRIP, :].T
     me = lax.axis_index("cache")
-    total_rows = devices * MSG
     wide[:, :HD] = values[...]
     wide[:, HD:] = jnp.ones((CAP * REGION, HD), jnp.bfloat16)
     for slot in range(CAP):
@@ -114,28 +114,31 @@
         blocks = jnp.clip((limit + STRIP - 1) // STRIP, 1, REGION // STRIP)
         busy[slot] = jnp.where(seen > slot, blocks, 0)
         cached[slot : slot + 1, :] = jnp.where(iota((1, REGION), 1) < limit, 0.0, FLOOR)
-        span_row = span[pl.ds(request, 1), :].astype(jnp.float32)
-        source = iota((devices, total_rows), 0)
-        spread = (iota((devices, total_rows), 1) // MSG == source).astype(jnp.bfloat16)
-        spans = jnp.broadcast_to(span_row, (16, devices)).astype(jnp.bfloat16)
-        key_span = dot(spans, spread, NN)[:1]
-        lane = iota((1, total_rows), 1)
-        key_spot = key_span.astype(jnp.int32) * TOK_REQ + lane % TOK_REQ
-        is_key = lane % MSG < TOK_REQ
-        if hit_count > 1:
-            is_key = is_key & (which == 0)
-        key_spot = jnp.where(is_key, key_spot, devices * TOK_REQ)
-        block = 16 * MSG
-
-        def one_block(at):
-            row_source = at * 16 + iota((block, devices), 0) // MSG
-            mine = iota((block, devices), 1) == row_source
-            row_span = jnp.sum(jnp.where(mine, span_row, 0.0), axis=1, keepdims=True)
-            row_spot = row_span.astype(jnp.int32) * TOK_REQ + iota((block, 1), 0) % TOK_REQ
-            here = pl.ds(slot * total_rows + at * block, block)
-            prompt[here, :] = jnp.where(key_spot <= row_spot, 0.0, FLOOR)
-
-        each_block(devices, one_block)
+        prompt_rows(devices, prompt, span, request, slot, hit_count == 1 or which == 0)
+
+
+def prompt_rows(devices, prompt, span, request, slot, counted):
+    total_rows = devices * MSG
+    span_row = span[pl.ds(request, 1), :].astype(jnp.float32)
+    source = iota((devices, total_rows), 0)
+    spread = (iota((devices, total_rows), 1) // MSG == source).astype(jnp.bfloat16)
+    spans = jnp.broadcast_to(span_row, (16, devices)).astype(jnp.bfloat16)
+    key_span = dot(spans, spread, NN)[:1]
+    lane = iota((1, total_rows), 1)
+    key_spot = key_span.astype(jnp.int32) * TOK_REQ + lane % TOK_REQ
+    is_key = (lane % MSG < TOK_REQ) & counted
+    key_spot = jnp.where(is_key, key_spot, devices * TOK_REQ)
+    block = 16 * MSG
+
+    def one_block(at):
+        row_source = at * 16 + iota((block, devices), 0) // MSG
+        mine = iota((block, devices), 1) == row_source
+        row_span = jnp.sum(jnp.where(mine, span_row, 0.0), axis=1, keepdims=True)
+        row_spot = row_span.astype(jnp.int32) * TOK_REQ + iota((block, 1), 0) % TOK_REQ
+        here = pl.ds(slot * total_rows + at * block, block)
+        prompt[here, :] = jnp.where(key_spot <= row_spot, 0.0, FLOOR)
+
+    each_block(devices, one_block)
 
 
 def each_block(devices, one_block):
@@ -227,6 +230,230 @@
             pl.when(strips == count)(functools.partial(attend, slot, count))
 
 
+def guest_plan(devices, owners, count, zero, host):
+    chips = devices // 2
+    for d in range(devices):
+        count[d] = 0
+    ranks = []
+    for r in range(REQUESTS):
+        owner = owners[r]
+        ranks.append(count[owner])
+        count[owner] = ranks[r] + 1
+    seconds = [jnp.where(count[d] > 1, 1, 0) for d in range(devices)]
+    for first in (0, chips // 2):
+        free, spare = jnp.int32(first), jnp.int32(first)
+        for x in range(first, first + chips // 2):
+            zero[free] = jnp.int32(x)
+            free = free + jnp.where(seconds[2 * x] + seconds[2 * x + 1] == 0, 1, 0)
+        for x in range(first, first + chips // 2):
+            both = seconds[2 * x] * seconds[2 * x + 1]
+            host[2 * x] = jnp.int32(x)
+            host[2 * x + 1] = jnp.where(both == 1, zero[spare], x)
+            spare = jnp.minimum(spare + both, first + chips // 2 - 1)
+    return ranks, seconds
+
+
+def guest_pack_kernel(
+    devices, hit_count, owners, q, k, v, send, places, held, held_guest, hits, *scalars
+):
+    count, zero, host, sems = scalars
+    half = WIDE // 2
+    moves = [
+        (q.at[:, pl.ds(0, WIDE)], held.at[pl.ds(0, ROWS), pl.ds(0, WIDE)]),
+        (q.at[:, pl.ds(WIDE, WIDE)], held.at[pl.ds(ROWS, ROWS), pl.ds(0, WIDE)]),
+        (k, held.at[pl.ds(0, ROWS), pl.ds(WIDE, HD)]),
+        (v, held.at[pl.ds(ROWS, ROWS), pl.ds(WIDE, HD)]),
+    ]
+    for g in range(4):
+        here = pl.ds(g * ROWS, ROWS)
+        moves.append((q.at[:, pl.ds(g * half, half)], held_guest.at[here, pl.ds(0, half)]))
+        moves.append((v if g % 2 else k, held_guest.at[here, pl.ds(half, HD)]))
+    first = pltpu.make_async_copy(owners, hits, sems.at[len(moves)])
+    first.start()
+    copies = [pltpu.make_async_copy(a, b, sems.at[n]) for n, (a, b) in enumerate(moves)]
+    for copy in copies:
+        copy.start()
+    first.wait()
+    ranks, _ = guest_plan(devices, hits, count, zero, host)
+    lane = iota((1, 4 * ROWS), 1)
+    lane_request = lane % ROWS // TOK_REQ
+    part = lane // ROWS
+    nowhere = -4 * MSG
+    own = jnp.full((1, 4 * ROWS), nowhere, jnp.int32)
+    guest = own
+    for r in range(REQUESTS):
+        owner = hits[r]
+        mine = lane_request == r
+        own = jnp.where(mine, jnp.where(ranks[r] == 0, owner * MSG, nowhere), own)
+        guest = jnp.where(mine, jnp.where(ranks[r] == 1, host[owner] * 2 * MSG, nowhere), guest)
+    own = own + part * TOK_REQ + lane % TOK_REQ
+    guest = guest + part * TOK_REQ + lane % TOK_REQ
+    places[0:1, :] = own
+    places[1:2, :] = guest
+    target = iota((devices * MSG, 4 * ROWS), 0)
+    pick = jnp.where(target[:, : 2 * ROWS] == own[:, : 2 * ROWS], 1.0, 0.0).astype(jnp.bfloat16)
+    pick_guest = jnp.where(target == guest, 1.0, 0.0).astype(jnp.bfloat16)
+    for copy in copies:
+        copy.wait()
+    send[:, : WIDE + HD] = dot(pick, held[...], NN).astype(jnp.bfloat16)
+    send[:, WIDE + HD :] = dot(pick_guest, held_guest[...], NN).astype(jnp.bfloat16)
+
+
+def guest_prep_kernel(
+    devices, hit_count, hits, prefix_len, span, places, keys, values, *refs
+):
+    plan, prompt, cached, turned, wide, picks, picks_guest, count, zero, host = refs
+    me = lax.axis_index("cache")
+    chip = me // 2
+    ranks, seconds = guest_plan(devices, hits, count, zero, host)
+    rows = iota((devices * MSG, 4 * ROWS), 0)
+    chosen = jnp.where(rows[:, : 2 * ROWS] == places[0:1, : 2 * ROWS], 1.0, 0.0)
+    picks[...] = chosen.T.astype(jnp.bfloat16)
+    chosen = jnp.where(rows == places[1:2, :], 1.0, 0.0)
+    picks_guest[...] = chosen.T.astype(jnp.bfloat16)
+    widen(keys[:REGION, :], values[:REGION, :], turned, wide)
+    first, guest, source = jnp.int32(-1), jnp.int32(-1), jnp.int32(0)
+    for r in range(REQUESTS):
+        owner = hits[r]
+        here = (ranks[r] == 1) & (host[owner] == chip)
+        first = jnp.where((ranks[r] == 0) & (owner == me), r, first)
+        guest = jnp.where(here, r, guest)
+        source = jnp.where(here, owner, source)
+    core = me % 2
+    from_first_core = jnp.where(source == 2 * chip, 1, 0)
+    plan[2] = jnp.where(core == 1, (source // 2) ^ chip, 0)
+    plan[3] = jnp.where(core == from_first_core, 1, 0)
+    for job, found in enumerate((first, guest)):
+        request = jnp.maximum(found, 0)
+        limit = prefix_len[request]
+        strips = jnp.clip((limit + STRIP - 1) // STRIP, 1, REGION // STRIP)
+        plan[job] = jnp.where(found >= 0, strips, 0)
+        cached[job : job + 1, :] = jnp.where(iota((1, REGION), 1) < limit, 0.0, FLOOR)
+        prompt_rows(devices, prompt, span, request, job, True)
+
+
+def widen(keys, values, turned, wide):
+    for n in range(0, REGION, STRIP):
+        turned[:, n : n + STRIP] = keys[n : n + STRIP].T
+    wide[:, :HD] = values
+    wide[:, HD:] = jnp.ones((REGION, HD), jnp.bfloat16)
+
+
+def lend_kernel(devices, hit_count, plan, keys, values, *refs):
+    lent, out, sems = refs[:-2], refs[-2], refs[-1]
+    own = [keys.at[pl.ds(REGION, REGION)], values.at[pl.ds(REGION, REGION)]]
+    sources = [own] + [[x.at[pl.ds(n * REGION, REGION)] for n in range(2)] for x in lent]
+    for choice, pair in enumerate(sources):
+
+        @pl.when(plan[2] == choice)
+        def _():
+            copies = [
+                pltpu.make_async_copy(pair[n], out.at[pl.ds(n * REGION, REGION)], sems.at[n])
+                for n in range(2)
+            ]
+            for copy in copies:
+                copy.start()
+            for copy in copies:
+                copy.wait()
+
+
+def host_kernel(devices, hit_count, plan, mine, other, turned, wide):
+    for choice, rows in enumerate((mine, other)):
+
+        @pl.when(plan[3] == choice)
+        def _():
+            widen(rows[:REGION, :], rows[REGION:, :], turned, wide)
+
+
+def guest_attend_kernel(
+    devices, hit_count, plan, prompt_mask, cached_mask, got, turned, wide, *refs
+):
+    turned_guest, wide_guest, out = refs
+    jobs = [
+        (0, 0, HALF, turned, wide),
+        (WIDE + HD, WIDE, HALF // 2, turned_guest, wide_guest),
+    ]
+    for job, (base, first, blocks, keys, values) in enumerate(jobs):
+        strips = plan[job]
+
+        @pl.when(strips == 0)
+        def _():
+            empty = jnp.zeros((devices * MSG, blocks * HD), jnp.bfloat16)
+            out[:, first : first + blocks * HD] = empty
+
+        for count in range(1, REGION // STRIP + 1):
+
+            @pl.when(strips == count)
+            def _():
+                whole = (count - 1) * STRIP
+                mask = prompt_mask[job * devices * MSG : (job + 1) * devices * MSG, :]
+                attend_rows(
+                    got,
+                    base,
+                    blocks,
+                    slice(0, devices * MSG),
+                    prompt_parts(got[:, base + blocks * HD : base + (blocks + 1) * HD]),
+                    mask,
+                    cached_mask[job : job + 1, whole : whole + STRIP],
+                    keys[:, :whole] if whole else None,
+                    keys[:, whole : whole + STRIP],
+                    values[:whole, :] if whole else None,
+                    values[whole : whole + STRIP, :],
+                    out,
+                    first,
+                )
+
+
+def prompt_parts(rows):
+    height = rows.shape[0]
+    wide = rows.astype(jnp.float32)
+    moved = pltpu.roll(wide, height - TOK_REQ, 0).astype(jnp.bfloat16)
+    values = jnp.concatenate([moved, jnp.ones((height, HD), jnp.bfloat16)], axis=1)
+    return wide.T.astype(jnp.bfloat16), values
+
+
+def attend_rows(
+    got, base, blocks, here, prompt, mask, tail_mask, head, tail, head_values, tail_values, out, first
+):
+    prompt_keys, prompt_values = prompt
+    factor = SCALE * math.log2(math.e)
+    mask = jnp.concatenate([mask, mask], axis=0)
+    height = mask.shape[0] // 2
+
+    def scores(c):
+        pair = jnp.concatenate(
+            [got[here, base + (c + n) * HD : base + (c + n + 1) * HD] for n in range(2)], axis=0
+        )
+        parts = [] if head is None else [dot(pair, head, NN)]
+        parts.append(dot(pair, tail, NN) + tail_mask)
+        parts.append(dot(pair, prompt_keys, NN) + mask)
+        return parts
+
+    parts = scores(0)
+    for c in range(0, blocks, 2):
+        later = scores(c + 2) if c + 2 < blocks else None
+        top = lanes_max(parts)
+        parts = [jnp.exp2((x - top) * factor).astype(jnp.bfloat16) for x in parts]
+        summed = dot(parts[-1], prompt_values, NN) + dot(parts[-2], tail_values, NN)
+        if head is not None:
+            summed = summed + dot(parts[0], head_values, NN)
+        result = (summed[:, :HD] / summed[:, HD:]).astype(jnp.bfloat16)
+        for n in range(2):
+            column = first + (c + n) * HD
+            out[here, column : column + HD] = result[n * height : (n + 1) * height]
+        parts = later
+
+
+def guest_unpack_kernel(devices, hit_count, picks, picks_guest, outs, result):
+    half = WIDE // 2
+    own = dot(picks[...], outs[:, :WIDE], NN)
+    guest = dot(picks_guest[...], outs[:, WIDE:], NN)
+    for g in range(4):
+        rows = own[g // 2 * ROWS : (g // 2 + 1) * ROWS, g % 2 * half : (g % 2 + 1) * half]
+        rows = rows + guest[g * ROWS : (g + 1) * ROWS]
+        result[:, g * half : (g + 1) * half] = rows.astype(jnp.bfloat16)
+
+
 def unpack_kernel(devices, hit_count, picks, *refs):
     outs, logs, result = refs[0], refs[1:-1], refs[-1]
 
@@ -305,6 +532,70 @@
             **kw,
         )
 
+    if hit_count == 1 and devices == 16:
+        pairs = rows * (HALF + HALF // 2) * (REGION + rows)
+        lent = jnp.concatenate([cache_keys[REGION:], cache_values[REGION:]], axis=0)
+        borrowed = [
+            lax.ppermute(lent, "cache", [(d, d ^ (2 * n)) for d in range(1, devices, 2)])
+            for n in range(1, 4)
+        ]
+        scalars = [pltpu.SMEM((devices,), jnp.int32)] * 3
+        send, places = call(
+            guest_pack_kernel,
+            [((rows, GUEST_MSG), jnp.bfloat16), ((2, 4 * ROWS), jnp.int32)],
+            "pack",
+            in_specs=hbm(4),
+            out_specs=vmem(2),
+            scratch_shapes=[
+                pltpu.VMEM((2 * ROWS, WIDE + HD), jnp.bfloat16),
+                pltpu.VMEM((4 * ROWS, WIDE // 2 + HD), jnp.bfloat16),
+                pltpu.SMEM((REQUESTS,), jnp.int32),
+                *scalars,
+                pltpu.SemaphoreType.DMA((13,)),
+            ],
+        )(*(pltpu.with_memory_space_constraint(x, pltpu.HBM) for x in fresh))
+        got = exchange(send)
+        shapes = [((HD, REGION), jnp.bfloat16), ((REGION, 2 * HD), jnp.bfloat16)]
+        plan, prompt_mask, cached_mask, turned, wide, picks, picks_guest = call(
+            guest_prep_kernel,
+            [((4,), jnp.int32), ((2 * rows, rows), jnp.float32), ((2, REGION), jnp.float32)]
+            + shapes
+            + [((2 * ROWS, rows), jnp.bfloat16), ((4 * ROWS, rows), jnp.bfloat16)],
+            "prep",
+            in_specs=smem(2) + vmem(4),
+            out_specs=smem(1) + vmem(6),
+            scratch_shapes=scalars,
+            cost_estimate=pl.CostEstimate(flops=10**6, bytes_accessed=2**22, transcendentals=0),
+        )(owners, prefix_len, span_block, places, cache_keys, cache_values)
+        (mine,) = call(
+            lend_kernel,
+            [((2 * REGION, HD), jnp.bfloat16)],
+            "lend",
+            in_specs=smem(1) + hbm(5),
+            out_specs=vmem(1),
+            scratch_shapes=[pltpu.SemaphoreType.DMA((2,))],
+        )(plan, cache_keys, cache_values, *borrowed)
+        other = lax.ppermute(mine, "cache", [(d, d ^ 1) for d in range(devices)])
+        turned_guest, wide_guest = call(
+            host_kernel, shapes, "host", in_specs=smem(1) + vmem(2), out_specs=vmem(2)
+        )(plan, mine, other)
+        (answer,) = call(
+            guest_attend_kernel,
+            [((rows, WIDE + WIDE // 2), jnp.bfloat16)],
+            "attend",
+            in_specs=smem(1) + vmem(7),
+            out_specs=vmem(1),
+            cost_estimate=pl.CostEstimate(
+                flops=4 * pairs * HD, bytes_accessed=8 * rows * WIDE, transcendentals=pairs
+            ),
+        )(plan, prompt_mask, cached_mask, got, turned, wide, turned_guest, wide_guest)
+        return call(
+            guest_unpack_kernel,
+            [((ROWS, HEADS * HD), jnp.bfloat16)],
+            "unpack",
+            in_specs=vmem(3),
+            out_specs=vmem(1),
+        )(picks, picks_guest, exchange(answer))[0]
     send, places = call(
         pack_kernel,
         [((rows, CAP * (WIDE + HD)), jnp.bfloat16), ((CAP * hit_count, 2 * ROWS), jnp.int32)],

time: 48.8 us -> 52.4 us (1.074); the launches traced: 47.9 us -> 52.2 us
  starting transfers between devices: 7.53 us -> 15.8 us
  waiting for transfers between devices: 13.4 us -> 8.5 us
  blocking collectives: 19 us -> 15.8 us
  local copies, waits for them, and re-layouts: 0.65 us -> 2.48 us
  Pallas kernels: 7.18 us -> 8.62 us
  other arithmetic: 0 us -> 0.82 us
    all_to_all x1, waiting for transfers between devices: 13.4 us -> 6.96 us  [exchange(): return lax.all_to_all(x, 'cache', split_axis=0, concat_axis=0, tiled=True)]
    all_to_all x1, starting transfers between devices: 7.53 us -> 13.3 us  [exchange(): return lax.all_to_all(x, 'cache', split_axis=0, concat_axis=0, tiled=True)]
    all_to_all x1, blocking collectives: 19 us -> 15.8 us  [exchange(): return lax.all_to_all(x, 'cache', split_axis=0, concat_axis=0, tiled=True)]
    ppermute x0 -> x4, starting transfers between devices: none -> 2.54 us  [the longest x3 2.07 us: body(): lax.ppermute(lent, 'cache', [(d, d ^ 2 * n) for d in range(1, devices, 2)])]
    ppermute x0 -> x4, waiting for transfers between devices: none -> 1.54 us  [the longest x1 1.53 us: body(): other = lax.ppermute(mine, 'cache', [(d, d ^ 1) for d in range(devices)])]
    pallas_call x4 -> x6, Pallas kernels: 7.18 us -> 8.62 us  [the longest x1 2.53 us: body(): call(guest_attend_kernel, [((rows, WIDE + WIDE // 2), jnp.bfloat16)], 'at...]
    slice x0 -> x4, local copies, waits for them, and re-layouts: none -> 1.03 us  [body(): lent = jnp.concatenate([cache_keys[REGION:], cache_values[REGION:]], axis=0)]
    concatenate x0 -> x1, other arithmetic: none -> 0.82 us  [body(): lent = jnp.concatenate([cache_keys[REGION:], cache_values[REGION:]], axis=0)]
  transfers between devices with their start and end apart: 1 -> 5, of which waited for: 1 -> 2; matrix products, arithmetic and copies ran while one was open for 0% -> 0% of each run, Pallas kernels for 3% -> 10%
where the time goes in v10:
time: 52.4 us; the launch traced here: 52.2 us
  starting transfers between devices  15.8 us (30%)
  blocking collectives  15.8 us (30%)
  Pallas kernels  8.62 us (16%)
  waiting for transfers between devices  8.5 us (16%)
  local copies, waits for them, and re-layouts  2.48 us (5%)
  other arithmetic  0.82 us (2%)
    all_to_all x1, blocking collectives, exchange(): return lax.all_to_all(x, 'cache', split_axis=0, concat_axis=0, tiled=True)  15.8 us
    all_to_all x1, starting transfers between devices, exchange(): return lax.all_to_all(x, 'cache', split_axis=0, concat_axis=0, tiled=True)  13.3 us
    all_to_all x1, waiting for transfers between devices, exchange(): return lax.all_to_all(x, 'cache', split_axis=0, concat_axis=0, tiled=True)  6.96 us
    pallas_call x1, Pallas kernels, body(): call(guest_attend_kernel, [((rows, WIDE + WIDE // 2), jnp.bfloat16)], 'at...  2.53 us
    pallas_call x1, Pallas kernels, body(): call(guest_pack_kernel, [((rows, GUEST_MSG), jnp.bfloat16), ((2, 4 * ROWS...  2.37 us
    ppermute x3, starting transfers between devices, body(): lax.ppermute(lent, 'cache', [(d, d ^ 2 * n) for d in range(1, devices, 2)])  2.07 us
    ppermute x1, waiting for transfers between devices, body(): other = lax.ppermute(mine, 'cache', [(d, d ^ 1) for d in range(devices)])  1.53 us
    unnamed x18, local copies, waits for them, and re-layouts  1.46 us
  transfers between devices with their start and end apart: 5, of which 2 were waited for; matrix products, arithmetic and copies ran while one was open for 0% of the time, Pallas kernels for 10%

profile of v10, /device:TPU:0, one launch (start us, length us, event | category | flops | bytes accessed | tf_op | source)
XLA Modules:
  0.0 52.2 jit_solution(4001546363470635493)
XLA Ops:
  0.0 0.0 slice-start
  0.0 0.0 slice-start.1
  0.0 0.9 %slice-done = bf16[1024,128]{1,0:T(8,128)(2,1)S(1)} async-done(((bf16[2048,128]{1,0:T(8,128)(2,1)}), bf16[1024,128]{1,0:T(8,128)(2,1)S(1)}, s32[]{:S(2)}) %slice-start) | async-done | bytes 262168 | tf_op jit(solution)/shard_map/slice | solution.py:537
  1.0 0.1 slice-done.1
  1.0 0.8 %pad_maximum_fusion = bf16[2048,128]{1,0:T(8,128)(2,1)} fusion(bf16[1024,128]{1,0:T(8,128)(2,1)S(1)} %slice-done.1, bf16[1024,128]{1,0:T(8,128)(2,1)S(1)} %slice-done), kind=kLoop, calls=%fused_computation | loop fusion | flops 1048576 | bytes 1048576 | tf_op jit(solution)/shard_map/concatenate | solution.py:537
  1.9 0.7 %collective-permute-start.2 = (bf16[2048,128]{1,0:T(8,128)(2,1)}, bf16[2048,128]{1,0:T(8,128)(2,1)S(1)}, u32[]{:S(2)}, u32[]{:S(2)}) collective-permute-start(bf16[2048,128]{1,0:T(8,128)(2,1)} %pad_maximum_fusion), channel_id=1, source_target_pairs={{1,7},{3,5},{5,3},{7,1},{9,15},{11,13},{13,11},{15,9},{17,23},{19,... | collective-permute-start | bytes 1572872 | tf_op jit(solution)/shard_map/ppermute | solution.py:539
  2.5 0.7 %collective-permute-start.1 = (bf16[2048,128]{1,0:T(8,128)(2,1)}, bf16[2048,128]{1,0:T(8,128)(2,1)S(1)}, u32[]{:S(2)}, u32[]{:S(2)}) collective-permute-start(bf16[2048,128]{1,0:T(8,128)(2,1)} %pad_maximum_fusion), channel_id=1, source_target_pairs={{1,5},{3,7},{5,1},{7,3},{9,13},{11,15},{13,9},{15,11},{17,21},{19,... | collective-permute-start | bytes 1572872 | tf_op jit(solution)/shard_map/ppermute | solution.py:539
  3.2 0.7 %collective-permute-start = (bf16[2048,128]{1,0:T(8,128)(2,1)}, bf16[2048,128]{1,0:T(8,128)(2,1)S(1)}, u32[]{:S(2)}, u32[]{:S(2)}) collective-permute-start(bf16[2048,128]{1,0:T(8,128)(2,1)} %pad_maximum_fusion), channel_id=1, source_target_pairs={{1,3},{3,1},{5,7},{7,5},{9,11},{11,9},{13,15},{15,13},{17,19},{19,... | collective-permute-start | bytes 1572872 | tf_op jit(solution)/shard_map/ppermute | solution.py:539
  3.9 0.0 copy-start.1
  4.0 2.4 %pack.1 = (bf16[128,1792]{1,0:T(8,128)(2,1)}, s32[2,256]{1,0:T(2,128)S(1)}) custom-call(s32[16]{0:T(128)} %bitcast.8, bf16[64,2048]{1,0:T(8,128)(2,1)} %q.1, bf16[64,128]{1,0:T(8,128)(2,1)} %k.1, bf16[64,128]{1,0:T(8,128)(2,1)} %v.1), custom_call_target="tpu_custom_call" | custom-call | tf_op jit(solution)/shard_map/pack/pallas_call | solution.py:543
  6.3 0.0 copy-start
  6.3 0.0 copy-start.2
  6.4 13.3 %all-to-all-start = ((bf16[16,8,1792]{2,1,0:T(8,128)(2,1)}), bf16[16,8,1792]{2,1,0:T(8,128)(2,1)S(1)}, u32[]{:S(2)}, u32[]{:S(2)}) async-start(bf16[16,8,1792]{2,1,0:T(8,128)(2,1)} %bitcast.1), calls=%async_computation | async-start | bytes 917504 | tf_op jit(solution)/shard_map/all_to_all | solution.py:524
  19.6 0.0 copy-start.3
  19.6 0.0 copy-start.4
  19.6 0.0 copy-done.1
  19.7 0.0 copy-done
  19.7 0.0 copy-done.2
  19.7 0.6 %copy-done.3 = s32[16,1]{0,1:T(1,128)S(1)} copy-done((s32[16,1]{0,1:T(1,128)S(1)}, s32[16,1]{0,1:T(1,128)}, u32[]{:S(2)}) %copy-start.3) | copy-done | bytes 88
  20.3 0.0 copy-done.4
  20.3 1.4 %prep.1 = (s32[4]{0:T(128)S(1)}, f32[256,128]{1,0:T(8,128)S(1)}, f32[2,1024]{1,0:T(2,128)S(1)}, bf16[128,1024]{1,0:T(8,128)(2,1)S(1)}, bf16[1024,256]{1,0:T(8,12...) custom-call(s32[16]{0:T(128)S(1)} %bitcast.9, s32[16]{0:T(128)S(1)} %copy-done.4, ...), custom_call_target="tpu_custom_call" | custom-call | flops 1000000 | bytes 4194304 | tf_op jit(solution)/shard_map/prep/pallas_call | solution.py:559
  21.7 0.0 copy-start.5
  21.7 0.8 %copy-done.5 = bf16[1024,256]{1,0:T(8,128)(2,1)} copy-done((bf16[1024,256]{1,0:T(8,128)(2,1)}, bf16[1024,256]{1,0:T(8,128)(2,1)S(1)}, u32[]{:S(2)}) %copy-start.5) | copy-done | bytes 524312
  22.5 0.0 copy-start.7
  22.5 0.0 collective-permute-done.2.refs_2_
  22.6 0.0 collective-permute-done.1.refs_1_
  22.6 0.0 collective-permute-done.refs_0_
  22.6 0.6 %lend.1.mine = bf16[2048,128]{1,0:T(8,128)(2,1)S(1)} custom-call(s32[4]{0:T(128)S(1)} %get-tuple-element.19.plan, bf16[2048,128]{1,0:T(8,128)(2,1)S(1)} %copy-done, bf16[2048,128]{1,0:T(8,128)(2,1)S(1)} %copy-done.1, bf16[2048,128]{1,0:T(8,128)(2,1)S(1)} %collective-permute-done.refs_0_, bf16[2048,128]{1,0:T(8,128)(2,1)S(1)} %collective-permute-done.1.refs_1_, ...), custom_call_target="tpu_custom_call" | custom-call | tf_op jit(solution)/shard_map/lend/pallas_call | solution.py:570
  23.2 0.0 copy-done.7
  23.2 0.0 copy-start.6
  23.2 0.5 collective-permute-start.3
  23.7 0.0 copy-start.8
  23.7 1.5 %collective-permute-done.3.other = bf16[2048,128]{1,0:T(8,128)(2,1)S(1)} collective-permute-done((bf16[2048,128]{1,0:T(8,128)(2,1)S(1)}, bf16[2048,128]{1,0:T(8,128)(2,1)S(1)}, u32[]{:S(2)}, u32[]{:S(2)}) %collective-permute-start.3) | collective-permute-done | bytes 524320 | tf_op jit(solution)/shard_map/ppermute | solution.py:578
  25.2 0.7 %host.1 = (bf16[128,1024]{1,0:T(8,128)(2,1)S(1)}, bf16[1024,256]{1,0:T(8,128)(2,1)S(1)}) custom-call(s32[4]{0:T(128)S(1)} %get-tuple-element.19.plan, bf16[2048,128]{1,0:T(8,128)(2,1)S(1)} %lend.1.mine, bf16[2048,128]{1,0:T(8,128)(2,1)S(1)} %collective-permute-done.3.other), custom_call_target="tpu_custom_call" | custom-call | tf_op jit(solution)/shard_map/host/pallas_call | solution.py:579
  25.9 7.0 %all-to-all-done = bf16[16,8,1792]{2,1,0:T(8,128)(2,1)S(1)} async-done(((bf16[16,8,1792]{2,1,0:T(8,128)(2,1)}), bf16[16,8,1792]{2,1,0:T(8,128)(2,1)S(1)}, u32[]{:S(2)}, u32[]{:S(2)}) %all-to-all-start) | async-done | bytes 458784 | tf_op jit(solution)/shard_map/all_to_all | solution.py:524
  32.9 0.0 copy-done.6
  32.9 0.0 copy-done.8
  32.9 2.5 %attend.1 = bf16[128,1536]{1,0:T(8,128)(2,1)S(1)} custom-call(s32[4]{0:T(128)S(1)} %get-tuple-element.19.plan, f32[256,128]{1,0:T(8,128)S(1)} %copy-done.8, f32[2,1024]{1,0:T(2,128)S(1)} %get-tuple-element.21.cached_mask, bf16[128,1792]{1,0:T(8,128)(2,1)S(1)} %bitcast.6, bf16[128,1024]{1,0:T(8,128)(2,1)S(1)} %get-tuple-element.23.turned, ...), custom_call_target="tpu_custom_call" | custom-call | flops 905969664 | bytes 1048576 | tf_op jit(solution)/shard_map/attend/pallas_call | solution.py:582
  35.4 15.8 %all_to_all.22 = bf16[16,8,1536]{2,1,0:T(8,128)(2,1)S(1)} all-to-all(bf16[16,8,1536]{2,1,0:T(8,128)(2,1)S(1)} %bitcast.7), channel_id=1, replica_groups=mesh['groups'=2,'cache'=16] {'cache'}, dimensions={0} | all-to-all | bytes 786432 | tf_op jit(solution)/shard_map/all_to_all | solution.py:524
  51.2 1.0 %unpack.1 = bf16[64,2048]{1,0:T(8,128)(2,1)} custom-call(bf16[128,128]{1,0:T(8,128)(2,1)S(1)} %get-tuple-element.17.picks, bf16[256,128]{1,0:T(8,128)(2,1)S(1)} %get-tuple-element.18.picks_guest, bf16[128,1536]{1,0:T(8,128)(2,1)S(1)} %bitcast.5), custom_call_target="tpu_custom_call" | custom-call | tf_op jit(solution)/shard_map/unpack/pallas_call | solution.py:592
Async XLA Ops:
  0.0 0.9 %slice-start = ((bf16[2048,128]{1,0:T(8,128)(2,1)}), bf16[1024,128]{1,0:T(8,128)(2,1)S(1)}, s32[]{:S(2)}) async-start(bf16[2048,128]{1,0:T(8,128)(2,1)} %keys.3), calls=%async_computation.2 | async-start | bytes 524288 | tf_op jit(solution)/shard_map/slice | solution.py:537
  0.0 1.0 %slice-start.1 = ((bf16[2048,128]{1,0:T(8,128)(2,1)}), bf16[1024,128]{1,0:T(8,128)(2,1)S(1)}, s32[]{:S(2)}) async-start(bf16[2048,128]{1,0:T(8,128)(2,1)} %values.3), calls=%async_computation.3 | async-start | bytes 524288 | tf_op jit(solution)/shard_map/slice | solution.py:537
  1.9 20.7 %collective-permute-start.2 = (bf16[2048,128]{1,0:T(8,128)(2,1)}, bf16[2048,128]{1,0:T(8,128)(2,1)S(1)}, u32[]{:S(2)}, u32[]{:S(2)}) collective-permute-start(bf16[2048,128]{1,0:T(8,128)(2,1)} %pad_maximum_fusion), channel_id=1, source_target_pairs={{1,7},{3,5},{5,3},{7,1},{9,15},{11,13},{13,11},{15,9},{17,23},{19,... | collective-permute-start | bytes 1572872 | tf_op jit(solution)/shard_map/ppermute | solution.py:539
  2.5 20.0 %collective-permute-start.1 = (bf16[2048,128]{1,0:T(8,128)(2,1)}, bf16[2048,128]{1,0:T(8,128)(2,1)S(1)}, u32[]{:S(2)}, u32[]{:S(2)}) collective-permute-start(bf16[2048,128]{1,0:T(8,128)(2,1)} %pad_maximum_fusion), channel_id=1, source_target_pairs={{1,5},{3,7},{5,1},{7,3},{9,13},{11,15},{13,9},{15,11},{17,21},{19,... | collective-permute-start | bytes 1572872 | tf_op jit(solution)/shard_map/ppermute | solution.py:539
  3.2 19.3 %collective-permute-start = (bf16[2048,128]{1,0:T(8,128)(2,1)}, bf16[2048,128]{1,0:T(8,128)(2,1)S(1)}, u32[]{:S(2)}, u32[]{:S(2)}) collective-permute-start(bf16[2048,128]{1,0:T(8,128)(2,1)} %pad_maximum_fusion), channel_id=1, source_target_pairs={{1,3},{3,1},{5,7},{7,5},{9,11},{11,9},{13,15},{15,13},{17,19},{19,... | collective-permute-start | bytes 1572872 | tf_op jit(solution)/shard_map/ppermute | solution.py:539
  3.9 15.7 %copy-start.1 = (bf16[2048,128]{1,0:T(8,128)(2,1)S(1)}, bf16[2048,128]{1,0:T(8,128)(2,1)}, u32[]{:S(2)}) copy-start(bf16[2048,128]{1,0:T(8,128)(2,1)} %values.3) | copy-start | bytes 1572868
  6.3 13.3 %copy-start = (bf16[2048,128]{1,0:T(8,128)(2,1)S(1)}, bf16[2048,128]{1,0:T(8,128)(2,1)}, u32[]{:S(2)}) copy-start(bf16[2048,128]{1,0:T(8,128)(2,1)} %keys.3) | copy-start | bytes 1572868
  6.3 13.3 %copy-start.2 = (s32[16,16]{1,0:T(8,128)S(1)}, s32[16,16]{1,0:T(8,128)}, u32[]{:S(2)}) copy-start(s32[16,16]{1,0:T(8,128)} %span.1) | copy-start | bytes 3076
  6.4 26.5 %all-to-all-start = ((bf16[16,8,1792]{2,1,0:T(8,128)(2,1)}), bf16[16,8,1792]{2,1,0:T(8,128)(2,1)S(1)}, u32[]{:S(2)}, u32[]{:S(2)}) async-start(bf16[16,8,1792]{2,1,0:T(8,128)(2,1)} %bitcast.1), calls=%async_computation | async-start | bytes 917504 | tf_op jit(solution)/shard_map/all_to_all | solution.py:524
  19.6 0.7 %copy-start.3 = (s32[16,1]{0,1:T(1,128)S(1)}, s32[16,1]{0,1:T(1,128)}, u32[]{:S(2)}) copy-start(s32[16,1]{0,1:T(1,128)} %param.9) | copy-start | bytes 196
  19.6 0.7 %copy-start.4 = (s32[16]{0:T(128)S(1)}, s32[16]{0:T(128)}, u32[]{:S(2)}) copy-start(s32[16]{0:T(128)} %prefix_len.1) | copy-start | bytes 196
  21.7 0.8 %copy-start.5 = (bf16[1024,256]{1,0:T(8,128)(2,1)}, bf16[1024,256]{1,0:T(8,128)(2,1)S(1)}, u32[]{:S(2)}) copy-start(bf16[1024,256]{1,0:T(8,128)(2,1)S(1)} %get-tuple-element.24.wide) | copy-start | bytes 1572868
  22.5 0.7 %copy-start.7 = (f32[256,128]{1,0:T(8,128)}, f32[256,128]{1,0:T(8,128)S(1)}, u32[]{:S(2)}) copy-start(f32[256,128]{1,0:T(8,128)S(1)} %get-tuple-element.20.prompt_mask) | copy-start | bytes 393220
  23.2 9.7 %copy-start.6 = (bf16[1024,256]{1,0:T(8,128)(2,1)S(1)}, bf16[1024,256]{1,0:T(8,128)(2,1)}, u32[]{:S(2)}) copy-start(bf16[1024,256]{1,0:T(8,128)(2,1)} %copy-done.5) | copy-start | bytes 1572868
  23.2 2.0 %collective-permute-start.3 = (bf16[2048,128]{1,0:T(8,128)(2,1)S(1)}, bf16[2048,128]{1,0:T(8,128)(2,1)S(1)}, u32[]{:S(2)}, u32[]{:S(2)}) collective-permute-start(bf16[2048,128]{1,0:T(8,128)(2,1)S(1)} %lend.1.mine), channel_id=1, source_target_pairs={{0,1},{1,0},{2,3},{3,2},{4,5},{5,4},{6,7},{7,6},{8,9},{9,8},{10,11... | collective-permute-start | bytes 1572872 | tf_op jit(solution)/shard_map/ppermute | solution.py:578
  23.7 9.2 %copy-start.8 = (f32[256,128]{1,0:T(8,128)S(1)}, f32[256,128]{1,0:T(8,128)}, u32[]{:S(2)}) copy-start(f32[256,128]{1,0:T(8,128)} %copy-done.7) | copy-start | bytes 393220
